TPU v7x, 32 devices: a whole 2x2x4 slice. The times are simulated.
32 devices in a mesh: dp: 8 (over z, y), tensor: 4 (over x, core).
Axes of the slice: x: 2, y: 2, z: 4, core: 2. Of those that a mesh axis runs over, the one named last changes fastest.
Arguments:
- tokens: bfloat16 [4608, 1024], P('dp'), may hold values from -6 to 6
- cotangent: bfloat16 [4608, 1024], P('dp'), may hold values from -6 to 6
- lengths: int32 [8, 3], P('dp'), may hold values from 1 to 512, 540 in all within a row
- packing: int32 [4608], replicated, may hold values from 0 to 4607, as said below
- w_qkv: float32 [3, 1024, 1024], P(None, None, 'tensor'), may hold values from -0.1875 to 0.1875
- w_out: float32 [1024, 1024], P('tensor'), may hold values from -0.75 to 0.75
- w_up: float32 [1024, 4096], P(None, 'tensor'), may hold values from -0.1875 to 0.1875
- w_down: float32 [4096, 1024], P('tensor'), may hold values from -0.09375 to 0.09375
- bias_qv: float32 [2, 1024], P(None, 'tensor'), may hold values from -1.75 to 1.75
- bias_up: float32 [4096], P('tensor'), may hold values from -1.75 to 1.75
- vectors: float32 [6, 1024], replicated, may hold values from -2.5 to 2.5
- mom_qkv: float32 [3, 1024, 1024], P(None, None, 'tensor'), may hold values from -128 to 128
- mom_out: float32 [1024, 1024], P('tensor'), may hold values from -128 to 128
- mom_up: float32 [1024, 4096], P(None, 'tensor'), may hold values from -128 to 128
- mom_down: float32 [4096, 1024], P('tensor'), may hold values from -128 to 128
- mom_bias_qv: float32 [2, 1024], P(None, 'tensor'), may hold values from -128 to 128
- mom_bias_up: float32 [4096], P('tensor'), may hold values from -128 to 128
- mom_vectors: float32 [6, 1024], replicated, may hold values from -128 to 128
Outputs:
- output: bfloat16 [4608, 1024], P('dp')
- grad_tokens: float32 [4608, 1024], P('dp')
- grad_qkv: float32 [3, 1024, 1024], P(None, None, 'tensor')
- grad_out: float32 [1024, 1024], P('tensor')
- grad_up: float32 [1024, 4096], P(None, 'tensor')
- grad_down: float32 [4096, 1024], P('tensor')
- grad_bias_qv: float32 [2, 1024], P(None, 'tensor')
- grad_bias_up: float32 [4096], P('tensor')
- grad_vectors: float32 [6, 1024], replicated
- moment_qkv: float32 [3, 1024, 1024], P(None, None, 'tensor')
- moment_out: float32 [1024, 1024], P('tensor')
- moment_up: float32 [1024, 4096], P(None, 'tensor')
- moment_down: float32 [4096, 1024], P('tensor')
- moment_bias_qv: float32 [2, 1024], P(None, 'tensor')
- moment_bias_up: float32 [4096], P('tensor')
- moment_vectors: float32 [6, 1024], replicated
- master_qkv: float32 [3, 1024, 1024], P(None, 'dp', 'tensor')
- master_out: float32 [1024, 1024], P('tensor', 'dp')
- master_up: float32 [1024, 4096], P('dp', 'tensor')
- master_down: float32 [4096, 1024], P('tensor', 'dp')
- master_bias_qv: float32 [2, 1024], P(None, 'tensor')
- master_bias_up: float32 [4096], P('tensor')
- master_vectors: float32 [6, 1024], replicated
Inputs may be any that keep to these rules, and one draw needn't show every extreme that they name: Each row lists the lengths of the 3 sequences that fill, in order, the first 540 slots of one index of dp; its last 36 slots are padding. `packing`: A permutation of the rows; the slots of one index of dp take the same number of rows, 576 divided by the size of dp, from each index of dp.
All inputs are finite; a program needn't handle non-finite values.
Results may differ from a plain program's by a relative error of at most 0.018.
The roundings to bfloat16 on the way count: a program that leaves them out, or rounds other values in their place, can miss the bound.
Values may be sent and summed in bfloat16 or wider, within the bound.
A program may use at most 192 MiB of HBM per device.

v0:
```python
import math

import jax
import jax.numpy as jnp
from jax import lax
from jax.sharding import PartitionSpec as P

D = 1024
FF = 4096
HEAD = 64


highest = lax.Precision.HIGHEST
eps_norm = 1e-05
coef_one = 3.4445
coef_two = -4.775
coef_three = 2.0315
momentum_decay = 0.9
rate_matrix = 0.1
masked_score = -1000000000.0


def shortened(value):
    return jax.tree.map(lambda a: a.astype(jnp.bfloat16) if a.dtype == jnp.float32 else a, value)


def broadcast(value, axis, root):
    mine = lax.axis_index(axis) == root
    return lax.psum(jnp.where(mine, value, jnp.zeros_like(value)), axis)


def segment_layout(length_row, row_count):
    seq_ends = jnp.cumsum(length_row, dtype=jnp.int32)
    position = jnp.arange(row_count, dtype=jnp.int32)
    counted = jnp.sum((position[:, None] >= seq_ends[None, :]).astype(jnp.int32), axis=1)
    filled = seq_ends[-1]
    beyond = jnp.maximum(position - filled, 0)
    return (counted + beyond, (position < filled).astype(jnp.float32))


def norm_forward(values, gain_row, shift_row):
    average = jnp.mean(values, axis=-1, keepdims=True)
    centred = values - average
    variance = jnp.mean(centred * centred, axis=-1, keepdims=True)
    inverse = lax.rsqrt(variance + eps_norm)
    normed = centred * inverse
    return (normed, inverse, normed * gain_row + shift_row)


def norm_backward(upstream, normed, inverse, gain_row):
    scaled = upstream * gain_row
    centre_term = jnp.mean(scaled, axis=-1, keepdims=True)
    slope_term = jnp.mean(scaled * normed, axis=-1, keepdims=True)
    return inverse * (scaled - centre_term - normed * slope_term)


def shard_gram(shard, by_columns):
    if by_columns:
        return jnp.einsum("ik,jk->ij", shard, shard, precision=highest)
    return jnp.einsum("ki,kj->ij", shard, shard, precision=highest)


def polar_factor(gram):
    identity = jnp.eye(gram.shape[0], dtype=jnp.float32)
    current = gram
    factor = identity
    for sweep in range(5):
        square = jnp.dot(current, current, precision=highest)
        poly = coef_one * identity + coef_two * current + coef_three * square
        if sweep == 0:
            factor = poly
        else:
            factor = jnp.dot(poly, factor, precision=highest)
        if sweep < 4:
            current = jnp.dot(jnp.dot(poly, current, precision=highest), poly, precision=highest)
    return factor


def body(
    tokens,
    cotangent,
    lengths,
    packing,
    w_qkv,
    w_out,
    w_up,
    w_down,
    bias_qv,
    bias_up,
    vectors,
    mom_qkv,
    mom_out,
    mom_up,
    mom_down,
    mom_bias_qv,
    mom_bias_up,
    mom_vectors,
):
    dp_count = lax.axis_size("dp")
    dp_index = lax.axis_index("dp")
    tensor_count = lax.axis_size("tensor")
    tensor_index = lax.axis_index("tensor")
    row_count = tokens.shape[0]
    per_peer = row_count // dp_count
    share_rows = row_count // tensor_count
    share_start = tensor_index * share_rows
    all_tokens = row_count * dp_count
    source = packing // row_count
    target = jnp.arange(all_tokens, dtype=jnp.int32) // row_count
    slot_order = jnp.argsort(target * dp_count + source, stable=True)
    slot_order = slot_order.reshape(dp_count, dp_count, per_peer)
    out_slots = jnp.take(slot_order, dp_index, axis=1).reshape(-1)
    my_rows = jnp.take(packing, out_slots) % row_count
    in_slots = jnp.take(slot_order, dp_index, axis=0).reshape(-1) - dp_index * row_count
    placing = jnp.argsort(in_slots)
    restore = jnp.argsort(my_rows)
    sent_x = jnp.take(tokens, my_rows, axis=0).reshape(dp_count, per_peer, D)
    sent_dy = jnp.take(cotangent, my_rows, axis=0).reshape(dp_count, per_peer, D)
    got_x, got_dy = (
        lax.all_to_all(sent_x, "dp", split_axis=0, concat_axis=0, tiled=True),
        lax.all_to_all(sent_dy, "dp", split_axis=0, concat_axis=0, tiled=True),
    )
    packed_x = jnp.take(got_x.reshape(row_count, D), placing, axis=0)
    packed_dy = jnp.take(got_dy.reshape(row_count, D), placing, axis=0)

    def local_rows(values):
        return lax.dynamic_slice_in_dim(values, share_start, share_rows, 0)

    def reduce_rows(term_of):
        return lax.psum_scatter(
            term_of(jnp.int32(0), share_rows * lax.axis_size("tensor")),
            "tensor",
            scatter_dimension=0,
            tiled=True,
        )

    def spread_rows(piece):
        return lax.all_gather(piece, "tensor", axis=0, tiled=True)

    wqkv_low = w_qkv.astype(jnp.bfloat16)
    wout_low = w_out.astype(jnp.bfloat16)
    wup_low = w_up.astype(jnp.bfloat16)
    wdown_low = w_down.astype(jnp.bfloat16)
    local_width = w_qkv.shape[2]
    head_count = local_width // HEAD
    score_scale = HEAD ** (-0.5)
    projected = jnp.einsum("td,kde->kte", packed_x, wqkv_low, preferred_element_type=jnp.float32)
    queries = (projected[0] + bias_qv[0]).astype(jnp.bfloat16)
    keys_low = projected[1].astype(jnp.bfloat16)
    values_low = (projected[2] + bias_qv[1]).astype(jnp.bfloat16)
    keys_heads = keys_low.reshape(row_count, head_count, HEAD)
    values_heads = values_low.reshape(row_count, head_count, HEAD)
    segments, valid = segment_layout(lengths[0], row_count)
    block_count = row_count // row_count

    def scores_of():
        query_block = queries.reshape(row_count, head_count, HEAD)
        raw_scores = jnp.einsum(
            "qhd,khd->hqk", query_block, keys_heads, preferred_element_type=jnp.float32
        )
        same_seg = segments[:, None] == segments[None, :]
        return (jnp.where(same_seg[None], raw_scores * score_scale, masked_score), query_block)

    def attend(block_index):
        masked, query_block = scores_of()
        row_max = jnp.max(masked, axis=-1, keepdims=True)
        exponent = jnp.exp(masked - row_max)
        row_total = jnp.sum(exponent, axis=-1, keepdims=True)
        probabilities = (exponent / row_total).astype(jnp.bfloat16)
        context_block = jnp.einsum(
            "hqk,khd->qhd", probabilities, values_heads, preferred_element_type=jnp.float32
        )
        log_total = (row_max + jnp.log(row_total))[..., 0]
        return (context_block.reshape(row_count, local_width).astype(jnp.bfloat16), log_total)

    context_blocks, log_totals = lax.map(attend, jnp.arange(block_count, dtype=jnp.int32))
    context = context_blocks.reshape(row_count, local_width)

    def attn_term(first, count):
        return jnp.dot(context, wout_low, preferred_element_type=jnp.float32)

    attn_local = reduce_rows(attn_term)
    mid_rows = local_rows(packed_x).astype(jnp.float32) + attn_local + vectors[0]
    normed_one, inverse_one, hidden = norm_forward(mid_rows, vectors[1], vectors[2])
    hidden_low = spread_rows(hidden.astype(jnp.bfloat16))
    pre_act = jnp.dot(hidden_low, wup_low, preferred_element_type=jnp.float32) + bias_up
    activated, gelu_pull = jax.vjp(lambda operand: jax.nn.gelu(operand, approximate=False), pre_act)
    act_low = activated.astype(jnp.bfloat16)

    def mlp_term(first, count):
        return jnp.dot(act_low, wdown_low, preferred_element_type=jnp.float32)

    mlp_local = reduce_rows(mlp_term)
    normed_two, inverse_two, result = norm_forward(
        hidden + mlp_local + vectors[3], vectors[4], vectors[5]
    )
    result_low = spread_rows(result.astype(jnp.bfloat16))
    back_y = jnp.take(result_low, in_slots, axis=0).reshape(dp_count, per_peer, D)
    got_y = lax.all_to_all(back_y, "dp", split_axis=0, concat_axis=0, tiled=True)
    output = jnp.take(got_y.reshape(row_count, D), restore, axis=0)
    grad_result = local_rows(packed_dy).astype(jnp.float32) * local_rows(valid)[:, None]
    grad_z = norm_backward(grad_result, normed_two, inverse_two, vectors[4])
    grad_z_low = spread_rows(grad_z.astype(jnp.bfloat16))
    grad_down_w = jnp.einsum("tf,td->fd", act_low, grad_z_low, preferred_element_type=jnp.float32)
    grad_act = jnp.einsum("td,fd->tf", grad_z_low, wdown_low, preferred_element_type=jnp.float32)
    grad_pre_low = gelu_pull(grad_act)[0].astype(jnp.bfloat16)
    grad_bias_hidden = jnp.sum(grad_pre_low, axis=0, dtype=jnp.float32)
    grad_up_w = jnp.einsum(
        "td,tf->df", hidden_low, grad_pre_low, preferred_element_type=jnp.float32
    )

    def hidden_term(first, count):
        return jnp.einsum("tf,df->td", grad_pre_low, wup_low, preferred_element_type=jnp.float32)

    grad_hidden = grad_z + reduce_rows(hidden_term)
    grad_mid = norm_backward(grad_hidden, normed_one, inverse_one, vectors[1])
    grad_mid_low = spread_rows(grad_mid.astype(jnp.bfloat16))
    grad_out_w = jnp.einsum("te,td->ed", context, grad_mid_low, preferred_element_type=jnp.float32)
    grad_context = jnp.einsum(
        "td,ed->te", grad_mid_low, wout_low, preferred_element_type=jnp.float32
    ).astype(jnp.bfloat16)

    def attend_back(running, block_index):
        acc_keys, acc_values = running
        masked, query_block = scores_of()
        probabilities = jnp.exp(masked - log_totals[block_index][..., None])
        prob_low = probabilities.astype(jnp.bfloat16)
        grad_ctx_block = grad_context.reshape(row_count, head_count, HEAD)
        grad_probs = jnp.einsum(
            "qhd,khd->hqk", grad_ctx_block, values_heads, preferred_element_type=jnp.float32
        )
        weighted = jnp.sum(probabilities * grad_probs, axis=-1, keepdims=True)
        grad_scores = (probabilities * (grad_probs - weighted)).astype(jnp.bfloat16)
        acc_values = acc_values + jnp.einsum(
            "hqk,qhd->khd", prob_low, grad_ctx_block, preferred_element_type=jnp.float32
        )
        acc_keys = (
            acc_keys
            + jnp.einsum(
                "hqk,qhd->khd", grad_scores, query_block, preferred_element_type=jnp.float32
            )
            * score_scale
        )
        grad_query_block = (
            jnp.einsum("hqk,khd->qhd", grad_scores, keys_heads, preferred_element_type=jnp.float32)
            * score_scale
        )
        return ((acc_keys, acc_values), grad_query_block.reshape(row_count, local_width))

    empty_heads = jnp.zeros((row_count, head_count, HEAD), jnp.float32)
    (grad_keys, grad_values), grad_query_blocks = lax.scan(
        attend_back, (empty_heads, empty_heads), jnp.arange(block_count, dtype=jnp.int32)
    )
    grad_queries = grad_query_blocks.reshape(row_count, local_width)
    grad_stack = jnp.stack(
        [
            grad_queries,
            grad_keys.reshape(row_count, local_width),
            grad_values.reshape(row_count, local_width),
        ]
    ).astype(jnp.bfloat16)
    grad_bias_pair = jnp.stack(
        [
            jnp.sum(grad_stack[0], axis=0, dtype=jnp.float32),
            jnp.sum(grad_stack[2], axis=0, dtype=jnp.float32),
        ]
    )
    grad_qkv_w = jnp.einsum("td,kte->kde", packed_x, grad_stack, preferred_element_type=jnp.float32)
    input_part = jnp.einsum("kte,kde->td", grad_stack, wqkv_low, preferred_element_type=jnp.float32)
    vector_part = jnp.stack(
        [
            jnp.sum(grad_mid, axis=0),
            jnp.sum(grad_hidden * normed_one, axis=0),
            jnp.sum(grad_hidden, axis=0),
            jnp.sum(grad_z, axis=0),
            jnp.sum(grad_result * normed_two, axis=0),
            jnp.sum(grad_result, axis=0),
        ]
    )
    own_part = lax.dynamic_slice_in_dim(input_part, share_start, share_rows, 0) + grad_mid
    input_term = lax.dynamic_update_slice_in_dim(input_part, own_part, share_start, 0)
    input_total, vector_total = (
        lax.psum(input_term.astype(jnp.bfloat16), "tensor").astype(jnp.float32),
        lax.psum(vector_part.astype(jnp.bfloat16), "tensor").astype(jnp.float32),
    )
    gradients = (
        lax.psum(grad_qkv_w.astype(jnp.bfloat16), "dp").astype(jnp.float32),
        lax.psum(grad_out_w.astype(jnp.bfloat16), "dp").astype(jnp.float32),
        lax.psum(grad_up_w.astype(jnp.bfloat16), "dp").astype(jnp.float32),
        lax.psum(grad_down_w.astype(jnp.bfloat16), "dp").astype(jnp.float32),
        lax.psum(grad_bias_pair.astype(jnp.bfloat16), "dp").astype(jnp.float32),
        lax.psum(grad_bias_hidden.astype(jnp.bfloat16), "dp").astype(jnp.float32),
        lax.psum(vector_total.astype(jnp.bfloat16), "dp").astype(jnp.float32),
    )
    moments_old = (mom_qkv, mom_out, mom_up, mom_down, mom_bias_qv, mom_bias_up, mom_vectors)
    moments_new = tuple(
        (
            momentum_decay * old_value + grad_value
            for old_value, grad_value in zip(moments_old, gradients)
        )
    )
    stride = dp_count // 6
    slot = jnp.minimum(dp_index // stride, 5)
    owner = jnp.logical_and(dp_index % stride == 0, dp_index // stride < 6)
    shards = (
        moments_new[0][0],
        moments_new[0][1],
        moments_new[0][2],
        moments_new[1],
        moments_new[2],
        moments_new[3],
    )
    by_columns = (True, True, True, False, True, False)
    long_sides = (D, D, D, D, FF, FF)

    def gram_branch(position):
        return lambda pieces: shard_gram(pieces[position], by_columns[position])

    def owned_gram(pieces):
        return lax.switch(slot, [gram_branch(position) for position in range(6)], pieces)

    def empty_gram(pieces):
        return jnp.zeros((D, D), jnp.float32)

    gram_part = lax.cond(owner, owned_gram, empty_gram, shards)
    gram = lax.psum(gram_part, "tensor")
    scale = lax.rsqrt(jnp.trace(gram) + 1e-07)
    factor = lax.cond(
        owner, polar_factor, lambda operand: jnp.zeros_like(operand), gram * (scale * scale)
    )

    def owned_update(position):
        root_index = position * stride
        multiplier = 0.2 * math.sqrt(long_sides[position])

        def apply_factor(operands):
            factor_now, shard = operands
            if by_columns[position]:
                return jnp.dot(factor_now, shard * scale, precision=highest) * multiplier
            return jnp.dot(shard * scale, factor_now, precision=highest) * multiplier

        stepped = lax.cond(
            dp_index == root_index,
            apply_factor,
            lambda operands: jnp.zeros_like(operands[1]),
            (factor, shards[position]),
        )
        return broadcast(shortened(stepped), "dp", root_index).astype(stepped.dtype)

    updates = [owned_update(position) for position in range(6)]
    dp_rows = D // dp_count
    dp_first = dp_index * dp_rows

    def mine(values, dim):
        return lax.dynamic_slice_in_dim(values, dp_first, dp_rows, dim)

    params = (w_qkv, w_out, w_up, w_down, bias_qv, bias_up, vectors)
    masters = [
        mine(w_qkv, 1) - rate_matrix * mine(jnp.stack(updates[0:3]), 1),
        mine(w_out, 1) - rate_matrix * mine(updates[3], 1),
        mine(w_up, 0) - rate_matrix * mine(updates[4], 0),
        mine(w_down, 1) - rate_matrix * mine(updates[5], 1),
    ]
    rate_vector = 0.2 / math.sqrt(all_tokens)
    for group_slot in range(4, 7):
        masters.append(params[group_slot] - rate_vector * moments_new[group_slot])
    back_dx = jnp.take(input_total, in_slots, axis=0).reshape(dp_count, per_peer, D)
    got_dx = lax.all_to_all(
        back_dx.astype(jnp.bfloat16), "dp", split_axis=0, concat_axis=0, tiled=True
    ).astype(back_dx.dtype)
    grad_tokens = jnp.take(got_dx.reshape(row_count, D), restore, axis=0)
    return (
        output,
        grad_tokens,
        gradients[0],
        gradients[1],
        gradients[2],
        gradients[3],
        gradients[4],
        gradients[5],
        gradients[6],
        moments_new[0],
        moments_new[1],
        moments_new[2],
        moments_new[3],
        moments_new[4],
        moments_new[5],
        moments_new[6],
        masters[0],
        masters[1],
        masters[2],
        masters[3],
        masters[4],
        masters[5],
        masters[6],
    )


def solution(mesh):
    placed = (
        P("dp", None),
        P("dp", None),
        P("dp", None),
        P(),
        P(None, None, "tensor"),
        P("tensor", None),
        P(None, "tensor"),
        P("tensor", None),
        P(None, "tensor"),
        P("tensor"),
        P(),
        P(None, None, "tensor"),
        P("tensor", None),
        P(None, "tensor"),
        P("tensor", None),
        P(None, "tensor"),
        P("tensor"),
        P(),
    )
    return jax.shard_map(
        body,
        mesh=mesh,
        in_specs=placed,
        out_specs=(
            P("dp", None),
            P("dp", None),
            P(None, None, "tensor"),
            P("tensor", None),
            P(None, "tensor"),
            P("tensor", None),
            P(None, "tensor"),
            P("tensor"),
            P(),
            P(None, None, "tensor"),
            P("tensor", None),
            P(None, "tensor"),
            P("tensor", None),
            P(None, "tensor"),
            P("tensor"),
            P(),
            P(None, "dp", "tensor"),
            P("tensor", "dp"),
            P("dp", "tensor"),
            P("tensor", "dp"),
            P(None, "tensor"),
            P("tensor"),
            P(),
        ),
        check_vma=False,
    )
```

profile of v0, /device:TPU:1, one launch (start us, length us, event | category | flops | bytes accessed | tf_op | source)
XLA Modules:
  0.0 1217.5 jit_solution(16872047666741612354)
XLA Ops:
  8.1 6.8 sort.48
  29.9 6.4 all-to-all-start
  42.2 21.8 %all-to-all-done = bf16[8,72,1024]{2,1,0:T(8,128)(2,1)S(1)} async-done(((bf16[8,72,1024]{2,1,0:T(8,128)(2,1)}), bf16[8,72,1024]{2,1,0:T(8,128)(2,1)S(1)}, u32[]{:S(2)}, u32[]{:S(2)}) %all-to-all-start) | async-done | bytes 1179680 | tf_op jit(solution)/shard_map/all_to_all | solution.py:120
  77.5 33.3 %reduce-scatter.4.cloned.1.call-done = f32[144,1024]{1,0:T(8,128)} async-done(((f32[576,1024]{1,0:T(8,128)}), f32[144,1024]{1,0:T(8,128)}) %reduce-scatter.4.cloned.1.call-update) | async-done | bytes 589840 | tf_op jit(solution)/shard_map/reduce_scatter | solution.py:130
  113.4 18.0 %all-gather.5.cloned.1.call-done = bf16[576,1024]{1,0:T(8,128)(2,1)} async-done(((bf16[144,1024]{1,0:T(8,128)(2,1)}), bf16[576,1024]{1,0:T(8,128)(2,1)}) %all-gather.5.cloned.1.call-update) | async-done | bytes 1179664 | tf_op jit(solution)/shard_map/all_gather | solution.py:138
  131.3 9.7 multiply_convert_fusion.3
  144.0 5.2 all-to-all-start.2
  150.5 26.9 %all-to-all-done.2 = bf16[8,72,1024]{2,1,0:T(8,128)(2,1)S(1)} async-done(((bf16[8,72,1024]{2,1,0:T(8,128)(2,1)}), bf16[8,72,1024]{2,1,0:T(8,128)(2,1)S(1)}, u32[]{:S(2)}, u32[]{:S(2)}) %all-to-all-start.2) | async-done | bytes 1179680 | tf_op jit(solution)/shard_map/all_to_all | solution.py:121
  187.8 16.8 %all-gather.9.cloned.1.call-done = bf16[576,1024]{1,0:T(8,128)(2,1)} async-done(((bf16[144,1024]{1,0:T(8,128)(2,1)}), bf16[576,1024]{1,0:T(8,128)(2,1)}) %all-gather.9.cloned.1.call-update) | async-done | bytes 1179664 | tf_op jit(solution)/shard_map/all_gather | solution.py:138
  204.6 6.9 fusion.203
  215.4 32.8 %reduce-scatter.8.cloned.1.call-done = f32[144,1024]{1,0:T(8,128)} async-done(((f32[576,1024]{1,0:T(8,128)}), f32[144,1024]{1,0:T(8,128)}) %reduce-scatter.8.cloned.1.call-update) | async-done | bytes 589840 | tf_op jit(solution)/shard_map/reduce_scatter | solution.py:130
  251.9 4.9 convolution_convert_fusion.1
  260.1 9.8 all-gather.11.cloned.1.call-done
  294.3 210.4 %all-reduce.14.cloned.1.call-done = (bf16[3,1024,256]{1,2,0:T(8,128)(2,1)}, bf16[256,1024]{1,0:T(8,128)(2,1)}, bf16[1024,1024]{1,0:T(8,128)(2,1)}, bf16[1024,1024]{1,0:T(8,128)(2,1)}) async-done(((bf16[3,1024,256]{1,2,0:T(8,128)(2,1)}, bf16[256,1024]{1,0:T(8,128)(2,1)}, bf16[1024,1024]{1,0:T(8,128)(2,1)}, bf16[1024,1024]{1,0:T(8,128)(2,1)}), (bf16[3,1024,256]{1,2,0:T(8,128)(2,1)}, ...) | async-done | bytes 6291472 | tf_op jit(solution)/shard_map/psum | solution.py:287
  512.8 4.9 multiply_add_fusion.1
  517.6 4.9 multiply_add_fusion
  522.5 12.6 %conditional.9 = (f32[1024,1024]{1,0:T(8,128)}) conditional(s32[]{:T(128)} %convert_element_type.270, () %tuple.94, (s32[]{:T(128)}, f32[1024,256]{0,1:T(8,128)S(1)}, f32[1024,256]{0,1:T(8,128)S(1)}, f32[1024,256]{0,1:T(8,128)}, f32[256,1024]{1,0:T(8,128)S(1)}, /*index=5*/f32[1024,1024]{1,0:T(8,128)}, f32[1024,1024]{1,0:T(8,128)}) %tuple.95), branch_computations={%region_37.40_spmd, %region_38.47_spmd} | conditional | flops 12884901888 | bytes 8388668 | solution.py:325
  522.5 5.9 conditional
  522.5 5.1 fusion.204
  540.7 91.0 %all-reduce.10.cloned.1.call-done = f32[1024,1024]{1,0:T(8,128)} async-done(((f32[1024,1024]{1,0:T(8,128)}), f32[1024,1024]{1,0:T(8,128)}) %all-reduce.10.cloned.1.call-update) | async-done | bytes 4194320 | tf_op jit(solution)/shard_map/psum | solution.py:326
  635.4 246.5 %conditional.10 = (f32[1024,1024]{1,0:T(8,128)}) conditional(s32[]{:T(128)} %convert_element_type.270, () %tuple.96, (f32[]{:T(128)}, f32[1024,1024]{1,0:T(8,128)}) %tuple.97), branch_computations={%region_47.50_spmd, %region_48.51_spmd} | conditional | flops 219115683840 | bytes 239075392 | solution.py:328
  635.4 18.9 %fusion.6 = f32[1024,1024]{1,0:T(8,128)S(1)} fusion(f32[1024,1024]{1,0:T(8,128)} %get-tuple-element.162, f32[]{:T(128)S(6)} %mul.142), kind=kOutput, calls=%fused_computation.19 | convolution fusion | flops 12893290496 | bytes 8388612 | tf_op jit(solution)/shard_map/cond/branch_1_fun/dot_general | solution.py:68
  654.4 13.5 %fusion.9 = f32[1024,1024]{1,0:T(8,128)S(1)} fusion(f32[1024,1024]{1,0:T(8,128)S(1)} %fusion.6, f32[1024,1024]{1,0:T(8,128)S(1)} %copy-done.14, f32[]{:T(128)S(6)} %mul.142), kind=kOutput, calls=%fused_computation.23 | convolution fusion | flops 12885950464 | bytes 12582916 | tf_op jit(solution)/shard_map/cond/branch_1_fun/dot_general | solution.py:75
  667.8 14.0 %fusion.210 = f32[1024,1024]{1,0:T(8,128)S(1)} fusion(f32[1024,1024]{1,0:T(8,128)S(1)} %fusion.9, f32[1024,1024]{1,0:T(8,128)S(1)} %fusion.6), kind=kOutput, calls=%fused_computation.338 | convolution fusion | flops 12884901888 | bytes 12582912 | tf_op jit(solution)/shard_map/cond/branch_1_fun/dot_general | solution.py:75
  681.9 14.1 %fusion.211 = f32[1024,1024]{1,0:T(8,128)S(1)} fusion(f32[1024,1024]{1,0:T(8,128)S(1)} %fusion.210), kind=kOutput, calls=%fused_computation.339 | convolution fusion | flops 12884901888 | bytes 8388608 | tf_op jit(solution)/shard_map/cond/branch_1_fun/dot_general | solution.py:68
  696.0 14.2 %fusion.15 = f32[1024,1024]{1,0:T(8,128)S(1)} fusion(f32[1024,1024]{1,0:T(8,128)S(1)} %fusion.6, f32[1024,1024]{1,0:T(8,128)S(1)} %fusion.211, f32[1024,1024]{1,0:T(8,128)S(1)} %fusion.210), kind=kOutput, calls=%fused_computation.27 | convolution fusion | flops 12891193344 | bytes 16777216 | tf_op jit(solution)/shard_map/cond/branch_1_fun/dot_general | solution.py:73
  710.2 14.2 %fusion.19 = f32[1024,1024]{1,0:T(8,128)S(1)} fusion(f32[1024,1024]{1,0:T(8,128)S(1)} %fusion.210, f32[1024,1024]{1,0:T(8,128)S(1)} %fusion.211), kind=kOutput, calls=%fused_computation.29 | convolution fusion | flops 12891193344 | bytes 12582912 | tf_op jit(solution)/shard_map/cond/branch_1_fun/dot_general | solution.py:75
  724.4 14.4 %fusion.17 = f32[1024,1024]{1,0:T(8,128)S(1)} fusion(f32[1024,1024]{1,0:T(8,128)S(1)} %fusion.19, f32[1024,1024]{1,0:T(8,128)S(1)} %fusion.211, f32[1024,1024]{1,0:T(8,128)S(1)} %fusion.210), kind=kOutput, calls=%fused_computation.28 | convolution fusion | flops 12891193344 | bytes 16777216 | tf_op jit(solution)/shard_map/cond/branch_1_fun/dot_general | solution.py:75
  738.8 13.9 %fusion.212 = f32[1024,1024]{1,0:T(8,128)S(1)} fusion(f32[1024,1024]{1,0:T(8,128)S(1)} %fusion.17), kind=kOutput, calls=%fused_computation.340 | convolution fusion | flops 12884901888 | bytes 8388608 | tf_op jit(solution)/shard_map/cond/branch_1_fun/dot_general | solution.py:68
  752.7 14.2 %fusion.21 = f32[1024,1024]{1,0:T(8,128)S(1)} fusion(f32[1024,1024]{1,0:T(8,128)S(1)} %fusion.15, f32[1024,1024]{1,0:T(8,128)S(1)} %fusion.212, f32[1024,1024]{1,0:T(8,128)S(1)} %fusion.17), kind=kOutput, calls=%fused_computation.30 | convolution fusion | flops 12891193344 | bytes 16777216 | tf_op jit(solution)/shard_map/cond/branch_1_fun/dot_general | solution.py:73
  766.9 14.4 %fusion.25 = f32[1024,1024]{1,0:T(8,128)S(1)} fusion(f32[1024,1024]{1,0:T(8,128)S(1)} %fusion.17, f32[1024,1024]{1,0:T(8,128)S(1)} %fusion.212), kind=kOutput, calls=%fused_computation.32 | convolution fusion | flops 12891193344 | bytes 12582912 | tf_op jit(solution)/shard_map/cond/branch_1_fun/dot_general | solution.py:75
  781.3 14.2 %fusion.23 = f32[1024,1024]{1,0:T(8,128)S(1)} fusion(f32[1024,1024]{1,0:T(8,128)S(1)} %fusion.25, f32[1024,1024]{1,0:T(8,128)S(1)} %fusion.212, f32[1024,1024]{1,0:T(8,128)S(1)} %fusion.17), kind=kOutput, calls=%fused_computation.31 | convolution fusion | flops 12891193344 | bytes 16777216 | tf_op jit(solution)/shard_map/cond/branch_1_fun/dot_general | solution.py:75
  795.4 13.9 %fusion.213 = f32[1024,1024]{1,0:T(8,128)S(1)} fusion(f32[1024,1024]{1,0:T(8,128)S(1)} %fusion.23), kind=kOutput, calls=%fused_computation.341 | convolution fusion | flops 12884901888 | bytes 8388608 | tf_op jit(solution)/shard_map/cond/branch_1_fun/dot_general | solution.py:68
  809.4 14.4 %fusion.27 = f32[1024,1024]{1,0:T(8,128)S(1)} fusion(f32[1024,1024]{1,0:T(8,128)S(1)} %fusion.21, f32[1024,1024]{1,0:T(8,128)S(1)} %fusion.213, f32[1024,1024]{1,0:T(8,128)S(1)} %fusion.23), kind=kOutput, calls=%fused_computation.33 | convolution fusion | flops 12891193344 | bytes 16777216 | tf_op jit(solution)/shard_map/cond/branch_1_fun/dot_general | solution.py:73
  823.8 14.2 %fusion.31 = f32[1024,1024]{1,0:T(8,128)S(1)} fusion(f32[1024,1024]{1,0:T(8,128)S(1)} %fusion.23, f32[1024,1024]{1,0:T(8,128)S(1)} %fusion.213), kind=kOutput, calls=%fused_computation.35 | convolution fusion | flops 12891193344 | bytes 12582912 | tf_op jit(solution)/shard_map/cond/branch_1_fun/dot_general | solution.py:75
  838.0 14.2 %fusion.29 = f32[1024,1024]{1,0:T(8,128)S(1)} fusion(f32[1024,1024]{1,0:T(8,128)S(1)} %fusion.31, f32[1024,1024]{1,0:T(8,128)S(1)} %fusion.213, f32[1024,1024]{1,0:T(8,128)S(1)} %fusion.23), kind=kOutput, calls=%fused_computation.34 | convolution fusion | flops 12891193344 | bytes 16777216 | tf_op jit(solution)/shard_map/cond/branch_1_fun/dot_general | solution.py:75
  852.2 14.1 %fusion.214 = f32[1024,1024]{1,0:T(8,128)S(1)} fusion(f32[1024,1024]{1,0:T(8,128)S(1)} %fusion.29), kind=kOutput, calls=%fused_computation.342 | convolution fusion | flops 12884901888 | bytes 8388608 | tf_op jit(solution)/shard_map/cond/branch_1_fun/dot_general | solution.py:68
  866.3 15.5 %fusion.1 = f32[1024,1024]{1,0:T(8,128)} fusion(f32[1024,1024]{1,0:T(8,128)S(1)} %fusion.27, f32[1024,1024]{1,0:T(8,128)S(1)} %fusion.214, f32[1024,1024]{1,0:T(8,128)S(1)} %fusion.29), kind=kOutput, calls=%fused_computation.15 | convolution fusion | flops 12891193344 | bytes 16777216 | tf_op jit(solution)/shard_map/cond/branch_1_fun/dot_general | solution.py:73
  883.6 12.2 %conditional.12 = (bf16[1024,256]{1,0:T(8,128)(2,1)}) conditional(s32[]{:T(128)} %convert_element_type.271, () %tuple.99, (f32[]{:T(128)}, f32[1024,256]{0,1:T(8,128)S(1)}, f32[1024,1024]{1,0:T(8,128)}) %tuple.100), branch_computations={%region_52.55_spmd, %region_53.56_spmd} | conditional | flops 3222011904 | bytes 8912908 | solution.py:342
  896.7 7.1 conditional.15
  905.2 10.4 conditional.11
  905.5 9.0 fusion.116
  921.9 5.3 gather_fusion.3
  927.2 5.3 gather_fusion.7
  934.2 81.3 %all_to_all.20 = bf16[8,72,1024]{2,1,0:T(8,128)(2,1)S(1)} all-to-all(bf16[8,72,1024]{2,1,0:T(8,128)(2,1)S(1)} %bitcast.134), channel_id=1, replica_groups=mesh['dp'=8,'tensor'=4] {'dp'}, dimensions={0} | all-to-all | bytes 2359296 | tf_op jit(solution)/shard_map/all_to_all | solution.py:199
  1024.4 10.3 psum.119
  1034.9 49.3 %all-reduce = (bf16[2,256]{1,0:T(2,128)(2,1)S(1)}, bf16[1024]{0:T(1024)(128)(2,1)S(1)}, bf16[6,1024]{1,0:T(8,128)(2,1)S(1)}) all-reduce(bf16[2,256]{1,0:T(2,128)(2,1)S(1)} %pad_maximum_fusion.3, bf16[1024]{0:T(1024)(128)(2,1)S(1)} %copy-done.53, bf16[6,1024]{1,0:T(8,128)(2,1)S(1)} %psum.119), channel_id=1, replica_groups=mesh['dp'=8,'tensor'=4] {'dp'}, use_global_device_ids=true, to_apply=%region_26.29 | all-reduce | flops 7680 | bytes 30720 | tf_op jit(solution)/shard_map/psum | solution.py:291
  1104.8 98.6 %all-reduce.12.cloned.1.call-done = (bf16[1,1024,256]{2,1,0:T(8,128)(2,1)}, bf16[1,1024,256]{2,1,0:T(8,128)(2,1)}, bf16[1,1024,256]{2,1,0:T(8,128)(2,1)}, bf16[2...) async-done(((bf16[1,1024,256]{2,1,0:T(8,128)(2,1)}, bf16[1,1024,256]{2,1,0:T(8,128)(2,1)}, bf16[1,1024,256]{2,1,0:T(8,128)(2,1)}, ...) | async-done | bytes 6291472 | tf_op jit(solution)/shard_map/psum | solution.py:29
  (291 shorter events, 157.0 us)
Async XLA Ops:
  7.2 15.3 %copy-start = (bf16[576,1024]{1,0:T(8,128)(2,1)S(1)}, bf16[576,1024]{1,0:T(8,128)(2,1)}, u32[]{:S(2)}) copy-start(bf16[576,1024]{1,0:T(8,128)(2,1)} %param.45) | copy-start | bytes 3538948
  7.2 13.7 %copy-start.56 = (s32[1,3]{1,0:T(1,128)S(1)}, s32[1,3]{1,0:T(1,128)}, u32[]{:S(2)}) copy-start(s32[1,3]{1,0:T(1,128)} %param.46) | copy-start | bytes 40
  15.0 7.4 copy-start.36
  28.2 9.1 copy-start.45
  29.9 34.1 %all-to-all-start = ((bf16[8,72,1024]{2,1,0:T(8,128)(2,1)}), bf16[8,72,1024]{2,1,0:T(8,128)(2,1)S(1)}, u32[]{:S(2)}, u32[]{:S(2)}) async-start(bf16[8,72,1024]{2,1,0:T(8,128)(2,1)} %bitcast.4), calls=%async_computation | async-start | bytes 2359296 | tf_op jit(solution)/shard_map/all_to_all | solution.py:120
  36.3 74.6 %reduce-scatter.4.cloned.1.call-start = ((), (), s32[]{:S(2)}) async-start(), calls=%async_computation.7 | async-start | bytes 2949120 | tf_op jit(solution)/shard_map/reduce_scatter | solution.py:130
  37.3 26.7 %copy-start.34 = (s32[576]{0:T(1024)}, s32[576]{0:T(1024)S(1)}, u32[]{:S(2)}) copy-start(s32[576]{0:T(1024)S(1)} %sub.135) | copy-start | bytes 6916
  75.2 38.1 %copy-start.24 = (bf16[4,64,576]{2,1,0:T(8,128)(2,1)}, bf16[4,64,576]{2,1,0:T(8,128)(2,1)S(1)}, u32[]{:S(2)}) copy-start(bf16[4,64,576]{2,1,0:T(8,128)(2,1)S(1)} %fusion.159) | copy-start | bytes 884740
  75.5 55.8 %copy-start.49 = (f32[1024]{0:T(1024)S(1)}, f32[1024]{0:T(1024)}, u32[]{:S(2)}) copy-start(f32[1024]{0:T(1024)} %param.53) | copy-start | bytes 12292
  77.4 53.9 %all-gather.5.cloned.1.call-start = ((), (), s32[]{:S(2)}) async-start(), calls=%async_computation.8 | async-start | bytes 1474560 | tf_op jit(solution)/shard_map/all_gather | solution.py:138
  113.3 67.5 %reduce-scatter.6.cloned.1.call-start = ((), (), s32[]{:S(2)}) async-start(), calls=%async_computation.9 | async-start | bytes 2949120 | tf_op jit(solution)/shard_map/reduce_scatter | solution.py:130
  131.3 9.8 copy-start.33
  144.0 33.4 %all-to-all-start.2 = ((bf16[8,72,1024]{2,1,0:T(8,128)(2,1)}), bf16[8,72,1024]{2,1,0:T(8,128)(2,1)S(1)}, u32[]{:S(2)}, u32[]{:S(2)}) async-start(bf16[8,72,1024]{2,1,0:T(8,128)(2,1)} %bitcast.133), calls=%async_computation.4 | async-start | bytes 2359296 | tf_op jit(solution)/shard_map/all_to_all | solution.py:121
  149.2 55.4 %all-gather.9.cloned.1.call-start = ((), (), s32[]{:S(2)}) async-start(), calls=%async_computation.11 | async-start | bytes 1474560 | tf_op jit(solution)/shard_map/all_gather | solution.py:138
  187.8 60.4 %reduce-scatter.8.cloned.1.call-start = ((), (), s32[]{:S(2)}) async-start(), calls=%async_computation.12 | async-start | bytes 2949120 | tf_op jit(solution)/shard_map/reduce_scatter | solution.py:130
  204.6 7.9 copy-start.32
  215.3 54.6 %all-gather.11.cloned.1.call-start = ((), (), s32[]{:S(2)}) async-start(), calls=%async_computation.13 | async-start | bytes 1474560 | tf_op jit(solution)/shard_map/all_gather | solution.py:138
  251.0 5.9 copy-start.7
  251.9 252.8 %all-reduce.14.cloned.1.call-start = ((), (), s32[]{:S(2)}) async-start(), calls=%async_computation.17 | async-start | bytes 12582912 | tf_op jit(solution)/shard_map/psum | solution.py:287
  251.9 5.0 copy-start.55
  251.9 5.0 copy-start.58
  271.9 8.7 slice-start
  290.5 341.3 %all-reduce.10.cloned.1.call-start = ((), (), s32[]{:S(2)}) async-start(), calls=%async_computation.15 | async-start | bytes 8388608 | tf_op jit(solution)/shard_map/psum | solution.py:326
  507.7 5.1 copy-start.20
  510.3 407.1 %copy-start.5 = (f32[256,1024]{1,0:T(8,128)}, f32[256,1024]{1,0:T(8,128)S(1)}, u32[]{:S(2)}) copy-start(f32[256,1024]{1,0:T(8,128)S(1)} %get-tuple-element.393) | copy-start | bytes 3145732
  512.8 4.9 copy-start.19
  535.2 386.7 %all-gather.7.cloned.1.call-start = ((), (), s32[]{:S(2)}) async-start(), calls=%async_computation.10 | async-start | bytes 1474560 | tf_op jit(solution)/shard_map/all_gather | solution.py:138
  535.9 391.3 %all-reduce.8.cloned.1.call-start = ((), (), s32[]{:S(2)}) async-start(), calls=%async_computation.14 | async-start | bytes 2359296 | tf_op jit(solution)/shard_map/psum | solution.py:283
  540.7 662.7 %all-reduce.12.cloned.1.call-start = ((), (), s32[]{:S(2)}) async-start(), calls=%async_computation.16 | async-start | bytes 12582912 | tf_op jit(solution)/shard_map/psum | solution.py:29
  635.4 19.0 %copy-start.14 = (f32[1024,1024]{1,0:T(8,128)S(1)}, f32[1024,1024]{1,0:T(8,128)}, u32[]{:S(2)}) copy-start(f32[1024,1024]{1,0:T(8,128)} %get-tuple-element.162) | copy-start | bytes 12582916 | tf_op jit(solution)/shard_map/cond
  932.6 87.3 %copy-start.38 = (s32[576]{0:T(1024)S(1)}, s32[576]{0:T(1024)}, u32[]{:S(2)}) copy-start(s32[576]{0:T(1024)} %copy-done.37) | copy-start | bytes 6916
  932.6 91.7 %copy-start.42 = (bf16[1024]{0:T(1024)(128)(2,1)S(1)}, bf16[1024]{0:T(1024)(128)(2,1)}, u32[]{:S(2)}) copy-start(bf16[1024]{0:T(1024)(128)(2,1)} %get-tuple-element.395) | copy-start | bytes 6148
  932.6 91.7 %copy-start.41 = (bf16[1024]{0:T(1024)(128)(2,1)S(1)}, bf16[1024]{0:T(1024)(128)(2,1)}, u32[]{:S(2)}) copy-start(bf16[1024]{0:T(1024)(128)(2,1)} %get-tuple-element.357) | copy-start | bytes 6148
  932.6 91.7 %copy-start.40 = (bf16[1024]{0:T(1024)(128)(2,1)S(1)}, bf16[1024]{0:T(1024)(128)(2,1)}, u32[]{:S(2)}) copy-start(bf16[1024]{0:T(1024)(128)(2,1)} %get-tuple-element.362) | copy-start | bytes 6148
  932.6 91.7 %copy-start.47 = (bf16[1024]{0:T(1024)(128)(2,1)S(1)}, bf16[1024]{0:T(1024)(128)(2,1)}, u32[]{:S(2)}) copy-start(bf16[1024]{0:T(1024)(128)(2,1)} %get-tuple-element.397) | copy-start | bytes 6148
  932.6 91.7 %copy-start.44 = (bf16[1024]{0:T(1024)(128)(2,1)S(1)}, bf16[1024]{0:T(1024)(128)(2,1)}, u32[]{:S(2)}) copy-start(bf16[1024]{0:T(1024)(128)(2,1)} %get-tuple-element.360) | copy-start | bytes 6148
  932.6 91.7 %copy-start.43 = (bf16[1024]{0:T(1024)(128)(2,1)S(1)}, bf16[1024]{0:T(1024)(128)(2,1)}, u32[]{:S(2)}) copy-start(bf16[1024]{0:T(1024)(128)(2,1)} %get-tuple-element.364) | copy-start | bytes 6148
  932.7 102.0 %copy-start.48 = (bf16[4,64]{1,0:T(4,128)(2,1)S(1)}, bf16[4,64]{1,0:T(4,128)(2,1)}, u32[]{:S(2)}) copy-start(bf16[4,64]{1,0:T(4,128)(2,1)} %get-tuple-element.431) | copy-start | bytes 1540
  932.7 102.1 %copy-start.52 = (bf16[4,64]{1,0:T(4,128)(2,1)S(1)}, bf16[4,64]{1,0:T(4,128)(2,1)}, u32[]{:S(2)}) copy-start(bf16[4,64]{1,0:T(4,128)(2,1)} %get-tuple-element.433) | copy-start | bytes 1540
  932.7 102.2 %copy-start.53 = (bf16[1024]{0:T(1024)(128)(2,1)S(1)}, bf16[1024]{0:T(1024)(128)(2,1)}, u32[]{:S(2)}) copy-start(bf16[1024]{0:T(1024)(128)(2,1)} %get-tuple-element.435) | copy-start | bytes 6148
  932.7 151.5 %copy-start.46 = (f32[2,256]{1,0:T(2,128)S(1)}, f32[2,256]{1,0:T(2,128)}, u32[]{:S(2)}) copy-start(f32[2,256]{1,0:T(2,128)} %param.52) | copy-start | bytes 6148
  932.7 151.5 %copy-start.54 = (f32[2,256]{1,0:T(2,128)S(1)}, f32[2,256]{1,0:T(2,128)}, u32[]{:S(2)}) copy-start(f32[2,256]{1,0:T(2,128)} %param.59) | copy-start | bytes 6148
  932.7 152.1 %copy-start.50 = (f32[1024]{0:T(1024)S(1)}, f32[1024]{0:T(1024)}, u32[]{:S(2)}) copy-start(f32[1024]{0:T(1024)} %param.53) | copy-start | bytes 12292
  932.7 152.1 %copy-start.51 = (f32[1024]{0:T(1024)S(1)}, f32[1024]{0:T(1024)}, u32[]{:S(2)}) copy-start(f32[1024]{0:T(1024)} %param.60) | copy-start | bytes 12292
  932.7 152.7 %copy-start.31 = (f32[6,1024]{1,0:T(8,128)S(1)}, f32[6,1024]{1,0:T(8,128)}, u32[]{:S(2)}) copy-start(f32[6,1024]{1,0:T(8,128)} %param.54) | copy-start | bytes 73732
  932.8 152.6 %copy-start.39 = (f32[6,1024]{1,0:T(8,128)S(1)}, f32[6,1024]{1,0:T(8,128)}, u32[]{:S(2)}) copy-start(f32[6,1024]{1,0:T(8,128)} %param.61) | copy-start | bytes 73732
  1015.6 73.9 %all-to-all-start.3 = ((bf16[8,72,1024]{2,1,0:T(8,128)(2,1)}), bf16[8,72,1024]{2,1,0:T(8,128)(2,1)}, u32[]{:S(2)}, u32[]{:S(2)}) async-start(bf16[8,72,1024]{2,1,0:T(8,128)(2,1)} %bitcast.34), calls=%async_computation.6 | async-start | bytes 2359296 | tf_op jit(solution)/shard_map/all_to_all | solution.py:368
  1100.9 109.8 %copy-start.1 = (bf16[576,1024]{1,0:T(8,128)(2,1)S(1)}, bf16[576,1024]{1,0:T(8,128)(2,1)}, u32[]{:S(2)}) copy-start(bf16[576,1024]{1,0:T(8,128)(2,1)} %param.45) | copy-start | bytes 3538948
  (28 other events, 85.3 us)
Sparse Core Ops, SparseCore 0:
  77.6 33.2 reduce-scatter.3
  113.4 17.8 all-gather.4
  144.1 32.6 reduce-scatter.5
  187.9 16.6 all-gather.8
  215.4 32.6 reduce-scatter.7
  252.0 17.8 all-gather.10
  290.6 213.9 all-reduce.13
  535.3 96.4 all-reduce.9
  633.4 18.1 all-gather.6
  654.6 36.8 all-reduce.7
  921.3 282.0 all-reduce.11
where the time goes:
time: 1220 us
  waiting for transfers between devices  560 us (46%)
  matrix products  320 us (26%)
  blocking collectives  141 us (12%)
  other arithmetic  79.1 us (6%)
  local copies, waits for them, and re-layouts  59.7 us (5%)
  loops' own time  24.9 us (2%)
  starting transfers between devices  17.1 us (1%)
  between operations  15.9 us (1%)
    psum x1, waiting for transfers between devices, body(): lax.psum(grad_qkv_w.astype(jnp.bfloat16), 'dp').astype(jnp.float32)  210 us
    psum x1, waiting for transfers between devices, broadcast(): return lax.psum(jnp.where(mine, value, jnp.zeros_like(value)), axis)  98.6 us
    psum x1, waiting for transfers between devices, body(): gram = lax.psum(gram_part, 'tensor')  91 us
    all_to_all x1, blocking collectives, body(): lax.all_to_all(back_y, 'dp', split_axis=0, concat_axis=0, tiled=True)  81.3 us
    dot_general x5, matrix products, polar_factor(): square = jnp.dot(current, current, precision=highest)  75 us
    reduce_scatter x3, waiting for transfers between devices, reduce_rows(): lax.psum_scatter(term_of(jnp.int32(0), share_rows * lax.axis_size('tensor...  66.1 us
    dot_general x4, matrix products, polar_factor(): factor = jnp.dot(poly, factor, precision=highest)  58.3 us
    dot_general x4, matrix products, polar_factor(): jnp.dot(jnp.dot(poly, current, precision=highest), poly, precision=highest)  56.8 us
  transfers between devices with their start and end apart: 14, of which 10 were waited for; matrix products, arithmetic and copies ran while one was open for 27% of the time, Pallas kernels for 0%

commit v1 on v0

v1 whole, which is shorter than its diff:
```python
import functools
import math

import jax
import jax.numpy as jnp
from jax import lax
from jax.experimental import pallas as pl
from jax.experimental.pallas import tpu as pltpu
from jax.sharding import PartitionSpec as P

D = 1024
HEAD = 64

eps_norm = 1e-05
coef_one = 3.4445
coef_two = -4.775
coef_three = 2.0315
momentum_decay = 0.9
rate_matrix = 0.1
masked_score = -1000000000.0
bf16 = jnp.bfloat16
f32 = jnp.float32


def short(value):
    return value.astype(bf16)


def wide(value):
    return value.astype(f32)


def mm(left, right):
    return jnp.dot(short(left), short(right), preferred_element_type=f32)


def mm_nt(left, right):
    return lax.dot_general(
        short(left), short(right), (((1,), (1,)), ((), ())), preferred_element_type=f32
    )


def mm_tn(left, right):
    return lax.dot_general(
        short(left), short(right), (((0,), (0,)), ((), ())), preferred_element_type=f32
    )


def norm_forward(values, gain_row, shift_row):
    average = jnp.mean(values, axis=-1, keepdims=True)
    centred = values - average
    variance = jnp.mean(centred * centred, axis=-1, keepdims=True)
    inverse = lax.rsqrt(variance + eps_norm)
    normed = centred * inverse
    return (normed, inverse, normed * gain_row + shift_row)


def norm_backward(upstream, normed, inverse, gain_row):
    scaled = upstream * gain_row
    centre_term = jnp.mean(scaled, axis=-1, keepdims=True)
    slope_term = jnp.mean(scaled * normed, axis=-1, keepdims=True)
    return inverse * (scaled - centre_term - normed * slope_term)


class Ring:
    def __init__(self, axes, sizes, digit, members=None):
        self.axes = axes
        self.count = sizes[digit]
        self.below = math.prod(sizes[digit + 1 :])
        self.total = math.prod(sizes)
        self.members = members

    def send(self, value, offset):
        count, below = self.count, self.below
        pairs = []
        for i in range(self.total):
            if self.members is not None and not self.members(i):
                continue
            at = (i // below) % count
            pairs.append((i, i + ((at + offset) % count - at) * below))
        return lax.ppermute(value, self.axes, pairs)

    def place(self, linear):
        return (linear // self.below) % self.count


def cut(value, index, size, axis):
    return lax.dynamic_slice_in_dim(value, index * size, size, axis)


def ring_scatter(value, axis, ring, place):
    size = value.shape[axis] // ring.count
    if ring.count == 1:
        return wide(value)
    total = short(cut(value, (place - 1) % ring.count, size, axis))
    for step in range(ring.count - 1):
        arrived = ring.send(total, 1)
        mine = cut(value, (place - 2 - step) % ring.count, size, axis)
        total = wide(mine) + wide(arrived)
        if step < ring.count - 2:
            total = short(total)
    return total


def ring_gather(piece, axis, ring, place):
    if ring.count == 1:
        return piece
    size = piece.shape[axis]
    shape = list(piece.shape)
    shape[axis] = size * ring.count
    whole = lax.dynamic_update_slice_in_dim(
        jnp.zeros(shape, piece.dtype), piece, place * size, axis
    )
    for step in range(1, ring.count):
        piece = ring.send(piece, 1)
        whole = lax.dynamic_update_slice_in_dim(
            whole, piece, ((place - step) % ring.count) * size, axis
        )
    return whole


def ring_sum_kernel(
    inner, halves, x_ref, small_ref, o_ref, small_sum_ref, got, small_got, send_sems, recv_sems, small_sems
):
    count = lax.axis_size("dp")
    index = lax.axis_index("dp")
    team = lax.axis_index("tensor")
    outer = count // inner
    if inner == 2:
        place = jnp.where(index % 2 == 0, index // 2, count - 1 - index // 2)

        def device(p):
            return jnp.where(p < outer, 2 * p, 2 * (count - 1 - p) + 1)
    else:
        place = index

        def device(p):
            return p

    targets = (device((place + 1) % count), device((place + count - 1) % count))
    barrier = pltpu.get_barrier_semaphore()

    def greet(hop, carry):
        pl.semaphore_signal(
            barrier,
            inc=1,
            device_id=((index + hop) % count, team),
            device_id_type=pl.DeviceIdType.MESH,
        )
        return carry

    lax.fori_loop(1, count, greet, 0)
    pl.semaphore_wait(barrier, count - 1)
    half = x_ref.shape[0] // 2
    chunk = half // count
    sub = chunk // halves
    streams = [(d, h) for h in range(halves) for d in range(2)]

    def rows(d, h, hop):
        at = (place + count - hop) % count if d == 0 else (place + hop) % count
        return pl.ds(pl.multiple_of(d * half + at * chunk + h * sub, 8), sub)

    def copy(d, h, step, src, dst):
        return pltpu.make_async_remote_copy(
            src_ref=src,
            dst_ref=dst,
            send_sem=send_sems.at[step, d, h],
            recv_sem=recv_sems.at[step, d, h],
            device_id=(targets[d], team),
            device_id_type=pl.DeviceIdType.MESH,
        )

    def copies(step):
        made = []
        for d, h in streams:
            if step < count - 1:
                slot = got.at[step, d, pl.ds(h * sub, sub)]
                src = x_ref.at[rows(d, h, 1)] if step == 0 else got.at[step - 1, d, pl.ds(h * sub, sub)]
                made.append(copy(d, h, step, src, slot))
            else:
                at = o_ref.at[rows(d, h, step - (count - 1))]
                made.append(copy(d, h, step, at, at))
        return made

    everything = []
    flying = copies(0)
    for one in flying:
        one.start()
    everything += flying

    def small_copy(hop):
        return pltpu.make_async_remote_copy(
            src_ref=small_ref,
            dst_ref=small_got.at[hop],
            send_sem=small_sems.at[0, hop],
            recv_sem=small_sems.at[1, hop],
            device_id=((index + hop) % count, team),
            device_id_type=pl.DeviceIdType.MESH,
        )

    def small_send(hop, carry):
        small_copy(hop).start()
        return carry

    def small_wait(hop, total):
        one = small_copy(hop)
        one.wait_send()
        one.wait_recv()
        return total + wide(small_got[hop])

    lax.fori_loop(1, count, small_send, 0)
    for step in range(2 * (count - 1)):
        following = copies(step + 1) if step < 2 * count - 3 else [None] * len(streams)
        for (d, h), one, then in zip(streams, flying, following):
            one.wait_recv()
            if step < count - 1:
                total = wide(got[step, d, pl.ds(h * sub, sub)]) + wide(x_ref[rows(d, h, step + 2)])
                if step < count - 2:
                    got[step, d, pl.ds(h * sub, sub)] = short(total)
                else:
                    o_ref[rows(d, h, 0)] = short(total)
            if then is not None:
                then.start()
        flying = following
        everything += [one for one in following if one is not None]
    small_sum_ref[...] = lax.fori_loop(1, count, small_wait, wide(small_ref[...]))
    for one in everything:
        one.wait_send()


def ring_sum(value, small, inner, groups):
    length, columns = value.shape
    halves = 2 if length % (64 * groups) == 0 else 1
    steps = 2 * (groups - 1)
    chunk = length // 2 // groups
    return pl.pallas_call(
        functools.partial(ring_sum_kernel, inner, halves),
        name="ring_sum",
        out_shape=(
            jax.ShapeDtypeStruct(value.shape, bf16),
            jax.ShapeDtypeStruct(small.shape, f32),
        ),
        in_specs=[pl.BlockSpec(memory_space=pltpu.VMEM)] * 2,
        out_specs=[pl.BlockSpec(memory_space=pltpu.VMEM)] * 2,
        scratch_shapes=[
            pltpu.VMEM((groups - 1, 2, chunk, columns), bf16),
            pltpu.VMEM((groups, *small.shape), bf16),
            pltpu.SemaphoreType.DMA((steps, 2, halves)),
            pltpu.SemaphoreType.DMA((steps, 2, halves)),
            pltpu.SemaphoreType.DMA((2, groups)),
        ],
        compiler_params=pltpu.CompilerParams(
            collective_id=0, has_side_effects=True, vmem_limit_bytes=40 * 2**20
        ),
        cost_estimate=pl.CostEstimate(
            flops=length * columns, bytes_accessed=4 * length * columns, transcendentals=0
        ),
    )(value, small)


def dot(left, right):
    return jnp.dot(left, right, preferred_element_type=f32)

def dot_nt(left, right):
    return lax.dot_general(left, right, (((1,), (1,)), ((), ())), preferred_element_type=f32)

def polar_kernel(block, m_ref, o_ref, x_ref, gram_ref, low_ref):
    size = m_ref.shape[0]
    keep = o_ref.shape[1]
    blocks = size // block

    def rows(i):
        return pl.ds(pl.multiple_of(i * block, block), block)

    def norm_step(i, total):
        part = wide(m_ref[rows(i), :])
        return total + jnp.sum(part * part, axis=0, keepdims=True)

    total = lax.fori_loop(0, blocks, norm_step, jnp.zeros((1, m_ref.shape[1]), f32))
    scale = lax.rsqrt(jnp.sum(total, axis=1, keepdims=True) + 1e-07)

    def scale_step(i, carry):
        x_ref[0, rows(i), :] = short(wide(m_ref[rows(i), :]) * scale)
        return carry

    lax.fori_loop(0, blocks, scale_step, 0)

    def sweep(now, last):
        x = x_ref.at[now]

        def gram_step(i, carry):
            gram = dot_nt(x[rows(i), :], x[...])
            gram_ref[rows(i), :] = gram
            low_ref[rows(i), :] = short(gram)
            return carry

        lax.fori_loop(0, blocks, gram_step, 0)

        def mix_step(i, carry):
            mixing = coef_two * gram_ref[rows(i), :] + coef_three * dot(low_ref[rows(i), :], low_ref[...])
            if last:
                o_ref[rows(i), :] = short(coef_one * wide(x[rows(i), :keep]) + dot(short(mixing), x[:, :keep]))
            else:
                x_ref[1 - now, rows(i), :] = short(coef_one * wide(x[rows(i), :]) + dot(short(mixing), x[...]))
            return carry

        lax.fori_loop(0, blocks, mix_step, 0)

    def two(k, carry):
        sweep(0, False)
        sweep(1, False)
        return carry

    lax.fori_loop(0, 2, two, 0)
    sweep(0, True)

def polar_columns(matrix, keep):
    size = matrix.shape[0]
    return pl.pallas_call(
        functools.partial(polar_kernel, 512),
        name="polar",
        out_shape=jax.ShapeDtypeStruct((size, keep), bf16),
        in_specs=[pl.BlockSpec(memory_space=pltpu.VMEM)],
        out_specs=pl.BlockSpec(memory_space=pltpu.VMEM),
        scratch_shapes=[
            pltpu.VMEM((2, size, matrix.shape[1]), bf16),
            pltpu.VMEM((size, size), f32),
            pltpu.VMEM((size, size), bf16),
        ],
        compiler_params=pltpu.CompilerParams(vmem_limit_bytes=32 * 2**20),
    )(matrix)


def factor_kernel(block, g_ref, o_ref, cur_ref, high_ref, low_ref, poly_ref, factor_ref):
    tile = g_ref.shape[1]
    tiles = cur_ref.shape[1] // tile
    size = cur_ref.shape[1]
    blocks = size // block
    keep = o_ref.shape[1]
    first = lax.axis_index("tensor") * keep
    k = 0
    trace = jnp.zeros((1, 1), f32)
    eye = (lax.broadcasted_iota(jnp.int32, (tile, tile), 0) == lax.broadcasted_iota(jnp.int32, (tile, tile), 1))
    for i in range(tiles):
        for j in range(i, tiles):
            part = g_ref[k]
            cur_ref[0, i*tile:(i+1)*tile, j*tile:(j+1)*tile] = part
            if i != j:
                cur_ref[0, j*tile:(j+1)*tile, i*tile:(i+1)*tile] = part.T
            else:
                diag = jnp.where(eye, part, 0.0)
                trace = trace + jnp.sum(jnp.sum(diag, axis=0, keepdims=True), axis=1, keepdims=True)
            k += 1
    scale = lax.rsqrt(trace + 1e-07)
    scale_two = scale * scale

    def rows(i):
        return pl.ds(pl.multiple_of(i * block, block), block)

    def scale_step(i, carry):
        cur_ref[0, rows(i), :] = cur_ref[0, rows(i), :] * scale_two
        return carry

    lax.fori_loop(0, blocks, scale_step, 0)

    def sweep(k, exact, finer):
        now = k % 2
        cur = cur_ref.at[now]

        def split_step(i, carry):
            value = cur[rows(i), :]
            high = short(value)
            high_ref[rows(i), :] = high
            if exact or finer:
                low_ref[rows(i), :] = short(value - wide(high))
            return carry

        lax.fori_loop(0, blocks, split_step, 0)

        def poly_step(i, carry):
            r = lax.broadcasted_iota(jnp.int32, (block, size), 0) + i * block
            c = lax.broadcasted_iota(jnp.int32, (block, size), 1)
            power = dot(high_ref[rows(i), :], high_ref[...])
            if finer:
                power = power + dot(high_ref[rows(i), :], low_ref[...])
            poly = coef_two * cur[rows(i), :] + coef_three * power
            poly = poly + jnp.where(r == c, coef_one, 0.0)
            poly_ref[rows(i), :] = short(poly)
            return carry

        lax.fori_loop(0, blocks, poly_step, 0)

        def next_step(i, carry):
            half = dot(poly_ref[rows(i), :], high_ref[...])
            if exact:
                half = half + dot(poly_ref[rows(i), :], low_ref[...])
            half_high = short(half)
            new = dot(half_high, poly_ref[...])
            if exact:
                new = new + dot(short(half - wide(half_high)), poly_ref[...])
            cur_ref[1 - now, rows(i), :] = new
            return carry

        if k < 4:
            lax.fori_loop(0, blocks, next_step, 0)

        def factor_step(i, carry):
            if k == 0:
                columns = pl.ds(pl.multiple_of(first, 128), keep)
                factor_ref[0, rows(i), :] = poly_ref[rows(i), columns]
            else:
                before = factor_ref[1 - now]
                new = dot(poly_ref[rows(i), :], before)
                if k < 4:
                    factor_ref[now, rows(i), :] = short(new)
                else:
                    o_ref[rows(i), :] = short(new * scale)
            return carry

        lax.fori_loop(0, blocks, factor_step, 0)

    for k in range(5):
        sweep(k, k < 2, k > 2)

def factor_columns(tiles, size, keep):
    return pl.pallas_call(
        functools.partial(factor_kernel, 512),
        name="factor",
        out_shape=jax.ShapeDtypeStruct((size, keep), bf16),
        in_specs=[pl.BlockSpec(memory_space=pltpu.VMEM)],
        out_specs=pl.BlockSpec(memory_space=pltpu.VMEM),
        scratch_shapes=[
            pltpu.VMEM((2, size, size), f32),
            pltpu.VMEM((size, size), bf16),
            pltpu.VMEM((size, size), bf16),
            pltpu.VMEM((size, size), bf16),
            pltpu.VMEM((2, size, keep), bf16),
        ],
        compiler_params=pltpu.CompilerParams(vmem_limit_bytes=40 * 2**20),
    )(tiles)


def body(
    layout,
    tokens,
    cotangent,
    lengths,
    packing,
    w_qkv,
    w_out,
    w_up,
    w_down,
    bias_qv,
    bias_up,
    vectors,
    mom_qkv,
    mom_out,
    mom_up,
    mom_down,
    mom_bias_qv,
    mom_bias_up,
    mom_vectors,
):
    inner, cores = layout
    groups = lax.axis_size("dp")
    teams = lax.axis_size("tensor")
    group = lax.axis_index("dp")
    team = lax.axis_index("tensor")
    outer, wides = groups // inner, teams // cores
    count = tokens.shape[0]
    per_peer = count // groups
    share = count // teams
    width = D // teams
    all_tokens = count * groups

    outer_ring = Ring("dp", (outer, inner), 0)
    inner_ring = Ring("dp", (outer, inner), 1)
    outer_at, inner_at = outer_ring.place(group), inner_ring.place(group)
    x_ring = Ring("tensor", (wides, cores), 0)
    core_ring = Ring("tensor", (wides, cores), 1)
    x_at, core_at = x_ring.place(team), core_ring.place(team)

    def team_of(rank):
        return ((x_at + rank % wides) % wides) * cores + (core_at + rank // wides) % cores

    def to_relative(value, size, axis=0):
        return jnp.concatenate([cut(value, team_of(r), size, axis) for r in range(teams)], axis)

    def to_given(value, size, axis=0):
        parts = []
        for other in range(teams):
            rank = ((other % cores - core_at) % cores) * wides + (other // cores - x_at) % wides
            parts.append(cut(value, rank, size, axis))
        return jnp.concatenate(parts, axis)

    def spread_list(piece, ring_x=x_ring, ring_core=core_ring):
        line = [piece]
        for _ in range(wides - 1):
            line.append(ring_x.send(line[-1], -1))
        pieces = list(line)
        for hop in range(1, cores):
            pieces += [ring_core.send(p, -hop) for p in line]
        return pieces

    def spread_rows(piece):
        return jnp.concatenate(spread_list(piece), 0)

    def spread_columns(piece):
        return to_given(jnp.concatenate(spread_list(piece), 1), piece.shape[1], 1)

    def reduce_rows(partial):
        block = wides * share
        held = partial[:block]
        for hop in range(1, cores):
            held = held + wide(core_ring.send(short(partial[hop * block : (hop + 1) * block]), hop))
        total = held[(wides - 1) * share :]
        for i in range(wides - 2, -1, -1):
            total = held[i * share : (i + 1) * share] + wide(x_ring.send(short(total), 1))
        return total

    def own_rows(value):
        return cut(value, team, share, 0)

    position = jnp.arange(count, dtype=jnp.int32)
    peer = jnp.arange(groups, dtype=jnp.int32)
    packed = packing.reshape(groups, count)
    source = packed // count
    source_mine = lax.dynamic_index_in_dim(source, group, 0, keepdims=False)
    masks = jnp.concatenate([source == group, source_mine[None, :] == peer[:, None]], 0)
    before = (position[:, None] < position[None, :]).astype(bf16)
    rank = mm(masks.astype(bf16), before).astype(jnp.int32)
    key = jnp.where(masks, rank, -1)
    value = jnp.concatenate(
        [packed % count, jnp.broadcast_to(position[None, :], (groups, count))], 0
    )
    slot_in_message = jnp.arange(per_peer, dtype=jnp.int32)
    picked = jnp.sum(
        jnp.where(key[:, None, :] == slot_in_message[None, :, None], value[:, None, :], 0), axis=-1
    )
    rows_sent = picked[:groups].reshape(count)
    slots = picked[groups:].reshape(count)
    choose = (rows_sent[:, None] == position[None, :]).astype(bf16)

    length_row = lengths[0]
    end_one = length_row[0]
    end_two = end_one + length_row[1]
    end_all = end_two + length_row[2]
    segments = (
        (slots >= end_one).astype(jnp.int32)
        + (slots >= end_two).astype(jnp.int32)
        + (slots >= end_all).astype(jnp.int32)
        + jnp.maximum(slots - end_all, 0)
    )
    valid_own = own_rows((slots < end_all).astype(f32))
    segments = to_relative(segments, share)

    def fetch(rows):
        sent = short(mm(choose, cut(rows, team, width, 1))).reshape(groups, per_peer, width)
        got = lax.all_to_all(sent, "dp", split_axis=0, concat_axis=0, tiled=True)
        return got.reshape(count, width)

    def give_back(rows):
        parts = len(rows)
        both = jnp.concatenate([r.reshape(share, teams, width) for r in rows], 2)
        columns = lax.all_to_all(
            both.reshape(share, teams * parts * width), "tensor", split_axis=1, concat_axis=0, tiled=True
        )
        got = lax.all_to_all(
            columns.reshape(groups, per_peer, parts * width), "dp", split_axis=0, concat_axis=0, tiled=True
        )
        pieces = spread_list(short(mm_tn(choose, got.reshape(count, parts * width))))
        return [
            to_given(jnp.concatenate([p[:, k * width : (k + 1) * width] for p in pieces], 1), width, 1)
            for k in range(parts)
        ]

    packed_x = to_relative(spread_columns(fetch(tokens)), share)
    grad_rows = lax.all_to_all(
        fetch(cotangent), "tensor", split_axis=0, concat_axis=1, tiled=True
    )

    wqkv_low = short(w_qkv)
    wout_low = short(w_out)
    wup_low = short(w_up)
    wdown_low = short(w_down)
    heads = width // HEAD
    score_scale = HEAD ** (-0.5)
    queries = short(mm(packed_x, wqkv_low[0]) + bias_qv[0]).reshape(count, heads, HEAD)
    keys = short(mm(packed_x, wqkv_low[1])).reshape(count, heads, HEAD)
    values = short(mm(packed_x, wqkv_low[2]) + bias_qv[1]).reshape(count, heads, HEAD)
    raw = jnp.einsum("qhd,khd->hqk", queries, keys, preferred_element_type=f32)
    same = segments[:, None] == segments[None, :]
    masked = jnp.where(same[None], raw * score_scale, masked_score)
    exponent = jnp.exp(masked - jnp.max(masked, axis=-1, keepdims=True))
    probs = exponent / jnp.sum(exponent, axis=-1, keepdims=True)
    probs_low = short(probs)
    context = short(
        jnp.einsum("hqk,khd->qhd", probs_low, values, preferred_element_type=f32)
    ).reshape(count, width)
    mid = wide(packed_x[:share]) + reduce_rows(mm(context, wout_low)) + vectors[0]
    normed_one, inverse_one, hidden = norm_forward(mid, vectors[1], vectors[2])
    hidden_low = spread_rows(short(hidden))
    pre_act = mm(hidden_low, wup_low) + bias_up
    phi = 0.5 * lax.erfc(-pre_act * math.sqrt(0.5))
    act_low = short(pre_act * phi)
    slope = phi + pre_act * jnp.exp(-0.5 * pre_act * pre_act) * (1.0 / math.sqrt(2.0 * math.pi))
    normed_two, inverse_two, result = norm_forward(
        hidden + reduce_rows(mm(act_low, wdown_low)) + vectors[3], vectors[4], vectors[5]
    )

    grad_result = wide(grad_rows) * valid_own[:, None]
    grad_z = norm_backward(grad_result, normed_two, inverse_two, vectors[4])
    grad_z_low = spread_rows(short(grad_z))
    grad_pre = short(mm_nt(grad_z_low, wdown_low) * slope)
    grad_hidden = grad_z + reduce_rows(mm_nt(grad_pre, wup_low))
    grad_down = short(mm_tn(act_low, grad_z_low))
    grad_up = short(mm_tn(hidden_low, grad_pre))
    grad_bias_up = jnp.sum(grad_pre, axis=0, dtype=f32)
    grad_mid = norm_backward(grad_hidden, normed_one, inverse_one, vectors[1])
    vector_part = jnp.stack(
        [
            jnp.sum(grad_mid, axis=0),
            jnp.sum(grad_hidden * normed_one, axis=0),
            jnp.sum(grad_hidden, axis=0),
            jnp.sum(grad_z, axis=0),
            jnp.sum(grad_result * normed_two, axis=0),
            jnp.sum(grad_result, axis=0),
        ]
    )
    extra = 16
    joined = jnp.concatenate(
        [short(grad_mid), short(vector_part), jnp.zeros((extra - 6, D), bf16)], 0
    )
    pieces = spread_list(joined)
    grad_mid_low = jnp.concatenate([p[:share] for p in pieces], 0)
    vector_part = sum(wide(p[share : share + 6]) for p in pieces)
    grad_out_t = short(mm_tn(grad_mid_low, context))
    grad_context = short(mm_nt(grad_mid_low, wout_low)).reshape(count, heads, HEAD)
    grad_probs = jnp.einsum("qhd,khd->hqk", grad_context, values, preferred_element_type=f32)
    weighted = jnp.sum(probs * grad_probs, axis=-1, keepdims=True)
    grad_scores = short(probs * (grad_probs - weighted))
    grad_values = short(
        jnp.einsum("hqk,qhd->khd", probs_low, grad_context, preferred_element_type=f32)
    ).reshape(count, width)
    grad_keys = short(
        jnp.einsum("hqk,qhd->khd", grad_scores, queries, preferred_element_type=f32) * score_scale
    ).reshape(count, width)
    grad_queries = short(
        jnp.einsum("hqk,khd->qhd", grad_scores, keys, preferred_element_type=f32) * score_scale
    ).reshape(count, width)
    grad_bias_pair = jnp.stack(
        [jnp.sum(grad_queries, axis=0, dtype=f32), jnp.sum(grad_values, axis=0, dtype=f32)]
    )
    grad_qkvo = jnp.concatenate(
        [
            short(mm_tn(packed_x, jnp.concatenate([grad_queries, grad_keys, grad_values], 1))),
            grad_out_t,
        ],
        1,
    )
    input_part = (
        mm_nt(grad_queries, wqkv_low[0])
        + mm_nt(grad_keys, wqkv_low[1])
        + mm_nt(grad_values, wqkv_low[2])
    )
    columns = D
    small = jnp.concatenate(
        [vector_part.reshape(-1), grad_bias_pair.reshape(-1), grad_bias_up.reshape(-1)]
    )
    parts = [
        grad_down.reshape(-1, columns),
        grad_up.reshape(-1, columns),
        grad_qkvo.reshape(-1, columns),
    ]
    rows_small = -(-small.size // (16 * columns)) * 16
    small = jnp.pad(short(small), (0, rows_small * columns - small.size)).reshape(rows_small, columns)
    total, small_sum = ring_sum(jnp.concatenate(parts, 0), small, inner, groups)
    sums, start = [], 0
    for part in parts:
        sums.append(total[start : start + part.shape[0]])
        start += part.shape[0]
    down_sum = sums[0].reshape(grad_down.shape)
    up_sum = sums[1].reshape(grad_up.shape)
    qkvo_sum = wide(sums[2].reshape(grad_qkvo.shape))
    small_sum = small_sum.reshape(-1)
    gradients = (
        jnp.stack([qkvo_sum[:, k * width : (k + 1) * width] for k in range(3)]),
        qkvo_sum[:, 3 * width :].T,
        wide(up_sum),
        wide(down_sum),
        small_sum[6 * D : 6 * D + 2 * width].reshape(2, width),
        small_sum[6 * D + 2 * width : 6 * D + 2 * width + bias_up.shape[0]],
        small_sum[: 6 * D].reshape(6, D),
    )
    moments_old = (mom_qkv, mom_out, mom_up, mom_down, mom_bias_qv, mom_bias_up, mom_vectors)
    moments = tuple(
        momentum_decay * old + grad for old, grad in zip(moments_old, gradients)
    )

    everyone = ("dp", "tensor")
    radices = (groups, wides, cores)

    def ring_within(digit, low, high):
        return Ring(everyone, radices, digit, lambda i: low <= i // teams < high)

    square_mine = lax.switch(
        jnp.minimum(group, 3),
        [
            lambda: short(moments[0][0]),
            lambda: short(moments[0][1]),
            lambda: short(moments[0][2]),
            lambda: short(moments[1]).T,
        ],
    )
    square = jnp.concatenate(
        spread_list(square_mine, ring_within(1, 0, 4), ring_within(2, 0, 4)), 1
    )

    up_low, down_low = short(moments[2]), short(moments[3])
    tile = D // 4
    pairs = [(i, j) for i in range(4) for j in range(i, 4)]

    def pack(gram):
        return jnp.concatenate(
            [gram[i * tile : (i + 1) * tile, j * tile : (j + 1) * tile] for i, j in pairs], 0
        )

    packed_gram = lax.switch(
        jnp.clip(group - 3, 0, 3),
        [
            lambda: jnp.zeros((len(pairs) * tile, tile), f32),
            lambda: pack(mm_nt(up_low, up_low)),
            lambda: pack(mm_tn(down_low, down_low)),
            lambda: jnp.zeros((len(pairs) * tile, tile), f32),
        ],
    )
    gram_x, gram_core = ring_within(1, 4, 6), ring_within(2, 4, 6)
    part_rows = len(pairs) * tile // cores
    held = cut(packed_gram, core_at, part_rows, 0)
    for hop in range(1, cores):
        held = held + gram_core.send(cut(packed_gram, (core_at + hop) % cores, part_rows, 0), hop)
    passing, total = held, held
    for _ in range(wides - 1):
        passing = gram_x.send(passing, 1)
        total = total + passing
    packed_gram = ring_gather(total, 0, gram_core, core_at)

    def no_work(square, blocks):
        return jnp.zeros((D, width), bf16)

    def square_work(square, blocks):
        return polar_columns(square, width)

    def gram_work(square, blocks):
        return factor_columns(blocks.reshape(len(pairs), tile, tile), D, width)

    stepped = lax.switch(
        (group >= 4).astype(jnp.int32) + (group >= 6).astype(jnp.int32),
        [square_work, gram_work, no_work],
        square,
        packed_gram,
    )
    dp_rows = D // groups
    steps = lax.all_to_all(
        stepped.reshape(groups, dp_rows, width), "dp", split_axis=0, concat_axis=0, tiled=True
    )
    factors = spread_columns(steps[4:6].reshape(2 * dp_rows, width))

    def mine(values_, dim):
        return lax.dynamic_slice_in_dim(values_, group * dp_rows, dp_rows, dim)

    short_rate = rate_matrix * 0.2 * math.sqrt(D)
    long_rate = rate_matrix * 0.2 * math.sqrt(w_up.shape[1] * teams)
    masters = [
        mine(w_qkv, 1) - short_rate * wide(steps[:3]),
        mine(w_out, 1) - short_rate * wide(steps[3]).T,
        mine(w_up, 0) - long_rate * mm(factors[:dp_rows], up_low),
        mine(w_down, 1) - long_rate * mm_nt(down_low, factors[dp_rows:]),
    ]
    rate_vector = 0.2 / math.sqrt(all_tokens)
    for param, moment in zip((bias_qv, bias_up, vectors), moments[4:]):
        masters.append(param - rate_vector * moment)

    output, grad_tokens = give_back(
        [short(result), short(grad_mid + reduce_rows(input_part))]
    )
    grad_tokens = wide(grad_tokens)
    return (output, grad_tokens, *gradients, *moments, *masters)


def axis_layout(mesh):
    grid = mesh.devices
    groups, teams = grid.shape
    places = [getattr(d, "coords", None) for d in grid[:, 0]]
    inner = 2 if groups % 2 == 0 else 1
    if places[0] is not None:
        moved = [k for k in range(3) if places[0][k] != places[1][k]]
        fixed = [k for k in range(3) if k not in moved]
        inner = 1
        while inner < groups and all(places[inner][k] == places[0][k] for k in fixed):
            inner += 1
        if groups % inner:
            inner = 1
    return inner, (2 if teams % 2 == 0 else 1)


def solution(mesh):
    grads = (
        P(None, None, "tensor"),
        P("tensor", None),
        P(None, "tensor"),
        P("tensor", None),
        P(None, "tensor"),
        P("tensor"),
        P(),
    )
    rows = P("dp", None)
    return jax.shard_map(
        functools.partial(body, axis_layout(mesh)),
        mesh=mesh,
        in_specs=(rows, rows, rows, P(), *grads, *grads),
        out_specs=(
            rows,
            rows,
            *grads,
            *grads,
            P(None, "dp", "tensor"),
            P("tensor", "dp"),
            P("dp", "tensor"),
            P("tensor", "dp"),
            P(None, "tensor"),
            P("tensor"),
            P(),
        ),
        check_vma=False,
    )
```

time: 1220 us -> 542 us (0.44)
  waiting for transfers between devices: 560 us -> 77.1 us
  matrix products: 320 us -> 64.2 us
  Pallas kernels: 0 us -> 165 us
  blocking collectives: 141 us -> 0 us
  starting transfers between devices: 17.1 us -> 115 us
  loops' own time: 24.9 us -> 3.05 us
  other arithmetic: 79.1 us -> 60.6 us
  local copies, waits for them, and re-layouts: 59.7 us -> 43.6 us
    psum x4 -> x0, waiting for transfers between devices: 400 us -> none  [the longest x1 210 us: body(): lax.psum(grad_qkv_w.astype(jnp.bfloat16), 'dp').astype(jnp.float32)]
    dot_general x37 -> x27, matrix products: 320 us -> 59.5 us  [the longest x10 22.9 us: mm(): return jnp.dot(short(left), short(right), preferred_element_type=f32)]
    pallas_call x0 -> x2, Pallas kernels: none -> 165 us  [the longest x1 129 us: ring_sum(): pl.pallas_call(functools.partial(ring_sum_kernel, inner, halves), name='r...]
    all_to_all x1 -> x0, blocking collectives: 81.3 us -> none  [body(): lax.all_to_all(back_y, 'dp', split_axis=0, concat_axis=0, tiled=True)]
    reduce_scatter x3 -> x0, waiting for transfers between devices: 66.1 us -> none  [reduce_rows(): lax.psum_scatter(term_of(jnp.int32(0), share_rows * lax.axis_size('tensor...]
    psum x2 -> x0, blocking collectives: 59.6 us -> none  [the longest x1 49.3 us: body(): lax.psum(grad_bias_pair.astype(jnp.bfloat16), 'dp').astype(jnp.float32)]
    ppermute x0 -> x32, waiting for transfers between devices: none -> 52.1 us  [send(): return lax.ppermute(value, self.axes, pairs)]
    all_to_all x3 -> x6, starting transfers between devices: 15.9 us -> 66.1 us  [the longest x1 30.8 us: body(): lax.all_to_all(stepped.reshape(groups, dp_rows, width), 'dp', split_axis=...]
  transfers between devices with their start and end apart: 14 -> 38, of which waited for: 10 -> 19; matrix products, arithmetic and copies ran while one was open for 27% -> 19% of each run, Pallas kernels for 0% -> 31%
where the time goes in v1:
time: 542 us; the launch traced here: 534 us
  Pallas kernels  165 us (30%)
  starting transfers between devices  115 us (21%)
  waiting for transfers between devices  77.1 us (14%)
  matrix products  64.2 us (12%)
  other arithmetic  60.6 us (11%)
  local copies, waits for them, and re-layouts  43.6 us (8%)
    pallas_call x1, Pallas kernels, ring_sum(): pl.pallas_call(functools.partial(ring_sum_kernel, inner, halves), name='r...  129 us
    ppermute x32, waiting for transfers between devices, send(): return lax.ppermute(value, self.axes, pairs)  52.1 us
    ppermute x32, starting transfers between devices, send(): return lax.ppermute(value, self.axes, pairs)  49.3 us
    pallas_call x1, Pallas kernels, polar_columns(): pl.pallas_call(functools.partial(polar_kernel, 512), name='polar', out_sh...  36.4 us
    all_to_all x1, starting transfers between devices, body(): lax.all_to_all(stepped.reshape(groups, dp_rows, width), 'dp', split_axis=...  30.8 us
    dot_general x10, matrix products, mm(): return jnp.dot(short(left), short(right), preferred_element_type=f32)  22.9 us
    unnamed x154, local copies, waits for them, and re-layouts  19.6 us
    concatenate x1, other arithmetic, body(): total, small_sum = ring_sum(jnp.concatenate(parts, 0), small, inner, groups)  19.4 us
  transfers between devices with their start and end apart: 38, of which 19 were waited for; matrix products, arithmetic and copies ran while one was open for 19% of the time, Pallas kernels for 31%

profile of v1, /device:TPU:1, one launch (start us, length us, event | category | flops | bytes accessed | tf_op | source)
XLA Modules:
  0.0 533.9 jit_solution(15444910511018946861)
XLA Ops:
  8.4 6.4 %all-to-all-start = ((bf16[8,72,256]{2,1,0:T(8,128)(2,1)}), bf16[8,72,256]{2,1,0:T(8,128)(2,1)S(1)}, u32[]{:S(2)}, u32[]{:S(2)}) async-start(bf16[8,72,256]{2,1,0:T(8,128)(2,1)} %bitcast.5), calls=%async_computation | async-start | bytes 589824 | tf_op jit(solution)/shard_map/all_to_all | solution.py:559
  14.8 2.1 convert_element_type.251
  17.0 5.7 %all-to-all-done = bf16[8,72,256]{2,1,0:T(8,128)(2,1)S(1)} async-done(((bf16[8,72,256]{2,1,0:T(8,128)(2,1)}), bf16[8,72,256]{2,1,0:T(8,128)(2,1)S(1)}, u32[]{:S(2)}, u32[]{:S(2)}) %all-to-all-start) | async-done | bytes 294944 | tf_op jit(solution)/shard_map/all_to_all | solution.py:559
  23.9 3.1 collective-permute-start.1
  28.2 3.9 collective-permute-start.2
  39.8 4.7 fusion.124
  44.5 3.5 fusion.35
  52.3 7.0 %collective-permute-done.4 = bf16[144,1024]{1,0:T(8,128)(2,1)S(1)} collective-permute-done((bf16[144,1024]{1,0:T(8,128)(2,1)S(1)}, bf16[144,1024]{1,0:T(8,128)(2,1)S(1)}, u32[]{:S(2)}, u32[]{:S(2)}) %collective-permute-start.4) | collective-permute-done | bytes 294944 | tf_op jit(solution)/shard_map/ppermute | solution.py:81
  62.7 4.6 collective-permute-done.5
  67.3 2.1 collective-permute-start.7
  69.4 2.1 fusion.44
  71.5 5.2 all-to-all-start.1
  76.8 10.9 %multiply_convert_fusion.1 = (bf16[576,1024]{1,0:T(8,128)(2,1)S(1)}, f32[576,1024]{1,0:T(8,128)}, f32[576,1024]{1,0:T(8,128)}) fusion(f32[1024]{0:T(1024)S(1)} %copy-done.56, f32[1024,1024]{1,0:T(8,128)} %param.35, bf16[144,1024]{1,0:T(8,128)(2,1)} %collective-permute-done.7, bf16[144,1024]{1,0:T(8,128)(2,1)S(1)} %collective-permute-done.6, ...), kind=kOutput, calls=%fused_computation.54 | convolution fusion | flops 1252655104 | bytes 11276288 | tf_op jit(solution)/shard_map/dot_general | solution.py:34
  91.8 3.6 all-to-all-start.2
  95.5 5.4 %all-to-all-done.2 = bf16[4,144,256]{2,1,0:T(8,128)(2,1)S(1)} async-done(((bf16[4,144,256]{2,1,0:T(8,128)(2,1)}), bf16[4,144,256]{2,1,0:T(8,128)(2,1)S(1)}, u32[]{:S(2)}, u32[]{:S(2)}) %all-to-all-start.2) | async-done | bytes 294944 | tf_op jit(solution)/shard_map/all_to_all | solution.py:578
  103.4 7.0 %collective-permute-done.9 = bf16[144,1024]{1,0:T(8,128)(2,1)S(1)} collective-permute-done((bf16[144,1024]{1,0:T(8,128)(2,1)S(1)}, bf16[144,1024]{1,0:T(8,128)(2,1)S(1)}, u32[]{:S(2)}, u32[]{:S(2)}) %collective-permute-start.9) | collective-permute-done | bytes 294944 | tf_op jit(solution)/shard_map/ppermute | solution.py:81
  114.2 4.3 collective-permute-done.10
  118.6 2.7 collective-permute-start.12
  131.0 2.5 copy.91
  134.3 4.6 collective-permute-done.14
  142.1 4.7 convolution_convert_fusion.1
  149.6 2.1 collective-permute-start.17
  151.7 4.1 convolution_convert_fusion
  161.8 4.5 bitcast_reduce_fusion
  166.3 3.8 multiply_reduce_fusion
  182.2 19.4 %maximum_maximum_fusion.x_ref = bf16[3072,1024]{1,0:T(8,128)(2,1)S(1)} fusion(bf16[1024,256]{1,0:T(8,128)(2,1)S(1)} %copy-done.29, bf16[1024,768]{1,0:T(8,128)(2,1)S(1)} %convolution_convert_fusion.2, bf16[1024,1024]{1,0:T(8,128)(2,1)S(1)} %copy-done.15, bf16[1024,1024]{1,0:T(8,128)(2,1)S(1)} %copy-done.14), kind=kLoop, calls=%fused_computation.27 | loop fusion | flops 25165824 | bytes 12582912 | tf_op jit(solution)/shard_map/concatenate | solution.py:677
  201.7 129.0 %ring_sum.1 = (bf16[3072,1024]{1,0:T(8,128)(2,1)S(1)}, f32[16,1024]{1,0:T(8,128)S(1)}) custom-call(bf16[3072,1024]{1,0:T(8,128)(2,1)S(1)} %maximum_maximum_fusion.x_ref, bf16[16,1024]{1,0:T(8,128)(2,1)S(1)} %reshape.284.small_ref), custom_call_target="tpu_custom_call" | custom-call | flops 3145728 | bytes 12582912 | tf_op jit(solution)/shard_map/ring_sum/pallas_call | solution.py:236
  330.7 7.9 %fusion.106 = (bf16[1024,1024]{1,0:T(8,128)(2,1)S(1)}, f32[1024,1024]{1,0:T(8,128)}, f32[1024,1024]{1,0:T(8,128)}, bf16[1024,1024]{1,0:T(8,128)(2,1)}, f32[1024,1024]{1,0:T(8,128)}, /*index=5*/f32[1024,1024]{1,0:T(8,128)}) fusion(f32[1024,1024]{1,0:T(8,128)S(1)} %copy-done.10, bf16[3072,1024]{1,0:T(8,128)(2,1)S(1)} %get-tuple-element.164, ...), kind=kLoop, calls=%fused_computation.280 | loop fusion | flops 8388608 | bytes 33554432 | tf_op jit(solution)/shard_map/convert_element_type | solution.py:26
  342.2 2.5 constant_dynamic-slice_fusion.5
  351.4 6.9 %collective-permute-done.19 = bf16[144,1024]{1,0:T(8,128)(2,1)S(1)} collective-permute-done((bf16[144,1024]{1,0:T(8,128)(2,1)S(1)}, bf16[144,1024]{1,0:T(8,128)(2,1)S(1)}, u32[]{:S(2)}, u32[]{:S(2)}) %collective-permute-start.19) | collective-permute-done | bytes 294944 | tf_op jit(solution)/shard_map/ppermute | solution.py:81
  359.3 5.8 %all-to-all-start.3 = ((bf16[144,4,512]{2,0,1:T(8,128)(2,1)}), bf16[144,4,512]{2,0,1:T(8,128)(2,1)}, u32[]{:S(2)}, u32[]{:S(2)}) async-start(bf16[144,4,512]{2,0,1:T(8,128)(2,1)} %pad_maximum_fusion.11), calls=%async_computation.3 | async-start | bytes 1179648 | tf_op jit(solution)/shard_map/all_to_all | solution.py:565
  368.7 5.1 all-to-all-done.3
  373.9 14.4 %all-to-all-start.4 = ((bf16[8,72,512]{2,1,0:T(8,128)(2,1)}), bf16[8,72,512]{2,1,0:T(8,128)(2,1)}, u32[]{:S(2)}, u32[]{:S(2)}) async-start(bf16[8,72,512]{2,1,0:T(8,128)(2,1)} %bitcast.38), calls=%async_computation.4 | async-start | bytes 1179648 | tf_op jit(solution)/shard_map/all_to_all | solution.py:568
  388.3 2.7 slice_bitcast_fusion
  391.4 2.1 multiply_add_fusion.2
  396.1 2.2 collective-permute-start.23
  401.6 3.3 collective-permute-start.24
  410.1 4.4 collective-permute-start.25
  416.9 2.5 add.504
  424.2 7.4 %collective-permute-done.20 = bf16[576,512]{1,0:T(8,128)(2,1)} collective-permute-done((bf16[576,512]{1,0:T(8,128)(2,1)S(1)}, bf16[576,512]{1,0:T(8,128)(2,1)}, u32[]{:S(2)}, u32[]{:S(2)}) %collective-permute-start.20) | collective-permute-done | bytes 589856 | tf_op jit(solution)/shard_map/ppermute | solution.py:81
  435.1 39.3 %conditional.5 = (bf16[1024,256]{1,0:T(8,128)(2,1)}) conditional(s32[]{:T(128)} %clamp.9, bf16[1024,1024]{1,0:T(8,128)(2,1)S(1)} %pad_maximum_fusion.1, (f32[1280,256]{1,0:T(8,128)}, s32[]{:T(128)}, s32[]{:T(128)}, s32[]{:T(128)}, f32[1280,256]{1,0:T(8,128)}, /*index=5*/s32[]{:T(128)}) %tuple.52, () %tuple.53), branch_computations={%region_29.30_spmd, %region_30.31_spmd, %region_31.32_spmd} | conditional | flops 16 | bytes 7864507 | solution.py:757
  435.3 36.4 %polar.1 = bf16[1024,256]{1,0:T(8,128)(2,1)} custom-call(bf16[1024,1024]{1,0:T(8,128)(2,1)S(1)} %m_ref), custom_call_target="tpu_custom_call" | custom-call | tf_op jit(solution)/shard_map/cond/branch_0_fun/polar/pallas_call | solution.py:319
  474.4 30.8 %all-to-all-start.5 = ((bf16[8,128,256]{2,1,0:T(8,128)(2,1)}), bf16[8,128,256]{2,1,0:T(8,128)(2,1)S(1)}, u32[]{:S(2)}, u32[]{:S(2)}) async-start(bf16[8,128,256]{2,1,0:T(8,128)(2,1)} %bitcast.48), calls=%async_computation.5 | async-start | bytes 1048576 | tf_op jit(solution)/shard_map/all_to_all | solution.py:764
  509.9 8.8 %all-to-all-done.5 = bf16[8,128,256]{2,1,0:T(8,128)(2,1)S(1)} async-done(((bf16[8,128,256]{2,1,0:T(8,128)(2,1)}), bf16[8,128,256]{2,1,0:T(8,128)(2,1)S(1)}, u32[]{:S(2)}, u32[]{:S(2)}) %all-to-all-start.5) | async-done | bytes 524320 | tf_op jit(solution)/shard_map/all_to_all | solution.py:764
  518.9 2.3 collective-permute-start.30
  522.6 3.2 collective-permute-start.31
  527.8 2.7 fusion.31
  530.4 2.9 fusion.32
  (339 shorter events, 115.5 us)
Async XLA Ops:
  8.4 14.2 %all-to-all-start = ((bf16[8,72,256]{2,1,0:T(8,128)(2,1)}), bf16[8,72,256]{2,1,0:T(8,128)(2,1)S(1)}, u32[]{:S(2)}, u32[]{:S(2)}) async-start(bf16[8,72,256]{2,1,0:T(8,128)(2,1)} %bitcast.5), calls=%async_computation | async-start | bytes 589824 | tf_op jit(solution)/shard_map/all_to_all | solution.py:559
  22.6 5.6 %collective-permute-start = (bf16[576,256]{1,0:T(8,128)(2,1)S(1)}, bf16[576,256]{1,0:T(8,128)(2,1)S(1)}, u32[]{:S(2)}, u32[]{:S(2)}) collective-permute-start(bf16[576,256]{1,0:T(8,128)(2,1)S(1)} %bitcast.146), channel_id=1, source_target_pairs={{0,2},{1,3},{2,0},{3,1},{4,6},{5,7},{6,4},{7,5},{8,10},{9,11},{10,... | collective-permute-start | bytes 884744 | tf_op jit(solution)/shard_map/ppermute | solution.py:81
  23.9 8.6 %collective-permute-start.1 = (bf16[576,256]{1,0:T(8,128)(2,1)S(1)}, bf16[576,256]{1,0:T(8,128)(2,1)S(1)}, u32[]{:S(2)}, u32[]{:S(2)}) collective-permute-start(bf16[576,256]{1,0:T(8,128)(2,1)S(1)} %bitcast.147), channel_id=1, source_target_pairs={{0,1},{1,0},{2,3},{3,2},{4,5},{5,4},{6,7},{7,6},{8,9},{9,8},{10,11... | collective-permute-start | bytes 884744 | tf_op jit(solution)/shard_map/ppermute | solution.py:81
  28.2 5.1 collective-permute-start.2
  33.9 25.3 %copy-start.27 = (bf16[144,1024]{1,0:T(8,128)(2,1)}, bf16[144,1024]{1,0:T(8,128)(2,1)S(1)}, u32[]{:S(2)}) copy-start(bf16[144,1024]{1,0:T(8,128)(2,1)S(1)} %get-tuple-element.292) | copy-start | bytes 884740
  48.7 2.0 collective-permute-start.3
  51.0 8.3 %collective-permute-start.4 = (bf16[144,1024]{1,0:T(8,128)(2,1)S(1)}, bf16[144,1024]{1,0:T(8,128)(2,1)S(1)}, u32[]{:S(2)}, u32[]{:S(2)}) collective-permute-start(bf16[144,1024]{1,0:T(8,128)(2,1)S(1)} %slice.496), channel_id=1, source_target_pairs={{0,2},{1,3},{2,0},{3,1},{4,6},{5,7},{6,4},{7,5},{8,10},{9,11},{10,... | collective-permute-start | bytes 884744 | tf_op jit(solution)/shard_map/ppermute | solution.py:81
  59.9 27.7 %copy-start.35 = (bf16[144,1024]{1,0:T(8,128)(2,1)}, bf16[144,1024]{1,0:T(8,128)(2,1)S(1)}, u32[]{:S(2)}) copy-start(bf16[144,1024]{1,0:T(8,128)(2,1)S(1)} %fusion.75) | copy-start | bytes 884740
  59.9 7.4 %collective-permute-start.5 = (bf16[144,1024]{1,0:T(8,128)(2,1)S(1)}, bf16[144,1024]{1,0:T(8,128)(2,1)S(1)}, u32[]{:S(2)}, u32[]{:S(2)}) collective-permute-start(bf16[144,1024]{1,0:T(8,128)(2,1)S(1)} %fusion.75), channel_id=1, source_target_pairs={{0,2},{1,3},{2,0},{3,1},{4,6},{5,7},{6,4},{7,5},{8,10},{9,11},{10,... | collective-permute-start | bytes 884744 | tf_op jit(solution)/shard_map/ppermute | solution.py:81
  61.2 15.6 %collective-permute-start.6 = (bf16[144,1024]{1,0:T(8,128)(2,1)S(1)}, bf16[144,1024]{1,0:T(8,128)(2,1)S(1)}, u32[]{:S(2)}, u32[]{:S(2)}) collective-permute-start(bf16[144,1024]{1,0:T(8,128)(2,1)S(1)} %fusion.75), channel_id=1, source_target_pairs={{0,1},{1,0},{2,3},{3,2},{4,5},{5,4},{6,7},{7,6},{8,9},{9,8},{10,11... | collective-permute-start | bytes 884744 | tf_op jit(solution)/shard_map/ppermute | solution.py:81
  67.3 20.4 %copy-start.59 = (bf16[144,1024]{1,0:T(8,128)(2,1)}, bf16[144,1024]{1,0:T(8,128)(2,1)S(1)}, u32[]{:S(2)}) copy-start(bf16[144,1024]{1,0:T(8,128)(2,1)S(1)} %collective-permute-done.5) | copy-start | bytes 884740
  67.3 9.5 %collective-permute-start.7 = (bf16[144,1024]{1,0:T(8,128)(2,1)S(1)}, bf16[144,1024]{1,0:T(8,128)(2,1)}, u32[]{:S(2)}, u32[]{:S(2)}) collective-permute-start(bf16[144,1024]{1,0:T(8,128)(2,1)S(1)} %collective-permute-done.5), channel_id=1, source_target_pairs={{0,1},{1,0},{2,3},{3,2},{4,5},{5,4},{6,7},{7,6},{8,9},{9,8},{10,11... | collective-permute-start | bytes 884744 | tf_op jit(solution)/shard_map/ppermute | solution.py:81
  71.5 20.2 %all-to-all-start.1 = ((bf16[8,72,256]{2,1,0:T(8,128)(2,1)}), bf16[8,72,256]{2,1,0:T(8,128)(2,1)}, u32[]{:S(2)}, u32[]{:S(2)}) async-start(bf16[8,72,256]{2,1,0:T(8,128)(2,1)} %bitcast.26), calls=%async_computation.1 | async-start | bytes 589824 | tf_op jit(solution)/shard_map/all_to_all | solution.py:559
  91.4 9.6 %collective-permute-start.8 = (bf16[288,1024]{1,0:T(8,128)(2,1)}, bf16[288,1024]{1,0:T(8,128)(2,1)}, u32[]{:S(2)}, u32[]{:S(2)}) collective-permute-start(bf16[288,1024]{1,0:T(8,128)(2,1)} %slice.491), channel_id=1, source_target_pairs={{0,1},{1,0},{2,3},{3,2},{4,5},{5,4},{6,7},{7,6},{8,9},{9,8},{10,11... | collective-permute-start | bytes 1769480 | tf_op jit(solution)/shard_map/ppermute | solution.py:81
  91.8 9.1 %all-to-all-start.2 = ((bf16[4,144,256]{2,1,0:T(8,128)(2,1)}), bf16[4,144,256]{2,1,0:T(8,128)(2,1)S(1)}, u32[]{:S(2)}, u32[]{:S(2)}) async-start(bf16[4,144,256]{2,1,0:T(8,128)(2,1)} %bitcast.27), calls=%async_computation.2 | async-start | bytes 589824 | tf_op jit(solution)/shard_map/all_to_all | solution.py:578
  101.0 21.5 %copy-start.67 = (f32[576,1024]{1,0:T(8,128)S(1)}, f32[576,1024]{1,0:T(8,128)}, u32[]{:S(2)}) copy-start(f32[576,1024]{1,0:T(8,128)} %get-tuple-element.335) | copy-start | bytes 7077892
  102.7 7.7 %collective-permute-start.9 = (bf16[144,1024]{1,0:T(8,128)(2,1)S(1)}, bf16[144,1024]{1,0:T(8,128)(2,1)S(1)}, u32[]{:S(2)}, u32[]{:S(2)}) collective-permute-start(bf16[144,1024]{1,0:T(8,128)(2,1)S(1)} %slice.495), channel_id=1, source_target_pairs={{0,2},{1,3},{2,0},{3,1},{4,6},{5,7},{6,4},{7,5},{8,10},{9,11},{10,... | collective-permute-start | bytes 884744 | tf_op jit(solution)/shard_map/ppermute | solution.py:81
  111.8 6.8 %collective-permute-start.10 = (bf16[144,1024]{1,0:T(8,128)(2,1)S(1)}, bf16[144,1024]{1,0:T(8,128)(2,1)S(1)}, u32[]{:S(2)}, u32[]{:S(2)}) collective-permute-start(bf16[144,1024]{1,0:T(8,128)(2,1)S(1)} %convert_element_type.278), channel_id=1, source_target_pairs={{0,2},{1,3},{2,0},{3,1},{4,6},{5,7},{6,4},{7,5},{8,10},{9,11},{10,... | collective-permute-start | bytes 884744 | tf_op jit(solution)/shard_map/ppermute | solution.py:81
  112.5 8.8 %collective-permute-start.11 = (bf16[144,1024]{1,0:T(8,128)(2,1)S(1)}, bf16[144,1024]{1,0:T(8,128)(2,1)S(1)}, u32[]{:S(2)}, u32[]{:S(2)}) collective-permute-start(bf16[144,1024]{1,0:T(8,128)(2,1)S(1)} %convert_element_type.278), channel_id=1, source_target_pairs={{0,1},{1,0},{2,3},{3,2},{4,5},{5,4},{6,7},{7,6},{8,9},{9,8},{10,11... | collective-permute-start | bytes 884744 | tf_op jit(solution)/shard_map/ppermute | solution.py:81
  118.6 3.9 collective-permute-start.12
  126.3 2.1 collective-permute-start.13
  130.3 8.5 %collective-permute-start.14 = (bf16[144,1024]{1,0:T(8,128)(2,1)}, bf16[144,1024]{1,0:T(8,128)(2,1)}, u32[]{:S(2)}, u32[]{:S(2)}) collective-permute-start(bf16[144,1024]{1,0:T(8,128)(2,1)} %slice.494), channel_id=1, source_target_pairs={{0,2},{1,3},{2,0},{3,1},{4,6},{5,7},{6,4},{7,5},{8,10},{9,11},{10,... | collective-permute-start | bytes 884744 | tf_op jit(solution)/shard_map/ppermute | solution.py:81
  140.8 18.3 %copy-start.24 = (bf16[144,1024]{1,0:T(8,128)(2,1)}, bf16[144,1024]{1,0:T(8,128)(2,1)S(1)}, u32[]{:S(2)}) copy-start(bf16[144,1024]{1,0:T(8,128)(2,1)S(1)} %convert_element_type.282) | copy-start | bytes 884740
  141.4 8.2 %collective-permute-start.15 = (bf16[160,1024]{1,0:T(8,128)(2,1)S(1)}, bf16[160,1024]{1,0:T(8,128)(2,1)}, u32[]{:S(2)}, u32[]{:S(2)}) collective-permute-start(bf16[160,1024]{1,0:T(8,128)(2,1)S(1)} %concatenate.87), channel_id=1, source_target_pairs={{0,2},{1,3},{2,0},{3,1},{4,6},{5,7},{6,4},{7,5},{8,10},{9,11},{10,... | collective-permute-start | bytes 983048 | tf_op jit(solution)/shard_map/ppermute | solution.py:81
  146.8 10.0 %collective-permute-start.16 = (bf16[160,1024]{1,0:T(8,128)(2,1)S(1)}, bf16[160,1024]{1,0:T(8,128)(2,1)}, u32[]{:S(2)}, u32[]{:S(2)}) collective-permute-start(bf16[160,1024]{1,0:T(8,128)(2,1)S(1)} %concatenate.87), channel_id=1, source_target_pairs={{0,1},{1,0},{2,3},{3,2},{4,5},{5,4},{6,7},{7,6},{8,9},{9,8},{10,11... | collective-permute-start | bytes 983048 | tf_op jit(solution)/shard_map/ppermute | solution.py:81
  149.6 8.4 %collective-permute-start.17 = (bf16[160,1024]{1,0:T(8,128)(2,1)}, bf16[160,1024]{1,0:T(8,128)(2,1)}, u32[]{:S(2)}, u32[]{:S(2)}) collective-permute-start(bf16[160,1024]{1,0:T(8,128)(2,1)} %collective-permute-done.15), channel_id=1, source_target_pairs={{0,1},{1,0},{2,3},{3,2},{4,5},{5,4},{6,7},{7,6},{8,9},{9,8},{10,11... | collective-permute-start | bytes 983048 | tf_op jit(solution)/shard_map/ppermute | solution.py:81
  181.1 167.5 %collective-permute-start.18 = (bf16[288,1024]{1,0:T(8,128)(2,1)S(1)}, bf16[288,1024]{1,0:T(8,128)(2,1)}, u32[]{:S(2)}, u32[]{:S(2)}) collective-permute-start(bf16[288,1024]{1,0:T(8,128)(2,1)S(1)} %slice.489), channel_id=1, source_target_pairs={{0,1},{1,0},{2,3},{3,2},{4,5},{5,4},{6,7},{7,6},{8,9},{9,8},{10,11... | collective-permute-start | bytes 1769480 | tf_op jit(solution)/shard_map/ppermute | solution.py:81
  182.2 148.5 %copy-start.11 = (f32[1024,1024]{1,0:T(8,128)S(1)}, f32[1024,1024]{1,0:T(8,128)}, u32[]{:S(2)}) copy-start(f32[1024,1024]{1,0:T(8,128)} %param.42) | copy-start | bytes 12582916
  201.7 129.0 %copy-start.10 = (f32[1024,1024]{1,0:T(8,128)S(1)}, f32[1024,1024]{1,0:T(8,128)}, u32[]{:S(2)}) copy-start(f32[1024,1024]{1,0:T(8,128)} %param.43) | copy-start | bytes 12582916
  344.6 20.5 %collective-permute-start.26 = (f32[1280,256]{1,0:T(8,128)}, f32[1280,256]{1,0:T(8,128)}, u32[]{:S(2)}, u32[]{:S(2)}) collective-permute-start(f32[1280,256]{1,0:T(8,128)} %constant_dynamic-slice_fusion.5), channel_id=1, source_target_pairs={{16,17},{17,16},{18,19},{19,18},{20,21},{21,20},{22,23},{23,22}} | collective-permute-start | bytes 3932168 | tf_op jit(solution)/shard_map/ppermute | solution.py:81
  350.5 7.8 %collective-permute-start.19 = (bf16[144,1024]{1,0:T(8,128)(2,1)S(1)}, bf16[144,1024]{1,0:T(8,128)(2,1)S(1)}, u32[]{:S(2)}, u32[]{:S(2)}) collective-permute-start(bf16[144,1024]{1,0:T(8,128)(2,1)S(1)} %slice.493), channel_id=1, source_target_pairs={{0,2},{1,3},{2,0},{3,1},{4,6},{5,7},{6,4},{7,5},{8,10},{9,11},{10,... | collective-permute-start | bytes 884744 | tf_op jit(solution)/shard_map/ppermute | solution.py:81
  359.3 14.6 %all-to-all-start.3 = ((bf16[144,4,512]{2,0,1:T(8,128)(2,1)}), bf16[144,4,512]{2,0,1:T(8,128)(2,1)}, u32[]{:S(2)}, u32[]{:S(2)}) async-start(bf16[144,4,512]{2,0,1:T(8,128)(2,1)} %pad_maximum_fusion.11), calls=%async_computation.3 | async-start | bytes 1179648 | tf_op jit(solution)/shard_map/all_to_all | solution.py:565
  367.0 49.9 %collective-permute-start.27 = (f32[1280,256]{1,0:T(8,128)S(1)}, f32[1280,256]{1,0:T(8,128)}, u32[]{:S(2)}, u32[]{:S(2)}) collective-permute-start(f32[1280,256]{1,0:T(8,128)S(1)} %dynamic-slice_add_fusion), channel_id=1, source_target_pairs={{16,18},{17,19},{18,16},{19,17},{20,22},{21,23},{22,20},{23,21}} | collective-permute-start | bytes 3932168 | tf_op jit(solution)/shard_map/ppermute | solution.py:81
  373.9 40.7 %all-to-all-start.4 = ((bf16[8,72,512]{2,1,0:T(8,128)(2,1)}), bf16[8,72,512]{2,1,0:T(8,128)(2,1)}, u32[]{:S(2)}, u32[]{:S(2)}) async-start(bf16[8,72,512]{2,1,0:T(8,128)(2,1)} %bitcast.38), calls=%async_computation.4 | async-start | bytes 1179648 | tf_op jit(solution)/shard_map/all_to_all | solution.py:568
  396.1 14.0 %collective-permute-start.23 = (bf16[1024,256]{1,0:T(8,128)(2,1)}, bf16[1024,256]{1,0:T(8,128)(2,1)}, u32[]{:S(2)}, u32[]{:S(2)}) collective-permute-start(bf16[1024,256]{1,0:T(8,128)(2,1)} %get-tuple-element.348), channel_id=1, source_target_pairs={{0,2},{1,3},{2,0},{3,1},{4,6},{5,7},{6,4},{7,5},{8,10},{9,11},{10,... | collective-permute-start | bytes 1572872 | tf_op jit(solution)/shard_map/ppermute | solution.py:81
  401.6 21.1 %collective-permute-start.24 = (bf16[1024,256]{1,0:T(8,128)(2,1)}, bf16[1024,256]{1,0:T(8,128)(2,1)}, u32[]{:S(2)}, u32[]{:S(2)}) collective-permute-start(bf16[1024,256]{1,0:T(8,128)(2,1)} %get-tuple-element.348), channel_id=1, source_target_pairs={{0,1},{1,0},{2,3},{3,2},{4,5},{5,4},{6,7},{7,6},{8,9},{9,8},{10,11... | collective-permute-start | bytes 1572872 | tf_op jit(solution)/shard_map/ppermute | solution.py:81
  410.1 12.6 %collective-permute-start.25 = (bf16[1024,256]{1,0:T(8,128)(2,1)}, bf16[1024,256]{1,0:T(8,128)(2,1)S(1)}, u32[]{:S(2)}, u32[]{:S(2)}) collective-permute-start(bf16[1024,256]{1,0:T(8,128)(2,1)} %collective-permute-done.23), channel_id=1, source_target_pairs={{0,1},{1,0},{2,3},{3,2},{4,5},{5,4},{6,7},{7,6},{8,9},{9,8},{10,11... | collective-permute-start | bytes 1572872 | tf_op jit(solution)/shard_map/ppermute | solution.py:81
  416.5 15.1 %collective-permute-start.20 = (bf16[576,512]{1,0:T(8,128)(2,1)S(1)}, bf16[576,512]{1,0:T(8,128)(2,1)}, u32[]{:S(2)}, u32[]{:S(2)}) collective-permute-start(bf16[576,512]{1,0:T(8,128)(2,1)S(1)} %fusion.30), channel_id=1, source_target_pairs={{0,2},{1,3},{2,0},{3,1},{4,6},{5,7},{6,4},{7,5},{8,10},{9,11},{10,... | collective-permute-start | bytes 1769480 | tf_op jit(solution)/shard_map/ppermute | solution.py:81
  419.5 15.7 %collective-permute-start.28 = (f32[1280,256]{1,0:T(8,128)}, f32[1280,256]{1,0:T(8,128)}, u32[]{:S(2)}, u32[]{:S(2)}) collective-permute-start(f32[1280,256]{1,0:T(8,128)} %add.504), channel_id=1, source_target_pairs={{16,17},{17,16},{18,19},{19,18},{20,21},{21,20},{22,23},{23,22}} | collective-permute-start | bytes 3932168 | tf_op jit(solution)/shard_map/ppermute | solution.py:81
  422.4 11.9 %collective-permute-start.21 = (bf16[576,512]{1,0:T(8,128)(2,1)S(1)}, bf16[576,512]{1,0:T(8,128)(2,1)S(1)}, u32[]{:S(2)}, u32[]{:S(2)}) collective-permute-start(bf16[576,512]{1,0:T(8,128)(2,1)S(1)} %fusion.30), channel_id=1, source_target_pairs={{0,1},{1,0},{2,3},{3,2},{4,5},{5,4},{6,7},{7,6},{8,9},{9,8},{10,11... | collective-permute-start | bytes 1769480 | tf_op jit(solution)/shard_map/ppermute | solution.py:81
  431.6 73.6 %collective-permute-start.22 = (bf16[576,512]{1,0:T(8,128)(2,1)}, bf16[576,512]{1,0:T(8,128)(2,1)}, u32[]{:S(2)}, u32[]{:S(2)}) collective-permute-start(bf16[576,512]{1,0:T(8,128)(2,1)} %collective-permute-done.20), channel_id=1, source_target_pairs={{0,1},{1,0},{2,3},{3,2},{4,5},{5,4},{6,7},{7,6},{8,9},{9,8},{10,11... | collective-permute-start | bytes 1769480 | tf_op jit(solution)/shard_map/ppermute | solution.py:81
  474.4 32.0 %copy-start.22 = (bf16[576,256]{1,0:T(8,128)(2,1)S(1)}, bf16[576,256]{1,0:T(8,128)(2,1)}, u32[]{:S(2)}) copy-start(bf16[576,256]{1,0:T(8,128)(2,1)} %get-tuple-element.304) | copy-start | bytes 884740
  474.4 32.0 %copy-start.23 = (bf16[576,256]{1,0:T(8,128)(2,1)S(1)}, bf16[576,256]{1,0:T(8,128)(2,1)}, u32[]{:S(2)}) copy-start(bf16[576,256]{1,0:T(8,128)(2,1)} %get-tuple-element.306) | copy-start | bytes 884740
  474.4 32.1 %copy-start.21 = (bf16[576,256]{1,0:T(8,128)(2,1)S(1)}, bf16[576,256]{1,0:T(8,128)(2,1)}, u32[]{:S(2)}) copy-start(bf16[576,256]{1,0:T(8,128)(2,1)} %get-tuple-element.305) | copy-start | bytes 884740
  474.4 44.3 %all-to-all-start.5 = ((bf16[8,128,256]{2,1,0:T(8,128)(2,1)}), bf16[8,128,256]{2,1,0:T(8,128)(2,1)S(1)}, u32[]{:S(2)}, u32[]{:S(2)}) async-start(bf16[8,128,256]{2,1,0:T(8,128)(2,1)} %bitcast.48), calls=%async_computation.5 | async-start | bytes 1048576 | tf_op jit(solution)/shard_map/all_to_all | solution.py:764
  518.7 3.9 collective-permute-start.29
  518.9 8.7 %collective-permute-start.30 = (bf16[256,256]{1,0:T(8,128)(2,1)S(1)}, bf16[256,256]{1,0:T(8,128)(2,1)S(1)}, u32[]{:S(2)}, u32[]{:S(2)}) collective-permute-start(bf16[256,256]{1,0:T(8,128)(2,1)S(1)} %bitcast.154), channel_id=1, source_target_pairs={{0,1},{1,0},{2,3},{3,2},{4,5},{5,4},{6,7},{7,6},{8,9},{9,8},{10,11... | collective-permute-start | bytes 393224 | tf_op jit(solution)/shard_map/ppermute | solution.py:81
  522.6 5.0 collective-permute-start.31
  (63 other events, 292.9 us)

commit v2 on v1

--- a/solution.py
+++ b/solution.py
@@ -88,43 +88,65 @@
     return lax.dynamic_slice_in_dim(value, index * size, size, axis)
 
 
-def ring_scatter(value, axis, ring, place):
-    size = value.shape[axis] // ring.count
-    if ring.count == 1:
-        return wide(value)
-    total = short(cut(value, (place - 1) % ring.count, size, axis))
-    for step in range(ring.count - 1):
-        arrived = ring.send(total, 1)
-        mine = cut(value, (place - 2 - step) % ring.count, size, axis)
-        total = wide(mine) + wide(arrived)
-        if step < ring.count - 2:
-            total = short(total)
-    return total
-
-
-def ring_gather(piece, axis, ring, place):
-    if ring.count == 1:
-        return piece
-    size = piece.shape[axis]
-    shape = list(piece.shape)
-    shape[axis] = size * ring.count
-    whole = lax.dynamic_update_slice_in_dim(
-        jnp.zeros(shape, piece.dtype), piece, place * size, axis
-    )
-    for step in range(1, ring.count):
-        piece = ring.send(piece, 1)
-        whole = lax.dynamic_update_slice_in_dim(
-            whole, piece, ((place - step) % ring.count) * size, axis
-        )
-    return whole
-
-
-def ring_sum_kernel(
-    inner, halves, x_ref, small_ref, o_ref, small_sum_ref, got, small_got, send_sems, recv_sems, small_sems
+def tile_pairs(tiles):
+    return [(i, j) for i in range(tiles) for j in range(i, tiles)]
+
+
+def pick(options, index):
+    chosen = jnp.int32(options[0])
+    for k in range(1, len(options)):
+        chosen = jnp.where(index == k, jnp.int32(options[k]), chosen)
+    return chosen
+
+
+def sum_kernel(
+    inner,
+    tile,
+    down_ref,
+    up_ref,
+    qkvo_ref,
+    small_ref,
+    mom_qkv_ref,
+    mom_out_ref,
+    mom_up_ref,
+    mom_down_ref,
+    down_sum_ref,
+    up_sum_ref,
+    qkvo_sum_ref,
+    small_sum_ref,
+    square_ref,
+    tiles_ref,
+    got_down,
+    got_up,
+    got_low,
+    got_high,
+    small_got,
+    mom_up,
+    mom_down,
+    mom_column,
+    mom_row,
+    up_low,
+    down_low,
+    part,
+    core_got,
+    chip_sum,
+    x_got,
+    ring_sems,
+    late_sems,
+    small_sems,
+    load_sem,
+    core_sems,
+    x_sems,
+    back_sems,
+    square_x_sems,
+    square_core_sems,
 ):
+    mesh_type = pl.DeviceIdType.MESH
     count = lax.axis_size("dp")
     index = lax.axis_index("dp")
     team = lax.axis_index("tensor")
+    wides = lax.axis_size("tensor") // 2
+    x_at, core = team // 2, team % 2
     outer = count // inner
     if inner == 2:
         place = jnp.where(index % 2 == 0, index // 2, count - 1 - index // 2)
@@ -137,65 +159,191 @@
         def device(p):
             return p
 
-    targets = (device((place + 1) % count), device((place + count - 1) % count))
+    ring_next = ((device((place + 1) % count), team), (device((place + count - 1) % count), team))
+    core_next = (index, x_at * 2 + 1 - core)
+    x_up = (index, ((x_at + 1) % wides) * 2 + core)
+    x_down = (index, ((x_at + wides - 1) % wides) * 2 + core)
+
     barrier = pltpu.get_barrier_semaphore()
 
     def greet(hop, carry):
         pl.semaphore_signal(
-            barrier,
-            inc=1,
-            device_id=((index + hop) % count, team),
-            device_id_type=pl.DeviceIdType.MESH,
+            barrier, inc=1, device_id=((index + hop) % count, team), device_id_type=mesh_type
         )
         return carry
 
     lax.fori_loop(1, count, greet, 0)
-    pl.semaphore_wait(barrier, count - 1)
-    half = x_ref.shape[0] // 2
-    chunk = half // count
-    sub = chunk // halves
-    streams = [(d, h) for h in range(halves) for d in range(2)]
-
-    def rows(d, h, hop):
-        at = (place + count - hop) % count if d == 0 else (place + hop) % count
-        return pl.ds(pl.multiple_of(d * half + at * chunk + h * sub, 8), sub)
-
-    def copy(d, h, step, src, dst):
+    others = [core_next, x_up] + ([x_down] if wides > 2 else [])
+    for other in others:
+        pl.semaphore_signal(barrier, inc=1, device_id=other, device_id_type=mesh_type)
+    pl.semaphore_wait(barrier, count - 1 + len(others))
+
+    def remote(src, dst, sems, at, target):
         return pltpu.make_async_remote_copy(
             src_ref=src,
             dst_ref=dst,
-            send_sem=send_sems.at[step, d, h],
-            recv_sem=recv_sems.at[step, d, h],
-            device_id=(targets[d], team),
-            device_id_type=pl.DeviceIdType.MESH,
+            send_sem=sems.at[(0, *at)],
+            recv_sem=sems.at[(1, *at)],
+            device_id=target,
+            device_id_type=mesh_type,
         )
 
-    def copies(step):
-        made = []
-        for d, h in streams:
+    sent = []
+
+    def ring(lanes, sems):
+        streams = []
+        for d, (x_ref, o_ref, first, length, got) in enumerate(lanes):
+            chunk = length // count
+            halves = 2 if chunk % 32 == 0 else 1
+            sub = chunk // halves
+            for h in range(halves):
+                streams.append((d, h, x_ref, o_ref, first, chunk, sub, got))
+        streams.sort(key=lambda one: one[1])
+
+        def rows(stream, hop):
+            d, h, _, _, first, chunk, sub, _ = stream
+            at = (place + count - hop) % count if d == 0 else (place + hop) % count
+            return pl.ds(pl.multiple_of(first + at * chunk + h * sub, 16), sub)
+
+        def copy(stream, step):
+            d, h, x_ref, o_ref, _, _, sub, got = stream
             if step < count - 1:
-                slot = got.at[step, d, pl.ds(h * sub, sub)]
-                src = x_ref.at[rows(d, h, 1)] if step == 0 else got.at[step - 1, d, pl.ds(h * sub, sub)]
-                made.append(copy(d, h, step, src, slot))
+                slot = pl.ds(h * sub, sub)
+                src = x_ref.at[rows(stream, 1)] if step == 0 else got.at[step - 1, slot]
+                dst = got.at[step, slot]
             else:
-                at = o_ref.at[rows(d, h, step - (count - 1))]
-                made.append(copy(d, h, step, at, at))
-        return made
-
-    everything = []
-    flying = copies(0)
-    for one in flying:
-        one.start()
-    everything += flying
+                src = dst = o_ref.at[rows(stream, step - (count - 1))]
+            return remote(src, dst, sems, (step, d, h), ring_next[d])
+
+        for stream in streams:
+            copy(stream, 0).start()
+        yield 0
+        for step in range(2 * (count - 1)):
+            for stream in streams:
+                _, h, x_ref, o_ref, _, _, sub, got = stream
+                one = copy(stream, step)
+                one.wait_recv()
+                sent.append(one)
+                if step < count - 1:
+                    slot = pl.ds(h * sub, sub)
+                    total = wide(got[step, slot]) + wide(x_ref[rows(stream, step + 2)])
+                    if step < count - 2:
+                        got[step, slot] = short(total)
+                    else:
+                        o_ref[rows(stream, 0)] = short(total)
+                if step < 2 * count - 3:
+                    copy(stream, step + 1).start()
+                yield step
+
+    half = qkvo_ref.shape[0] // 2
+    first_ring = ring(
+        [
+            (down_ref, down_sum_ref, 0, down_ref.shape[0], got_down),
+            (up_ref, up_sum_ref, 0, up_ref.shape[0], got_up),
+        ],
+        ring_sems,
+    )
+    second_ring = ring(
+        [(qkvo_ref, qkvo_sum_ref, 0, half, got_low), (qkvo_ref, qkvo_sum_ref, half, half, got_high)],
+        late_sems,
+    )
+
+    is_up, is_down = index == 4, index == 5
+    is_gram = jnp.logical_or(is_up, is_down)
+    size = up_ref.shape[0]
+    pairs = tile_pairs(size // tile)
+    share = len(pairs) // 2
+    load_up = pltpu.make_async_copy(mom_up_ref, mom_up, load_sem.at[0])
+    load_down = pltpu.make_async_copy(mom_down_ref, mom_down, load_sem.at[0])
+
+    def gram_tasks():
+        for ref, mom, total, low, load, mine in (
+            (mom_up_ref, mom_up, up_sum_ref, up_low, load_up, is_up),
+            (mom_down_ref, mom_down, down_sum_ref, down_low, load_down, is_down),
+        ):
+
+            @pl.when(mine)
+            def _():
+                load.wait()
+
+            for start in range(0, ref.shape[0], 256):
+
+                @pl.when(mine)
+                def _():
+                    rows = pl.ds(start, 256)
+                    low[rows, :] = short(momentum_decay * mom[rows, :] + wide(total[rows, :]))
+
+            yield
+
+        def compute(k):
+            row = pl.ds(pl.multiple_of(pick([p[0] for p in pairs], k) * tile, tile), tile)
+            column = pl.ds(pl.multiple_of(pick([p[1] for p in pairs], k) * tile, tile), tile)
+
+            @pl.when(is_up)
+            def _():
+                part[k] = mm_nt(up_low[row, :], up_low[column, :])
+
+            @pl.when(is_down)
+            def _():
+                part[k] = mm_tn(down_low[:, row], down_low[:, column])
+
+        def to_core(i):
+            return remote(part.at[(1 - core) * share + i], core_got.at[i], core_sems, (i,), core_next)
+
+        def to_x(i, hop):
+            src = chip_sum.at[i] if hop == 0 else x_got.at[hop - 1, i]
+            return remote(src, x_got.at[hop, i], x_sems, (hop, i), x_up)
+
+        def to_back(i):
+            at = tiles_ref.at[core * share + i]
+            return remote(at, at, back_sems, (i,), core_next)
+
+        for i in range(share):
+            compute((1 - core) * share + i)
+
+            @pl.when(is_gram)
+            def _():
+                to_core(i).start()
+
+            yield
+        for i in range(share):
+            compute(core * share + i)
+            yield
+        for i in range(share):
+
+            @pl.when(is_gram)
+            def _():
+                to_core(i).wait_recv()
+                chip_sum[i] = part[core * share + i] + core_got[i]
+                to_x(i, 0).start()
+
+            yield
+        yield "late"
+        for hop in range(wides - 1):
+            for i in range(share):
+
+                @pl.when(is_gram)
+                def _():
+                    to_x(i, hop).wait_recv()
+                    before = chip_sum[i] if hop == 0 else tiles_ref[core * share + i]
+                    tiles_ref[core * share + i] = before + x_got[hop, i]
+                    if hop < wides - 2:
+                        to_x(i, hop + 1).start()
+                    else:
+                        to_back(i).start()
+
+        @pl.when(is_gram)
+        def _():
+            for i in range(share):
+                to_back(i).wait_recv()
+                to_core(i).wait_send()
+                to_back(i).wait_send()
+                for hop in range(wides - 1):
+                    to_x(i, hop).wait_send()
 
     def small_copy(hop):
-        return pltpu.make_async_remote_copy(
-            src_ref=small_ref,
-            dst_ref=small_got.at[hop],
-            send_sem=small_sems.at[0, hop],
-            recv_sem=small_sems.at[1, hop],
-            device_id=((index + hop) % count, team),
-            device_id_type=pl.DeviceIdType.MESH,
+        return remote(
+            small_ref, small_got.at[hop], small_sems, (hop,), ((index + hop) % count, team)
         )
 
     def small_send(hop, carry):
@@ -208,54 +356,154 @@
         one.wait_recv()
         return total + wide(small_got[hop])
 
+    is_column, is_row = index < 3, index == 3
+    is_square = index < 4
+    width = square_ref.shape[2]
+    load_column = pltpu.make_async_copy(
+        mom_qkv_ref.at[jnp.minimum(index, 2)], mom_column, load_sem.at[0]
+    )
+    load_row = pltpu.make_async_copy(mom_out_ref, mom_row, load_sem.at[0])
+    square_rows = square_ref.shape[1]
+    block = 256
+    blocks = square_rows // block
+
+    def square_x(hop, b):
+        rows = pl.ds(b * block, block)
+        return remote(
+            square_ref.at[hop, rows], square_ref.at[hop + 1, rows], square_x_sems, (hop, b), x_down
+        )
+
+    def square_core(hop, b):
+        rows = pl.ds(b * block, block)
+        return remote(
+            square_ref.at[hop, rows], square_ref.at[wides + hop, rows], square_core_sems, (hop, b), core_next
+        )
+
+    def square_work():
+        columns = pl.ds(pl.multiple_of(jnp.minimum(index, 3) * width, 128), width)
+        for b in range(blocks):
+            rows = pl.ds(b * block, block)
+            fresh = wide(qkvo_sum_ref[rows, columns])
+
+            @pl.when(is_column)
+            def _():
+                if b == 0:
+                    load_column.wait()
+                square_ref[0, rows] = short(momentum_decay * mom_column[rows, :] + fresh)
+
+            @pl.when(is_row)
+            def _():
+                if b == 0:
+                    load_row.wait()
+                square_ref[0, rows] = short(momentum_decay * mom_row[:, rows].T + fresh)
+
+            square_x(0, b).start()
+            square_core(0, b).start()
+        for hop in range(1, wides):
+            for b in range(blocks):
+                square_x(hop - 1, b).wait_recv()
+                if hop < wides - 1:
+                    square_x(hop, b).start()
+                square_core(hop, b).start()
+        for hop in range(wides):
+            for b in range(blocks):
+                square_core(hop, b).wait_recv()
+        for hop in range(wides):
+            for b in range(blocks):
+                square_core(hop, b).wait_send()
+                if hop < wides - 1:
+                    square_x(hop, b).wait_send()
+
+    next(first_ring)
     lax.fori_loop(1, count, small_send, 0)
-    for step in range(2 * (count - 1)):
-        following = copies(step + 1) if step < 2 * count - 3 else [None] * len(streams)
-        for (d, h), one, then in zip(streams, flying, following):
-            one.wait_recv()
-            if step < count - 1:
-                total = wide(got[step, d, pl.ds(h * sub, sub)]) + wide(x_ref[rows(d, h, step + 2)])
-                if step < count - 2:
-                    got[step, d, pl.ds(h * sub, sub)] = short(total)
-                else:
-                    o_ref[rows(d, h, 0)] = short(total)
-            if then is not None:
-                then.start()
-        flying = following
-        everything += [one for one in following if one is not None]
+    for one, mine in (
+        (load_up, is_up),
+        (load_down, is_down),
+        (load_column, is_column),
+        (load_row, is_row),
+    ):
+
+        @pl.when(mine)
+        def _():
+            one.start()
+
+    begun = False
+    for step in first_ring:
+        if step == 2 * count - 4 and not begun:
+            next(second_ring)
+            begun = True
+    side = gram_tasks()
+    late = False
+    for _ in second_ring:
+        if not late:
+            late = next(side) == "late"
+    while not late:
+        late = next(side) == "late"
+    pl.when(is_square)(square_work)
+    for _ in side:
+        pass
     small_sum_ref[...] = lax.fori_loop(1, count, small_wait, wide(small_ref[...]))
-    for one in everything:
+    for one in sent:
         one.wait_send()
 
 
-def ring_sum(value, small, inner, groups):
-    length, columns = value.shape
-    halves = 2 if length % (64 * groups) == 0 else 1
+def sums_over_dp(inner, down, up, qkvo, small, moments_old):
+    groups, teams = lax.axis_size("dp"), lax.axis_size("tensor")
+    wides = teams // 2
+    size, width = qkvo.shape[0], qkvo.shape[1] // 4
+    tile = size // 4
+    pairs = len(tile_pairs(4))
     steps = 2 * (groups - 1)
-    chunk = length // 2 // groups
+    mom_qkv, mom_out, mom_up, mom_down = moments_old
+    dma = pltpu.SemaphoreType.DMA
+    vmem = pl.BlockSpec(memory_space=pltpu.VMEM)
+    length = down.size + up.size + qkvo.size
     return pl.pallas_call(
-        functools.partial(ring_sum_kernel, inner, halves),
-        name="ring_sum",
+        functools.partial(sum_kernel, inner, tile),
+        name="sums_over_dp",
         out_shape=(
-            jax.ShapeDtypeStruct(value.shape, bf16),
+            jax.ShapeDtypeStruct(down.shape, bf16),
+            jax.ShapeDtypeStruct(up.shape, bf16),
+            jax.ShapeDtypeStruct(qkvo.shape, bf16),
             jax.ShapeDtypeStruct(small.shape, f32),
+            jax.ShapeDtypeStruct((teams, size, width), bf16),
+            jax.ShapeDtypeStruct((pairs, tile, tile), f32),
         ),
-        in_specs=[pl.BlockSpec(memory_space=pltpu.VMEM)] * 2,
-        out_specs=[pl.BlockSpec(memory_space=pltpu.VMEM)] * 2,
+        in_specs=[vmem] * 4 + [pl.BlockSpec(memory_space=pl.ANY)] * 4,
+        out_specs=[vmem] * 6,
         scratch_shapes=[
-            pltpu.VMEM((groups - 1, 2, chunk, columns), bf16),
+            pltpu.VMEM((groups - 1, down.shape[0] // groups, down.shape[1]), bf16),
+            pltpu.VMEM((groups - 1, up.shape[0] // groups, up.shape[1]), bf16),
+            pltpu.VMEM((groups - 1, size // 2 // groups, qkvo.shape[1]), bf16),
+            pltpu.VMEM((groups - 1, size // 2 // groups, qkvo.shape[1]), bf16),
             pltpu.VMEM((groups, *small.shape), bf16),
-            pltpu.SemaphoreType.DMA((steps, 2, halves)),
-            pltpu.SemaphoreType.DMA((steps, 2, halves)),
-            pltpu.SemaphoreType.DMA((2, groups)),
+            pltpu.VMEM(up.shape, f32),
+            pltpu.VMEM(down.shape, f32),
+            pltpu.VMEM((size, width), f32),
+            pltpu.VMEM((width, size), f32),
+            pltpu.VMEM(up.shape, bf16),
+            pltpu.VMEM(down.shape, bf16),
+            pltpu.VMEM((pairs, tile, tile), f32),
+            pltpu.VMEM((pairs // 2, tile, tile), f32),
+            pltpu.VMEM((pairs // 2, tile, tile), f32),
+            pltpu.VMEM((wides - 1, pairs // 2, tile, tile), f32),
+            dma((2, steps, 2, 2)),
+            dma((2, steps, 2, 2)),
+            dma((2, groups)),
+            dma((1,)),
+            dma((2, pairs // 2)),
+            dma((2, wides - 1, pairs // 2)),
+            dma((2, pairs // 2)),
+            dma((2, wides - 1, size // 256)),
+            dma((2, wides, size // 256)),
         ],
         compiler_params=pltpu.CompilerParams(
-            collective_id=0, has_side_effects=True, vmem_limit_bytes=40 * 2**20
+            collective_id=0, has_side_effects=True, vmem_limit_bytes=52 * 2**20
         ),
         cost_estimate=pl.CostEstimate(
-            flops=length * columns, bytes_accessed=4 * length * columns, transcendentals=0
+            flops=length, bytes_accessed=4 * length, transcendentals=0
         ),
-    )(value, small)
+    )(down, up, qkvo, small, mom_qkv, mom_out, mom_up, mom_down)
 
 
 def dot(left, right):
@@ -265,7 +513,7 @@
     return lax.dot_general(left, right, (((1,), (1,)), ((), ())), preferred_element_type=f32)
 
 def polar_kernel(block, m_ref, o_ref, x_ref, gram_ref, low_ref):
-    size = m_ref.shape[0]
+    teams, size, width = m_ref.shape
     keep = o_ref.shape[1]
     blocks = size // block
 
@@ -273,14 +521,17 @@
         return pl.ds(pl.multiple_of(i * block, block), block)
 
     def norm_step(i, total):
-        part = wide(m_ref[rows(i), :])
-        return total + jnp.sum(part * part, axis=0, keepdims=True)
-
-    total = lax.fori_loop(0, blocks, norm_step, jnp.zeros((1, m_ref.shape[1]), f32))
+        for r in range(teams):
+            part = wide(m_ref[r, rows(i), :])
+            total = total + jnp.sum(part * part, axis=0, keepdims=True)
+        return total
+
+    total = lax.fori_loop(0, blocks, norm_step, jnp.zeros((1, width), f32))
     scale = lax.rsqrt(jnp.sum(total, axis=1, keepdims=True) + 1e-07)
 
     def scale_step(i, carry):
-        x_ref[0, rows(i), :] = short(wide(m_ref[rows(i), :]) * scale)
+        for r in range(teams):
+            x_ref[0, rows(i), r * width : (r + 1) * width] = short(wide(m_ref[r, rows(i), :]) * scale)
         return carry
 
     lax.fori_loop(0, blocks, scale_step, 0)
@@ -314,16 +565,16 @@
     lax.fori_loop(0, 2, two, 0)
     sweep(0, True)
 
-def polar_columns(matrix, keep):
-    size = matrix.shape[0]
+def polar_columns(matrix):
+    teams, size, width = matrix.shape
     return pl.pallas_call(
         functools.partial(polar_kernel, 512),
         name="polar",
-        out_shape=jax.ShapeDtypeStruct((size, keep), bf16),
+        out_shape=jax.ShapeDtypeStruct((size, width), bf16),
         in_specs=[pl.BlockSpec(memory_space=pltpu.VMEM)],
         out_specs=pl.BlockSpec(memory_space=pltpu.VMEM),
         scratch_shapes=[
-            pltpu.VMEM((2, size, matrix.shape[1]), bf16),
+            pltpu.VMEM((2, size, teams * width), bf16),
             pltpu.VMEM((size, size), f32),
             pltpu.VMEM((size, size), bf16),
         ],
@@ -667,21 +918,12 @@
     small = jnp.concatenate(
         [vector_part.reshape(-1), grad_bias_pair.reshape(-1), grad_bias_up.reshape(-1)]
     )
-    parts = [
-        grad_down.reshape(-1, columns),
-        grad_up.reshape(-1, columns),
-        grad_qkvo.reshape(-1, columns),
-    ]
     rows_small = -(-small.size // (16 * columns)) * 16
     small = jnp.pad(short(small), (0, rows_small * columns - small.size)).reshape(rows_small, columns)
-    total, small_sum = ring_sum(jnp.concatenate(parts, 0), small, inner, groups)
-    sums, start = [], 0
-    for part in parts:
-        sums.append(total[start : start + part.shape[0]])
-        start += part.shape[0]
-    down_sum = sums[0].reshape(grad_down.shape)
-    up_sum = sums[1].reshape(grad_up.shape)
-    qkvo_sum = wide(sums[2].reshape(grad_qkvo.shape))
+    down_sum, up_sum, qkvo_sum, small_sum, square, gram_tiles = sums_over_dp(
+        inner, grad_down, grad_up, grad_qkvo, small, (mom_qkv, mom_out, mom_up, mom_down)
+    )
+    qkvo_sum = wide(qkvo_sum)
     small_sum = small_sum.reshape(-1)
     gradients = (
         jnp.stack([qkvo_sum[:, k * width : (k + 1) * width] for k in range(3)]),
@@ -697,68 +939,22 @@
         momentum_decay * old + grad for old, grad in zip(moments_old, gradients)
     )
 
-    everyone = ("dp", "tensor")
-    radices = (groups, wides, cores)
-
-    def ring_within(digit, low, high):
-        return Ring(everyone, radices, digit, lambda i: low <= i // teams < high)
-
-    square_mine = lax.switch(
-        jnp.minimum(group, 3),
-        [
-            lambda: short(moments[0][0]),
-            lambda: short(moments[0][1]),
-            lambda: short(moments[0][2]),
-            lambda: short(moments[1]).T,
-        ],
-    )
-    square = jnp.concatenate(
-        spread_list(square_mine, ring_within(1, 0, 4), ring_within(2, 0, 4)), 1
-    )
-
     up_low, down_low = short(moments[2]), short(moments[3])
-    tile = D // 4
-    pairs = [(i, j) for i in range(4) for j in range(i, 4)]
-
-    def pack(gram):
-        return jnp.concatenate(
-            [gram[i * tile : (i + 1) * tile, j * tile : (j + 1) * tile] for i, j in pairs], 0
-        )
-
-    packed_gram = lax.switch(
-        jnp.clip(group - 3, 0, 3),
-        [
-            lambda: jnp.zeros((len(pairs) * tile, tile), f32),
-            lambda: pack(mm_nt(up_low, up_low)),
-            lambda: pack(mm_tn(down_low, down_low)),
-            lambda: jnp.zeros((len(pairs) * tile, tile), f32),
-        ],
-    )
-    gram_x, gram_core = ring_within(1, 4, 6), ring_within(2, 4, 6)
-    part_rows = len(pairs) * tile // cores
-    held = cut(packed_gram, core_at, part_rows, 0)
-    for hop in range(1, cores):
-        held = held + gram_core.send(cut(packed_gram, (core_at + hop) % cores, part_rows, 0), hop)
-    passing, total = held, held
-    for _ in range(wides - 1):
-        passing = gram_x.send(passing, 1)
-        total = total + passing
-    packed_gram = ring_gather(total, 0, gram_core, core_at)
 
     def no_work(square, blocks):
         return jnp.zeros((D, width), bf16)
 
     def square_work(square, blocks):
-        return polar_columns(square, width)
+        return polar_columns(square)
 
     def gram_work(square, blocks):
-        return factor_columns(blocks.reshape(len(pairs), tile, tile), D, width)
+        return factor_columns(blocks, D, width)
 
     stepped = lax.switch(
         (group >= 4).astype(jnp.int32) + (group >= 6).astype(jnp.int32),
         [square_work, gram_work, no_work],
         square,
-        packed_gram,
+        gram_tiles,
     )
     dp_rows = D // groups
     steps = lax.all_to_all(

time: 542 us -> 499 us (0.921)
  Pallas kernels: 165 us -> 196 us
  starting transfers between devices: 115 us -> 84.7 us
  other arithmetic: 60.6 us -> 44 us
  local copies, waits for them, and re-layouts: 43.6 us -> 27.2 us
  waiting for transfers between devices: 77.1 us -> 64.4 us
    pallas_call x1, Pallas kernels: 129 us -> 160 us  [sums_over_dp(): pl.pallas_call(functools.partial(sum_kernel, inner, tile), name='sums_ove...]
    concatenate x2 -> x1, other arithmetic: 20.9 us -> 1.61 us  [body(): jnp.concatenate([short(mm_tn(packed_x, jnp.concatenate([grad_queries, gra...]
    add x2 -> x3, other arithmetic: 2.35 us -> 17.2 us  [body(): momentum_decay * old + grad]
    ppermute x32 -> x26, starting transfers between devices: 49.3 us -> 35.4 us  [send(): return lax.ppermute(value, self.axes, pairs)]
    all_to_all x1, starting transfers between devices: 14.4 us -> 5.43 us  [give_back(): lax.all_to_all(columns.reshape(groups, per_peer, parts * width), 'dp', sp...]
    all_to_all x1, waiting for transfers between devices: 8.78 us -> 0.01 us  [body(): lax.all_to_all(stepped.reshape(groups, dp_rows, width), 'dp', split_axis=...]
    all_to_all x1, starting transfers between devices: 30.8 us -> 23.4 us  [body(): lax.all_to_all(stepped.reshape(groups, dp_rows, width), 'dp', split_axis=...]
    unnamed x154 -> x166, local copies, waits for them, and re-layouts: 19.6 us -> 12.7 us
  transfers between devices with their start and end apart: 38 -> 32, of which waited for: 19 -> 19; matrix products, arithmetic and copies ran while one was open for 19% -> 15% of each run, Pallas kernels for 31% -> 40%
where the time goes in v2:
time: 499 us; the launch traced here: 491 us
  Pallas kernels  196 us (39%)
  starting transfers between devices  84.7 us (17%)
  waiting for transfers between devices  64.4 us (13%)
  matrix products  63.4 us (13%)
  other arithmetic  44 us (9%)
  local copies, waits for them, and re-layouts  27.2 us (5%)
  loops' own time  6.31 us (1%)
    pallas_call x1, Pallas kernels, sums_over_dp(): pl.pallas_call(functools.partial(sum_kernel, inner, tile), name='sums_ove...  160 us
    ppermute x26, waiting for transfers between devices, send(): return lax.ppermute(value, self.axes, pairs)  46.1 us
    pallas_call x1, Pallas kernels, polar_columns(): pl.pallas_call(functools.partial(polar_kernel, 512), name='polar', out_sh...  36.4 us
    ppermute x26, starting transfers between devices, send(): return lax.ppermute(value, self.axes, pairs)  35.4 us
    all_to_all x1, starting transfers between devices, body(): lax.all_to_all(stepped.reshape(groups, dp_rows, width), 'dp', split_axis=...  23.4 us
    dot_general x10, matrix products, mm(): return jnp.dot(short(left), short(right), preferred_element_type=f32)  21.7 us
    add x3, other arithmetic, body(): momentum_decay * old + grad  17.2 us
    dot_general x7, matrix products, mm_nt(): lax.dot_general(short(left), short(right), (((1,), (1,)), ((), ())), pref...  12.7 us
  transfers between devices with their start and end apart: 32, of which 19 were waited for; matrix products, arithmetic and copies ran while one was open for 15% of the time, Pallas kernels for 40%

profile of v2, /device:TPU:1, one launch (start us, length us, event | category | flops | bytes accessed | tf_op | source)
XLA Modules:
  0.0 490.7 jit_solution(5330294964107192665)
XLA Ops:
  8.4 6.4 %all-to-all-start = ((bf16[8,72,256]{2,1,0:T(8,128)(2,1)}), bf16[8,72,256]{2,1,0:T(8,128)(2,1)S(1)}, u32[]{:S(2)}, u32[]{:S(2)}) async-start(bf16[8,72,256]{2,1,0:T(8,128)(2,1)} %bitcast), calls=%async_computation | async-start | bytes 589824 | tf_op jit(solution)/shard_map/all_to_all | solution.py:810
  14.9 2.1 convert_element_type.230
  17.0 5.6 %all-to-all-done = bf16[8,72,256]{2,1,0:T(8,128)(2,1)S(1)} async-done(((bf16[8,72,256]{2,1,0:T(8,128)(2,1)}), bf16[8,72,256]{2,1,0:T(8,128)(2,1)S(1)}, u32[]{:S(2)}, u32[]{:S(2)}) %all-to-all-start) | async-done | bytes 294944 | tf_op jit(solution)/shard_map/all_to_all | solution.py:810
  23.9 3.1 collective-permute-start.1
  28.2 3.9 collective-permute-start.2
  35.5 1.7 fusion.52
  37.7 4.7 fusion.133
  42.4 3.4 fusion.46
  50.8 6.4 %collective-permute-done.4 = bf16[144,1024]{1,0:T(8,128)(2,1)S(1)} collective-permute-done((bf16[144,1024]{1,0:T(8,128)(2,1)S(1)}, bf16[144,1024]{1,0:T(8,128)(2,1)S(1)}, u32[]{:S(2)}, u32[]{:S(2)}) %collective-permute-start.4) | collective-permute-done | bytes 294944 | tf_op jit(solution)/shard_map/ppermute | solution.py:81
  60.5 4.6 collective-permute-done.5
  65.1 2.1 collective-permute-start.7
  67.3 2.1 fusion.55
  69.4 5.2 %all-to-all-start.1 = ((bf16[8,72,256]{2,1,0:T(8,128)(2,1)}), bf16[8,72,256]{2,1,0:T(8,128)(2,1)}, u32[]{:S(2)}, u32[]{:S(2)}) async-start(bf16[8,72,256]{2,1,0:T(8,128)(2,1)} %bitcast.21), calls=%async_computation.1 | async-start | bytes 589824 | tf_op jit(solution)/shard_map/all_to_all | solution.py:810
  74.6 11.4 %multiply_convert_fusion.1 = (bf16[576,1024]{1,0:T(8,128)(2,1)S(1)}, f32[576,1024]{1,0:T(8,128)}, f32[576,1024]{1,0:T(8,128)}) fusion(f32[1024]{0:T(1024)S(1)} %copy-done.59, f32[1024,1024]{1,0:T(8,128)} %param.27, bf16[144,1024]{1,0:T(8,128)(2,1)S(1)} %collective-permute-done.7, bf16[144,1024]{1,0:T(8,128)(2,1)S(1)} %collective-permute-done.6, ...), kind=kOutput, calls=%fused_computation.27 | convolution fusion | flops 1252655104 | bytes 11276288 | tf_op jit(solution)/shard_map/dot_general | solution.py:34
  89.4 3.5 all-to-all-start.2
  93.6 4.8 all-to-all-done.2
  100.8 7.0 %collective-permute-done.9 = bf16[144,1024]{1,0:T(8,128)(2,1)S(1)} collective-permute-done((bf16[144,1024]{1,0:T(8,128)(2,1)S(1)}, bf16[144,1024]{1,0:T(8,128)(2,1)S(1)}, u32[]{:S(2)}, u32[]{:S(2)}) %collective-permute-start.9) | collective-permute-done | bytes 294944 | tf_op jit(solution)/shard_map/ppermute | solution.py:81
  109.9 1.7 collective-permute-start.11
  111.6 4.3 collective-permute-done.10
  116.0 2.7 collective-permute-start.12
  119.9 1.9 fusion.134
  130.8 4.5 collective-permute-done.14
  138.5 4.7 convolution_convert_fusion.1.down_ref
  145.8 2.1 collective-permute-start.17
  147.9 3.2 convolution_convert_fusion.up_ref
  155.2 4.5 bitcast_reduce_fusion
  159.8 3.8 multiply_reduce_fusion
  177.8 159.7 %sums_over_dp.1 = (bf16[1024,1024]{1,0:T(8,128)(2,1)}, bf16[1024,1024]{1,0:T(8,128)(2,1)}, bf16[1024,1024]{1,0:T(8,128)(2,1)}, f32[16,1024]{1,0:T(8,128)S(1)}, b...) custom-call(bf16[1024,1024]{1,0:T(8,128)(2,1)} %convolution_convert_fusion.1.down_ref, ...), custom_call_target="tpu_custom_call" | custom-call | flops 3145728 | bytes 12582912 | tf_op jit(solution)/shard_map/sums_over_dp/pallas_call | solution.py:461
  337.6 42.7 %conditional.1 = (bf16[1024,256]{1,0:T(8,128)(2,1)}) conditional(s32[]{:T(128)} %clamp.3, bf16[4,1024,256]{2,1,0:T(8,128)(2,1)S(1)} %get-tuple-element.39, f32[10,256,256]{2,1,0:T(8,128)} %get-tuple-element.40, () %tuple.17), branch_computations={%region_21.22_spmd, %region_22.23_spmd, %region_23.24_spmd} | conditional | bytes 524298 | solution.py:953
  337.7 36.4 %polar.1 = bf16[1024,256]{1,0:T(8,128)(2,1)} custom-call(bf16[4,1024,256]{2,1,0:T(8,128)(2,1)S(1)} %m_ref), custom_call_target="tpu_custom_call" | custom-call | tf_op jit(solution)/shard_map/cond/branch_0_fun/polar/pallas_call | solution.py:570
  380.2 23.4 %all-to-all-start.5 = ((bf16[8,128,256]{2,1,0:T(8,128)(2,1)}), bf16[8,128,256]{2,1,0:T(8,128)(2,1)S(1)}, u32[]{:S(2)}, u32[]{:S(2)}) async-start(bf16[8,128,256]{2,1,0:T(8,128)(2,1)} %bitcast.43), calls=%async_computation.5 | async-start | bytes 1048576 | tf_op jit(solution)/shard_map/all_to_all | solution.py:960
  403.6 11.4 %multiply_add_fusion = (f32[1024,1024]{1,0:T(8,128)}, f32[1024,1024]{1,0:T(8,128)}, f32[1024,1024]{1,0:T(8,128)}, f32[1024,1024]{1,0:T(8,128)}) fusion(f32[1024,1024]{1,0:T(8,128)} %mom_down_ref.1, bf16[1024,1024]{1,0:T(8,128)(2,1)S(1)} %copy-done.11, bf16[1024,1024]{1,0:T(8,128)(2,1)} %get-tuple-element.36, f32[1024,1024]{1,0:T(8,128)} %mom_up_ref.1), kind=kLoop, calls=%fused_computation.6 | loop fusion | flops 6291456 | bytes 29360128 | tf_op jit(solution)/shard_map/add | solution.py:939
  415.1 2.0 convert_element_type.286
  417.1 1.8 slice_bitcast_fusion
  426.2 2.5 copy.93
  429.4 2.7 collective-permute-done.19
  434.3 5.4 %all-to-all-start.3 = ((bf16[144,4,512]{2,0,1:T(8,128)(2,1)}), bf16[144,4,512]{2,0,1:T(8,128)(2,1)}, u32[]{:S(2)}, u32[]{:S(2)}) async-start(bf16[144,4,512]{2,0,1:T(8,128)(2,1)} %pad_maximum_fusion.11), calls=%async_computation.3 | async-start | bytes 1179648 | tf_op jit(solution)/shard_map/all_to_all | solution.py:816
  439.7 5.6 %multiply_add_fusion.2 = (f32[3,1024,256]{2,1,0:T(8,128)}, f32[3,1024,256]{2,1,0:T(8,128)}) fusion(f32[3,1024,256]{2,1,0:T(8,128)} %mom_qkv_ref.1, f32[1,1024,256]{2,1,0:T(8,128)S(1)} %get-tuple-element.147, f32[1,1024,256]{2,1,0:T(8,128)S(1)} %copy-done.8, f32[1,1024,256]{2,1,0:T(8,128)} %get-tuple-element.149), kind=kLoop, calls=%fused_computation.11 | loop fusion | flops 3145728 | bytes 12582912 | tf_op jit(solution)/shard_map/add | solution.py:939
  445.2 3.2 all-to-all-done.3
  448.4 5.4 %all-to-all-start.4 = ((bf16[8,72,512]{2,1,0:T(8,128)(2,1)}), bf16[8,72,512]{2,1,0:T(8,128)(2,1)S(1)}, u32[]{:S(2)}, u32[]{:S(2)}) async-start(bf16[8,72,512]{2,1,0:T(8,128)(2,1)} %bitcast.33), calls=%async_computation.4 | async-start | bytes 1179648 | tf_op jit(solution)/shard_map/all_to_all | solution.py:819
  456.6 4.2 collective-permute-done.23
  461.6 1.8 multiply_subtract_fusion
  463.7 4.7 all-to-all-done.4
  469.9 4.0 fusion.41
  473.9 2.4 collective-permute-start.21
  476.2 2.3 fusion.35
  478.5 3.2 collective-permute-done.20
  481.7 3.3 collective-permute-start.22
  (331 shorter events, 83.1 us)
Async XLA Ops:
  7.3 60.0 %copy-start.57 = (s32[576]{0:T(1024)}, s32[576]{0:T(1024)S(1)}, u32[]{:S(2)}) copy-start(s32[576]{0:T(1024)S(1)} %eq.126) | copy-start | bytes 6916
  8.4 14.2 %all-to-all-start = ((bf16[8,72,256]{2,1,0:T(8,128)(2,1)}), bf16[8,72,256]{2,1,0:T(8,128)(2,1)S(1)}, u32[]{:S(2)}, u32[]{:S(2)}) async-start(bf16[8,72,256]{2,1,0:T(8,128)(2,1)} %bitcast), calls=%async_computation | async-start | bytes 589824 | tf_op jit(solution)/shard_map/all_to_all | solution.py:810
  17.0 18.6 %copy-start.6 = (bf16[3,1024,256]{2,1,0:T(8,128)(2,1)}, bf16[3,1024,256]{2,1,0:T(8,128)(2,1)S(1)}, u32[]{:S(2)}) copy-start(bf16[3,1024,256]{2,1,0:T(8,128)(2,1)S(1)} %convert_element_type.230) | copy-start | bytes 4718596
  22.6 5.6 %collective-permute-start = (bf16[576,256]{1,0:T(8,128)(2,1)S(1)}, bf16[576,256]{1,0:T(8,128)(2,1)S(1)}, u32[]{:S(2)}, u32[]{:S(2)}) collective-permute-start(bf16[576,256]{1,0:T(8,128)(2,1)S(1)} %bitcast.130), channel_id=1, source_target_pairs={{0,2},{1,3},{2,0},{3,1},{4,6},{5,7},{6,4},{7,5},{8,10},{9,11},{10,... | collective-permute-start | bytes 884744 | tf_op jit(solution)/shard_map/ppermute | solution.py:81
  23.9 8.6 %collective-permute-start.1 = (bf16[576,256]{1,0:T(8,128)(2,1)S(1)}, bf16[576,256]{1,0:T(8,128)(2,1)S(1)}, u32[]{:S(2)}, u32[]{:S(2)}) collective-permute-start(bf16[576,256]{1,0:T(8,128)(2,1)S(1)} %bitcast.131), channel_id=1, source_target_pairs={{0,1},{1,0},{2,3},{3,2},{4,5},{5,4},{6,7},{7,6},{8,9},{9,8},{10,11... | collective-permute-start | bytes 884744 | tf_op jit(solution)/shard_map/ppermute | solution.py:81
  28.2 5.1 %collective-permute-start.2 = (bf16[576,256]{1,0:T(8,128)(2,1)S(1)}, bf16[576,256]{1,0:T(8,128)(2,1)S(1)}, u32[]{:S(2)}, u32[]{:S(2)}) collective-permute-start(bf16[576,256]{1,0:T(8,128)(2,1)S(1)} %collective-permute-done), channel_id=1, source_target_pairs={{0,1},{1,0},{2,3},{3,2},{4,5},{5,4},{6,7},{7,6},{8,9},{9,8},{10,11... | collective-permute-start | bytes 884744 | tf_op jit(solution)/shard_map/ppermute | solution.py:81
  34.0 23.2 %copy-start.19 = (bf16[144,1024]{1,0:T(8,128)(2,1)}, bf16[144,1024]{1,0:T(8,128)(2,1)S(1)}, u32[]{:S(2)}) copy-start(bf16[144,1024]{1,0:T(8,128)(2,1)S(1)} %get-tuple-element.158) | copy-start | bytes 884740
  46.6 2.0 collective-permute-start.3
  48.9 8.3 %collective-permute-start.4 = (bf16[144,1024]{1,0:T(8,128)(2,1)S(1)}, bf16[144,1024]{1,0:T(8,128)(2,1)S(1)}, u32[]{:S(2)}, u32[]{:S(2)}) collective-permute-start(bf16[144,1024]{1,0:T(8,128)(2,1)S(1)} %slice.363), channel_id=1, source_target_pairs={{0,2},{1,3},{2,0},{3,1},{4,6},{5,7},{6,4},{7,5},{8,10},{9,11},{10,... | collective-permute-start | bytes 884744 | tf_op jit(solution)/shard_map/ppermute | solution.py:81
  50.7 18.6 %copy-start.43 = (f32[1,1024]{1,0:T(1,128)}, f32[1,1024]{1,0:T(1,128)S(1)}, u32[]{:S(2)}) copy-start(f32[1,1024]{1,0:T(1,128)S(1)} %get-tuple-element.183) | copy-start | bytes 12292
  57.1 17.5 %copy-start.59 = (f32[1024]{0:T(1024)S(1)}, f32[1024]{0:T(1024)}, u32[]{:S(2)}) copy-start(f32[1024]{0:T(1024)} %param.30) | copy-start | bytes 12292
  57.6 28.4 %copy-start.46 = (f32[144]{0:T(256)}, f32[144]{0:T(256)S(1)}, u32[]{:S(2)}) copy-start(f32[144]{0:T(256)S(1)} %add_rsqrt_fusion.1) | copy-start | bytes 1732
  57.8 28.2 %copy-start.27 = (bf16[144,1024]{1,0:T(8,128)(2,1)}, bf16[144,1024]{1,0:T(8,128)(2,1)S(1)}, u32[]{:S(2)}) copy-start(bf16[144,1024]{1,0:T(8,128)(2,1)S(1)} %fusion.86) | copy-start | bytes 884740
  57.8 7.4 %collective-permute-start.5 = (bf16[144,1024]{1,0:T(8,128)(2,1)S(1)}, bf16[144,1024]{1,0:T(8,128)(2,1)S(1)}, u32[]{:S(2)}, u32[]{:S(2)}) collective-permute-start(bf16[144,1024]{1,0:T(8,128)(2,1)S(1)} %fusion.86), channel_id=1, source_target_pairs={{0,2},{1,3},{2,0},{3,1},{4,6},{5,7},{6,4},{7,5},{8,10},{9,11},{10,... | collective-permute-start | bytes 884744 | tf_op jit(solution)/shard_map/ppermute | solution.py:81
  59.1 15.5 %collective-permute-start.6 = (bf16[144,1024]{1,0:T(8,128)(2,1)S(1)}, bf16[144,1024]{1,0:T(8,128)(2,1)S(1)}, u32[]{:S(2)}, u32[]{:S(2)}) collective-permute-start(bf16[144,1024]{1,0:T(8,128)(2,1)S(1)} %fusion.86), channel_id=1, source_target_pairs={{0,1},{1,0},{2,3},{3,2},{4,5},{5,4},{6,7},{7,6},{8,9},{9,8},{10,11... | collective-permute-start | bytes 884744 | tf_op jit(solution)/shard_map/ppermute | solution.py:81
  65.1 20.8 %copy-start.63 = (bf16[144,1024]{1,0:T(8,128)(2,1)}, bf16[144,1024]{1,0:T(8,128)(2,1)S(1)}, u32[]{:S(2)}) copy-start(bf16[144,1024]{1,0:T(8,128)(2,1)S(1)} %collective-permute-done.5) | copy-start | bytes 884740
  65.1 9.5 %collective-permute-start.7 = (bf16[144,1024]{1,0:T(8,128)(2,1)S(1)}, bf16[144,1024]{1,0:T(8,128)(2,1)S(1)}, u32[]{:S(2)}, u32[]{:S(2)}) collective-permute-start(bf16[144,1024]{1,0:T(8,128)(2,1)S(1)} %collective-permute-done.5), channel_id=1, source_target_pairs={{0,1},{1,0},{2,3},{3,2},{4,5},{5,4},{6,7},{7,6},{8,9},{9,8},{10,11... | collective-permute-start | bytes 884744 | tf_op jit(solution)/shard_map/ppermute | solution.py:81
  69.4 20.0 %all-to-all-start.1 = ((bf16[8,72,256]{2,1,0:T(8,128)(2,1)}), bf16[8,72,256]{2,1,0:T(8,128)(2,1)}, u32[]{:S(2)}, u32[]{:S(2)}) async-start(bf16[8,72,256]{2,1,0:T(8,128)(2,1)} %bitcast.21), calls=%async_computation.1 | async-start | bytes 589824 | tf_op jit(solution)/shard_map/all_to_all | solution.py:810
  88.3 10.2 %collective-permute-start.8 = (bf16[288,1024]{1,0:T(8,128)(2,1)}, bf16[288,1024]{1,0:T(8,128)(2,1)}, u32[]{:S(2)}, u32[]{:S(2)}) collective-permute-start(bf16[288,1024]{1,0:T(8,128)(2,1)} %slice.358), channel_id=1, source_target_pairs={{0,1},{1,0},{2,3},{3,2},{4,5},{5,4},{6,7},{7,6},{8,9},{9,8},{10,11... | collective-permute-start | bytes 1769480 | tf_op jit(solution)/shard_map/ppermute | solution.py:81
  89.4 9.0 %all-to-all-start.2 = ((bf16[4,144,256]{2,1,0:T(8,128)(2,1)}), bf16[4,144,256]{2,1,0:T(8,128)(2,1)S(1)}, u32[]{:S(2)}, u32[]{:S(2)}) async-start(bf16[4,144,256]{2,1,0:T(8,128)(2,1)} %bitcast.22), calls=%async_computation.2 | async-start | bytes 589824 | tf_op jit(solution)/shard_map/all_to_all | solution.py:829
  98.6 21.3 %copy-start.73 = (f32[576,1024]{1,0:T(8,128)S(1)}, f32[576,1024]{1,0:T(8,128)}, u32[]{:S(2)}) copy-start(f32[576,1024]{1,0:T(8,128)} %get-tuple-element.201) | copy-start | bytes 7077892
  100.1 7.7 %collective-permute-start.9 = (bf16[144,1024]{1,0:T(8,128)(2,1)S(1)}, bf16[144,1024]{1,0:T(8,128)(2,1)S(1)}, u32[]{:S(2)}, u32[]{:S(2)}) collective-permute-start(bf16[144,1024]{1,0:T(8,128)(2,1)S(1)} %slice.362), channel_id=1, source_target_pairs={{0,2},{1,3},{2,0},{3,1},{4,6},{5,7},{6,4},{7,5},{8,10},{9,11},{10,... | collective-permute-start | bytes 884744 | tf_op jit(solution)/shard_map/ppermute | solution.py:81
  107.8 12.1 %copy-start.72 = (f32[576,1024]{1,0:T(8,128)S(1)}, f32[576,1024]{1,0:T(8,128)}, u32[]{:S(2)}) copy-start(f32[576,1024]{1,0:T(8,128)} %get-tuple-element.141) | copy-start | bytes 7077892
  108.2 11.7 %copy-start.40 = (f32[1024,1024]{1,0:T(8,128)S(1)}, f32[1024,1024]{1,0:T(8,128)}, u32[]{:S(2)}) copy-start(f32[1024,1024]{1,0:T(8,128)} %param.28) | copy-start | bytes 12582916
  109.1 12.6 %copy-start.29 = (bf16[144,1024]{1,0:T(8,128)(2,1)}, bf16[144,1024]{1,0:T(8,128)(2,1)S(1)}, u32[]{:S(2)}) copy-start(bf16[144,1024]{1,0:T(8,128)(2,1)S(1)} %convert_element_type.257) | copy-start | bytes 884740
  109.2 6.8 %collective-permute-start.10 = (bf16[144,1024]{1,0:T(8,128)(2,1)S(1)}, bf16[144,1024]{1,0:T(8,128)(2,1)S(1)}, u32[]{:S(2)}, u32[]{:S(2)}) collective-permute-start(bf16[144,1024]{1,0:T(8,128)(2,1)S(1)} %convert_element_type.257), channel_id=1, source_target_pairs={{0,2},{1,3},{2,0},{3,1},{4,6},{5,7},{6,4},{7,5},{8,10},{9,11},{10,... | collective-permute-start | bytes 884744 | tf_op jit(solution)/shard_map/ppermute | solution.py:81
  109.9 8.8 %collective-permute-start.11 = (bf16[144,1024]{1,0:T(8,128)(2,1)S(1)}, bf16[144,1024]{1,0:T(8,128)(2,1)S(1)}, u32[]{:S(2)}, u32[]{:S(2)}) collective-permute-start(bf16[144,1024]{1,0:T(8,128)(2,1)S(1)} %convert_element_type.257), channel_id=1, source_target_pairs={{0,1},{1,0},{2,3},{3,2},{4,5},{5,4},{6,7},{7,6},{8,9},{9,8},{10,11... | collective-permute-start | bytes 884744 | tf_op jit(solution)/shard_map/ppermute | solution.py:81
  116.0 3.9 collective-permute-start.12
  123.7 2.1 collective-permute-start.13
  127.0 8.3 %collective-permute-start.14 = (bf16[144,1024]{1,0:T(8,128)(2,1)S(1)}, bf16[144,1024]{1,0:T(8,128)(2,1)S(1)}, u32[]{:S(2)}, u32[]{:S(2)}) collective-permute-start(bf16[144,1024]{1,0:T(8,128)(2,1)S(1)} %slice.361), channel_id=1, source_target_pairs={{0,2},{1,3},{2,0},{3,1},{4,6},{5,7},{6,4},{7,5},{8,10},{9,11},{10,... | collective-permute-start | bytes 884744 | tf_op jit(solution)/shard_map/ppermute | solution.py:81
  137.7 8.1 %collective-permute-start.15 = (bf16[160,1024]{1,0:T(8,128)(2,1)S(1)}, bf16[160,1024]{1,0:T(8,128)(2,1)S(1)}, u32[]{:S(2)}, u32[]{:S(2)}) collective-permute-start(bf16[160,1024]{1,0:T(8,128)(2,1)S(1)} %concatenate.70), channel_id=1, source_target_pairs={{0,2},{1,3},{2,0},{3,1},{4,6},{5,7},{6,4},{7,5},{8,10},{9,11},{10,... | collective-permute-start | bytes 983048 | tf_op jit(solution)/shard_map/ppermute | solution.py:81
  143.1 8.1 %collective-permute-start.16 = (bf16[160,1024]{1,0:T(8,128)(2,1)S(1)}, bf16[160,1024]{1,0:T(8,128)(2,1)}, u32[]{:S(2)}, u32[]{:S(2)}) collective-permute-start(bf16[160,1024]{1,0:T(8,128)(2,1)S(1)} %concatenate.70), channel_id=1, source_target_pairs={{0,1},{1,0},{2,3},{3,2},{4,5},{5,4},{6,7},{7,6},{8,9},{9,8},{10,11... | collective-permute-start | bytes 983048 | tf_op jit(solution)/shard_map/ppermute | solution.py:81
  145.8 6.4 %collective-permute-start.17 = (bf16[160,1024]{1,0:T(8,128)(2,1)S(1)}, bf16[160,1024]{1,0:T(8,128)(2,1)}, u32[]{:S(2)}, u32[]{:S(2)}) collective-permute-start(bf16[160,1024]{1,0:T(8,128)(2,1)S(1)} %collective-permute-done.15), channel_id=1, source_target_pairs={{0,1},{1,0},{2,3},{3,2},{4,5},{5,4},{6,7},{7,6},{8,9},{9,8},{10,11... | collective-permute-start | bytes 983048 | tf_op jit(solution)/shard_map/ppermute | solution.py:81
  176.2 242.9 %collective-permute-start.18 = (bf16[288,1024]{1,0:T(8,128)(2,1)}, bf16[288,1024]{1,0:T(8,128)(2,1)}, u32[]{:S(2)}, u32[]{:S(2)}) collective-permute-start(bf16[288,1024]{1,0:T(8,128)(2,1)} %slice.356), channel_id=1, source_target_pairs={{0,1},{1,0},{2,3},{3,2},{4,5},{5,4},{6,7},{7,6},{8,9},{9,8},{10,11... | collective-permute-start | bytes 1769480 | tf_op jit(solution)/shard_map/ppermute | solution.py:81
  337.6 66.1 %copy-start.11 = (bf16[1024,1024]{1,0:T(8,128)(2,1)S(1)}, bf16[1024,1024]{1,0:T(8,128)(2,1)}, u32[]{:S(2)}) copy-start(bf16[1024,1024]{1,0:T(8,128)(2,1)} %get-tuple-element.37) | copy-start | bytes 6291460
  380.2 54.0 %all-to-all-start.5 = ((bf16[8,128,256]{2,1,0:T(8,128)(2,1)}), bf16[8,128,256]{2,1,0:T(8,128)(2,1)S(1)}, u32[]{:S(2)}, u32[]{:S(2)}) async-start(bf16[8,128,256]{2,1,0:T(8,128)(2,1)} %bitcast.43), calls=%async_computation.5 | async-start | bytes 1048576 | tf_op jit(solution)/shard_map/all_to_all | solution.py:960
  423.6 8.5 %collective-permute-start.19 = (bf16[144,1024]{1,0:T(8,128)(2,1)}, bf16[144,1024]{1,0:T(8,128)(2,1)}, u32[]{:S(2)}, u32[]{:S(2)}) collective-permute-start(bf16[144,1024]{1,0:T(8,128)(2,1)} %slice.360), channel_id=1, source_target_pairs={{0,2},{1,3},{2,0},{3,1},{4,6},{5,7},{6,4},{7,5},{8,10},{9,11},{10,... | collective-permute-start | bytes 884744 | tf_op jit(solution)/shard_map/ppermute | solution.py:81
  434.3 14.2 %all-to-all-start.3 = ((bf16[144,4,512]{2,0,1:T(8,128)(2,1)}), bf16[144,4,512]{2,0,1:T(8,128)(2,1)}, u32[]{:S(2)}, u32[]{:S(2)}) async-start(bf16[144,4,512]{2,0,1:T(8,128)(2,1)} %pad_maximum_fusion.11), calls=%async_computation.3 | async-start | bytes 1179648 | tf_op jit(solution)/shard_map/all_to_all | solution.py:816
  439.7 14.2 %copy-start.56 = (f32[2,256]{1,0:T(2,128)S(1)}, f32[2,256]{1,0:T(2,128)}, u32[]{:S(2)}) copy-start(f32[2,256]{1,0:T(2,128)} %param.29) | copy-start | bytes 6148
  439.7 14.2 %copy-start.62 = (f32[2,256]{1,0:T(2,128)S(1)}, f32[2,256]{1,0:T(2,128)}, u32[]{:S(2)}) copy-start(f32[2,256]{1,0:T(2,128)} %param.36) | copy-start | bytes 6148
  448.4 19.9 %all-to-all-start.4 = ((bf16[8,72,512]{2,1,0:T(8,128)(2,1)}), bf16[8,72,512]{2,1,0:T(8,128)(2,1)S(1)}, u32[]{:S(2)}, u32[]{:S(2)}) async-start(bf16[8,72,512]{2,1,0:T(8,128)(2,1)} %bitcast.33), calls=%async_computation.4 | async-start | bytes 1179648 | tf_op jit(solution)/shard_map/all_to_all | solution.py:819
  454.5 13.9 %copy-start.58 = (s32[576]{0:T(1024)S(1)}, s32[576]{0:T(1024)}, u32[]{:S(2)}) copy-start(s32[576]{0:T(1024)} %copy-done.57) | copy-start | bytes 6916
  454.5 8.9 %collective-permute-start.24 = (bf16[256,256]{1,0:T(8,128)(2,1)S(1)}, bf16[256,256]{1,0:T(8,128)(2,1)S(1)}, u32[]{:S(2)}, u32[]{:S(2)}) collective-permute-start(bf16[256,256]{1,0:T(8,128)(2,1)S(1)} %bitcast.138), channel_id=1, source_target_pairs={{0,1},{1,0},{2,3},{3,2},{4,5},{5,4},{6,7},{7,6},{8,9},{9,8},{10,11... | collective-permute-start | bytes 393224 | tf_op jit(solution)/shard_map/ppermute | solution.py:81
  455.7 5.1 %collective-permute-start.23 = (bf16[256,256]{1,0:T(8,128)(2,1)S(1)}, bf16[256,256]{1,0:T(8,128)(2,1)S(1)}, u32[]{:S(2)}, u32[]{:S(2)}) collective-permute-start(bf16[256,256]{1,0:T(8,128)(2,1)S(1)} %bitcast.139), channel_id=1, source_target_pairs={{0,2},{1,3},{2,0},{3,1},{4,6},{5,7},{6,4},{7,5},{8,10},{9,11},{10,... | collective-permute-start | bytes 393224 | tf_op jit(solution)/shard_map/ppermute | solution.py:81
  460.8 2.6 collective-permute-start.25
  469.2 12.5 %collective-permute-start.20 = (bf16[576,512]{1,0:T(8,128)(2,1)S(1)}, bf16[576,512]{1,0:T(8,128)(2,1)S(1)}, u32[]{:S(2)}, u32[]{:S(2)}) collective-permute-start(bf16[576,512]{1,0:T(8,128)(2,1)S(1)} %fusion.31), channel_id=1, source_target_pairs={{0,2},{1,3},{2,0},{3,1},{4,6},{5,7},{6,4},{7,5},{8,10},{9,11},{10,... | collective-permute-start | bytes 1769480 | tf_op jit(solution)/shard_map/ppermute | solution.py:81
  473.9 11.2 %collective-permute-start.21 = (bf16[576,512]{1,0:T(8,128)(2,1)S(1)}, bf16[576,512]{1,0:T(8,128)(2,1)S(1)}, u32[]{:S(2)}, u32[]{:S(2)}) collective-permute-start(bf16[576,512]{1,0:T(8,128)(2,1)S(1)} %fusion.31), channel_id=1, source_target_pairs={{0,1},{1,0},{2,3},{3,2},{4,5},{5,4},{6,7},{7,6},{8,9},{9,8},{10,11... | collective-permute-start | bytes 1769480 | tf_op jit(solution)/shard_map/ppermute | solution.py:81
  481.7 4.9 %collective-permute-start.22 = (bf16[576,512]{1,0:T(8,128)(2,1)S(1)}, bf16[576,512]{1,0:T(8,128)(2,1)S(1)}, u32[]{:S(2)}, u32[]{:S(2)}) collective-permute-start(bf16[576,512]{1,0:T(8,128)(2,1)S(1)} %collective-permute-done.20), channel_id=1, source_target_pairs={{0,1},{1,0},{2,3},{3,2},{4,5},{5,4},{6,7},{7,6},{8,9},{9,8},{10,11... | collective-permute-start | bytes 1769480 | tf_op jit(solution)/shard_map/ppermute | solution.py:81
  (63 other events, 311.8 us)

commit v3 on v2

--- a/solution.py
+++ b/solution.py
@@ -106,6 +106,9 @@
     up_ref,
     qkvo_ref,
     small_ref,
+    input_ref,
+    mid_ref,
+    result_ref,
     mom_qkv_ref,
     mom_out_ref,
     mom_up_ref,
@@ -116,6 +119,7 @@
     small_sum_ref,
     square_ref,
     tiles_ref,
+    given_ref,
     got_down,
     got_up,
     got_low,
@@ -140,6 +144,16 @@
     back_sems,
     square_x_sems,
     square_core_sems,
+    input_core,
+    input_x,
+    input_out,
+    input_own,
+    stage,
+    back,
+    input_core_sems,
+    input_x_sems,
+    stage_sems,
+    given_sems,
 ):
     mesh_type = pl.DeviceIdType.MESH
     count = lax.axis_size("dp")
@@ -173,10 +187,14 @@
         return carry
 
     lax.fori_loop(1, count, greet, 0)
-    others = [core_next, x_up] + ([x_down] if wides > 2 else [])
-    for other in others:
-        pl.semaphore_signal(barrier, inc=1, device_id=other, device_id_type=mesh_type)
-    pl.semaphore_wait(barrier, count - 1 + len(others))
+    for hop in range(1, 2 * wides):
+        pl.semaphore_signal(
+            barrier,
+            inc=1,
+            device_id=(index, (team + hop) % (2 * wides)),
+            device_id_type=mesh_type,
+        )
+    pl.semaphore_wait(barrier, count - 1 + 2 * wides - 1)
 
     def remote(src, dst, sems, at, target):
         return pltpu.make_async_remote_copy(
@@ -248,6 +266,74 @@
         late_sems,
     )
 
+    teams = 2 * wides
+    peers = count // teams
+
+    def input_tasks():
+
+        def over_core(i):
+            return remote(input_ref.at[wides + i], input_core.at[i], input_core_sems, (i,), core_next)
+
+        def over_x(hop):
+            return remote(input_out.at[hop], input_x.at[hop], input_x_sems, (hop,), x_up)
+
+        def over_teams(hop):
+            target = (team + hop) % teams
+            mine = back.at[pl.ds(team * peers, peers)]
+            return remote(stage.at[hop], mine, stage_sems, (hop,), (index, target))
+
+        for i in range(wides - 1, -1, -1):
+            over_core(i).start()
+        for _ in range(5):
+            yield
+        for hop in range(wides):
+            i = wides - 1 - hop
+            over_core(i).wait_recv()
+            total = wide(input_ref[i]) + wide(input_core[i])
+            if hop > 0:
+                over_x(hop - 1).wait_recv()
+                total = total + wide(input_x[hop - 1])
+            if i > 0:
+                input_out[hop] = short(total)
+                over_x(hop).start()
+                for _ in range(8):
+                    yield
+            else:
+                input_own[...] = short(total + mid_ref[...])
+        yield
+        part_width = result_ref.shape[2] // teams
+        for hop in range(teams):
+            columns = pl.ds(pl.multiple_of((team + hop) % teams * part_width, 128), part_width)
+            for k, rows_ref in enumerate((result_ref, input_own)):
+                stage[hop, :, :, k * part_width : (k + 1) * part_width] = rows_ref[:, :, columns]
+            if hop > 0:
+                over_teams(hop).start()
+            else:
+                back[pl.ds(team * peers, peers)] = stage[0]
+            yield
+        for _ in range(8):
+            yield
+        for i in range(wides):
+            over_core(i).wait_send()
+        for hop in range(wides - 1):
+            over_x(hop).wait_send()
+        for hop in range(1, teams):
+            over_teams(hop).wait_recv()
+            over_teams(hop).wait_send()
+
+    def give(hop):
+        target = (index + hop) % count
+        return remote(back.at[target], given_ref.at[index], given_sems, (hop,), (target, team))
+
+    def give_start(hop, carry):
+        give(hop).start()
+        return carry
+
+    def give_wait(hop, carry):
+        give(hop).wait_recv()
+        give(hop).wait_send()
+        return carry
+
     is_up, is_down = index == 4, index == 5
     is_gram = jnp.logical_or(is_up, is_down)
     size = up_ref.shape[0]
@@ -318,7 +404,8 @@
                 to_x(i, 0).start()
 
             yield
-        yield "late"
+        for _ in range(12):
+            yield
         for hop in range(wides - 1):
             for i in range(share):
 
@@ -331,6 +418,9 @@
                         to_x(i, hop + 1).start()
                     else:
                         to_back(i).start()
+
+                for _ in range(2):
+                    yield
 
         @pl.when(is_gram)
         def _():
@@ -427,27 +517,28 @@
         def _():
             one.start()
 
-    begun = False
+    beside = input_tasks()
     for step in first_ring:
-        if step == 2 * count - 4 and not begun:
-            next(second_ring)
-            begun = True
+        next(beside, None)
+        if step >= 2 * count - 6:
+            next(second_ring, None)
+    for _ in beside:
+        pass
     side = gram_tasks()
-    late = False
     for _ in second_ring:
-        if not late:
-            late = next(side) == "late"
-    while not late:
-        late = next(side) == "late"
+        next(side, None)
+    lax.fori_loop(1, count, give_start, 0)
+    given_ref[index] = back[index]
     pl.when(is_square)(square_work)
     for _ in side:
         pass
+    lax.fori_loop(1, count, give_wait, 0)
     small_sum_ref[...] = lax.fori_loop(1, count, small_wait, wide(small_ref[...]))
     for one in sent:
         one.wait_send()
 
 
-def sums_over_dp(inner, down, up, qkvo, small, moments_old):
+def sums_over_dp(inner, down, up, qkvo, small, input_part, grad_mid, result, moments_old):
     groups, teams = lax.axis_size("dp"), lax.axis_size("tensor")
     wides = teams // 2
     size, width = qkvo.shape[0], qkvo.shape[1] // 4
@@ -458,6 +549,7 @@
     dma = pltpu.SemaphoreType.DMA
     vmem = pl.BlockSpec(memory_space=pltpu.VMEM)
     length = down.size + up.size + qkvo.size
+    peers, rows, model = result.shape
     return pl.pallas_call(
         functools.partial(sum_kernel, inner, tile),
         name="sums_over_dp",
@@ -468,9 +560,10 @@
             jax.ShapeDtypeStruct(small.shape, f32),
             jax.ShapeDtypeStruct((teams, size, width), bf16),
             jax.ShapeDtypeStruct((pairs, tile, tile), f32),
+            jax.ShapeDtypeStruct((groups, rows, 2 * (model // teams)), bf16),
         ),
-        in_specs=[vmem] * 4 + [pl.BlockSpec(memory_space=pl.ANY)] * 4,
-        out_specs=[vmem] * 6,
+        in_specs=[vmem] * 7 + [pl.BlockSpec(memory_space=pl.ANY)] * 4,
+        out_specs=[vmem] * 7,
         scratch_shapes=[
             pltpu.VMEM((groups - 1, down.shape[0] // groups, down.shape[1]), bf16),
             pltpu.VMEM((groups - 1, up.shape[0] // groups, up.shape[1]), bf16),
@@ -496,6 +589,16 @@
             dma((2, pairs // 2)),
             dma((2, wides - 1, size // 256)),
             dma((2, wides, size // 256)),
+            pltpu.VMEM((wides, peers, rows, model), bf16),
+            pltpu.VMEM((wides - 1, peers, rows, model), bf16),
+            pltpu.VMEM((wides - 1, peers, rows, model), bf16),
+            pltpu.VMEM((peers, rows, model), bf16),
+            pltpu.VMEM((teams, peers, rows, 2 * (model // teams)), bf16),
+            pltpu.VMEM((groups, rows, 2 * (model // teams)), bf16),
+            dma((2, wides)),
+            dma((2, wides - 1)),
+            dma((2, teams)),
+            dma((2, groups)),
         ],
         compiler_params=pltpu.CompilerParams(
             collective_id=0, has_side_effects=True, vmem_limit_bytes=52 * 2**20
@@ -503,7 +606,9 @@
         cost_estimate=pl.CostEstimate(
             flops=length, bytes_accessed=4 * length, transcendentals=0
         ),
-    )(down, up, qkvo, small, mom_qkv, mom_out, mom_up, mom_down)
+    )(
+        down, up, qkvo, small, input_part, grad_mid, result, mom_qkv, mom_out, mom_up, mom_down
+    )
 
 
 def dot(left, right):
@@ -512,13 +617,291 @@
 def dot_nt(left, right):
     return lax.dot_general(left, right, (((1,), (1,)), ((), ())), preferred_element_type=f32)
 
-def polar_kernel(block, m_ref, o_ref, x_ref, gram_ref, low_ref):
+def middle_kernel(
+    context_ref,
+    x_ref,
+    out_ref,
+    up_ref,
+    down_ref,
+    bias_ref,
+    vectors_ref,
+    upstream_ref,
+    valid_ref,
+    hidden_ref,
+    act_ref,
+    grad_z_ref,
+    grad_pre_ref,
+    grad_mid_ref,
+    own_grad_mid_ref,
+    result_ref,
+    vector_sum_ref,
+    grad_down_ref,
+    grad_up_ref,
+    slope,
+    held,
+    core_out,
+    core_got,
+    x_out,
+    x_got,
+    normed_one,
+    own_hidden,
+    normed_two,
+    own_grad_z,
+    vector_own,
+    vector_got,
+    core_sems,
+    x_sems,
+    spread_x_sems,
+    spread_core_sems,
+    vector_sems,
+):
+    mesh_type = pl.DeviceIdType.MESH
+    index = lax.axis_index("dp")
+    team = lax.axis_index("tensor")
+    teams = lax.axis_size("tensor")
+    wides = teams // 2
+    x_at, core = team // 2, team % 2
+    core_next = (index, x_at * 2 + 1 - core)
+    x_up = (index, ((x_at + 1) % wides) * 2 + core)
+    x_down = (index, ((x_at + wides - 1) % wides) * 2 + core)
+    barrier = pltpu.get_barrier_semaphore()
+    for hop in range(1, teams):
+        pl.semaphore_signal(
+            barrier, inc=1, device_id=(index, (team + hop) % teams), device_id_type=mesh_type
+        )
+    pl.semaphore_wait(barrier, teams - 1)
+    sent = []
+
+    def remote(src, dst, sems, at, target):
+        return pltpu.make_async_remote_copy(
+            src_ref=src,
+            dst_ref=dst,
+            send_sem=sems.at[(0, *at)],
+            recv_sem=sems.at[(1, *at)],
+            device_id=target,
+            device_id_type=mesh_type,
+        )
+
+    def start(one):
+        one.start()
+        sent.append(one)
+
+    def over_core(s, i):
+        return remote(core_out.at[s, i], core_got.at[s, i], core_sems, (s, i), core_next)
+
+    def over_x(s, hop):
+        return remote(x_out.at[s, hop], x_got.at[s, hop], x_sems, (s, hop), x_up)
+
+    def finish(s, filler):
+        for hop in range(wides):
+            i = wides - 1 - hop
+            over_core(s, i).wait_recv()
+            total = held[i] + wide(core_got[s, i])
+            if hop > 0:
+                if filler is not None:
+                    filler()
+                    filler = None
+                over_x(s, hop - 1).wait_recv()
+                total = total + wide(x_got[s, hop - 1])
+            if i > 0:
+                x_out[s, hop] = short(total)
+                start(over_x(s, hop))
+        return total
+
+    def along_x(s, ref, i):
+        return remote(ref.at[i], ref.at[i + 1], spread_x_sems, (s, i), x_down)
+
+    def across(s, ref, i):
+        return remote(ref.at[i], ref.at[wides + i], spread_core_sems, (s, i), core_next)
+
+    def spread(s, ref):
+        start(along_x(s, ref, 0))
+        start(across(s, ref, 0))
+
+    def arrive(s, ref, i):
+        if i > 0:
+            along_x(s, ref, i - 1).wait_recv()
+            start(across(s, ref, i))
+            if i < wides - 1:
+                start(along_x(s, ref, i))
+        across(s, ref, i).wait_recv()
+
+    share = x_ref.shape[0]
+
+    def pair(ref, i):
+        return jnp.concatenate([ref[i], ref[wides + i]], 0)
+
+    def put_pair(ref, i, value):
+        ref[i] = value[:share]
+        ref[wides + i] = value[share:]
+
+    def keep(s, i, partial):
+        core_out[s, i] = short(partial[share:])
+        start(over_core(s, i))
+        held[i] = partial[:share]
+
+    def sums(value):
+        return jnp.sum(value, axis=0, keepdims=True)
+
+    for i in range(wides - 1, -1, -1):
+        keep(0, i, dot(pair(context_ref, i), out_ref[...]))
+    mid = wide(x_ref[...]) + finish(0, None) + vectors_ref[0:1, :]
+    normed, inverse_one, hidden = norm_forward(mid, vectors_ref[1:2, :], vectors_ref[2:3, :])
+    normed_one[...] = normed
+    own_hidden[...] = hidden
+    hidden_ref[0] = short(hidden)
+    spread(0, hidden_ref)
+
+    units = up_ref.shape[1]
+    step = min(units, 512)
+    for i in range(wides):
+        arrive(0, hidden_ref, i)
+        rows = pair(hidden_ref, i)
+        for c in range(0, units, step):
+            at = slice(c, c + step)
+            pre = dot(rows, up_ref[:, at]) + bias_ref[:, at]
+            phi = 0.5 + 0.5 * lax.erf(pre * math.sqrt(0.5))
+            act = short(pre * phi)
+            bend = phi + pre * jnp.exp(-0.5 * pre * pre) * (1.0 / math.sqrt(2.0 * math.pi))
+            for r, part in ((i, slice(0, share)), (wides + i, slice(share, 2 * share))):
+                act_ref[r, :, at] = act[part]
+                slope[r, :, at] = bend[part]
+        keep(1, i, dot(pair(act_ref, i), down_ref[...]))
+    summed = own_hidden[...] + finish(1, None) + vectors_ref[3:4, :]
+    gain_two = vectors_ref[4:5, :]
+    normed, inverse_two, result = norm_forward(summed, gain_two, vectors_ref[5:6, :])
+    result_ref[...] = short(result)
+    upstream = wide(upstream_ref[...]) * valid_ref[...]
+    grad_z = norm_backward(upstream, normed, inverse_two, gain_two)
+    own_grad_z[...] = grad_z
+    grad_z_ref[0] = short(grad_z)
+    spread(1, grad_z_ref)
+    vector_own[...] = jnp.zeros_like(vector_own)
+    vector_own[3:4, :] = sums(grad_z)
+    vector_own[4:5, :] = sums(upstream * normed)
+    vector_own[5:6, :] = sums(upstream)
+
+    for i in range(wides):
+        arrive(1, grad_z_ref, i)
+        rows = pair(grad_z_ref, i)
+        for c in range(0, units, step):
+            at = slice(c, c + step)
+            grad = dot_nt(rows, down_ref[at, :])
+            for r, part in ((i, slice(0, share)), (wides + i, slice(share, 2 * share))):
+                grad_pre_ref[r, :, at] = short(grad[part] * slope[r, :, at])
+        keep(2, i, dot_nt(pair(grad_pre_ref, i), up_ref[...]))
+
+    def every(ref, at):
+        return jnp.concatenate([ref[r, :, at] for r in range(teams)], 0)
+
+    def down_filler():
+        def one(k, carry):
+            at = pl.ds(pl.multiple_of(k * 128, 128), 128)
+            grad_down_ref[at, :] = short(mm_tn(every(act_ref, at), every(grad_z_ref, slice(None))))
+            return carry
+
+        lax.fori_loop(0, units // 128, one, 0)
+
+    grad_hidden = own_grad_z[...] + finish(2, down_filler)
+    grad_mid = norm_backward(grad_hidden, normed_one[...], inverse_one, vectors_ref[1:2, :])
+    own_grad_mid_ref[...] = grad_mid
+    grad_mid_ref[0] = short(grad_mid)
+    spread(2, grad_mid_ref)
+    vector_own[0:1, :] = sums(grad_mid)
+    vector_own[1:2, :] = sums(grad_hidden * normed_one[...])
+    vector_own[2:3, :] = sums(grad_hidden)
+
+    def to_team(hop):
+        return remote(
+            vector_own, vector_got.at[hop], vector_sems, (hop,), (index, (team + hop) % teams)
+        )
+
+    for hop in range(1, teams):
+        start(to_team(hop))
+
+    def up_filler(k, carry):
+        at = pl.ds(pl.multiple_of(k * 128, 128), 128)
+        grad_up_ref[at, :] = short(mm_tn(every(hidden_ref, at), every(grad_pre_ref, slice(None))))
+        return carry
+
+    lax.fori_loop(0, hidden_ref.shape[2] // 128, up_filler, 0)
+    for i in range(wides):
+        arrive(2, grad_mid_ref, i)
+    total = vector_own[...]
+    for hop in range(1, teams):
+        to_team(hop).wait_recv()
+        total = total + vector_got[hop]
+    vector_sum_ref[...] = total
+    for one in sent:
+        one.wait_send()
+
+
+def middle(context, x_own, w_out, w_up, w_down, bias_up, vectors, upstream, valid):
+    teams, share, width = context.shape
+    model, units = w_up.shape
+    wides = teams // 2
+    dma = pltpu.SemaphoreType.DMA
+    vmem = pl.BlockSpec(memory_space=pltpu.VMEM)
+    rows = jax.ShapeDtypeStruct((teams, share, model), bf16)
+    inner = jax.ShapeDtypeStruct((teams, share, units), bf16)
+    own = pltpu.VMEM((share, model), f32)
+    return pl.pallas_call(
+        middle_kernel,
+        name="middle",
+        out_shape=(
+            rows,
+            inner,
+            rows,
+            inner,
+            rows,
+            jax.ShapeDtypeStruct((share, model), f32),
+            jax.ShapeDtypeStruct((share, model), bf16),
+            jax.ShapeDtypeStruct((8, model), f32),
+            jax.ShapeDtypeStruct((units, model), bf16),
+            jax.ShapeDtypeStruct((model, units), bf16),
+        ),
+        in_specs=[vmem] * 9,
+        out_specs=[vmem] * 10,
+        scratch_shapes=[
+            pltpu.VMEM((teams, share, units), f32),
+            pltpu.VMEM((wides, share, model), f32),
+            pltpu.VMEM((3, wides, share, model), bf16),
+            pltpu.VMEM((3, wides, share, model), bf16),
+            pltpu.VMEM((3, wides - 1, share, model), bf16),
+            pltpu.VMEM((3, wides - 1, share, model), bf16),
+            own,
+            own,
+            own,
+            own,
+            pltpu.VMEM((8, model), f32),
+            pltpu.VMEM((teams, 8, model), f32),
+            dma((2, 3, wides)),
+            dma((2, 3, wides - 1)),
+            dma((2, 3, wides - 1)),
+            dma((2, 3, wides)),
+            dma((2, teams)),
+        ],
+        compiler_params=pltpu.CompilerParams(
+            collective_id=1, has_side_effects=True, vmem_limit_bytes=48 * 2**20
+        ),
+        cost_estimate=pl.CostEstimate(
+            flops=12 * teams * share * model * units,
+            bytes_accessed=8 * model * units,
+            transcendentals=0,
+        ),
+    )(context, x_own, w_out, w_up, w_down, bias_up.reshape(1, units), vectors, upstream, valid)
+
+
+def polar_kernel(block, m_ref, o_ref, x_ref, gram_ref, low_ref, mix_ref):
     teams, size, width = m_ref.shape
     keep = o_ref.shape[1]
-    blocks = size // block
+    bits = 256
 
     def rows(i):
-        return pl.ds(pl.multiple_of(i * block, block), block)
+        return pl.ds(pl.multiple_of(i * bits, bits), bits)
+
+    def columns(j):
+        return pl.ds(pl.multiple_of(j * block, block), block)
 
     def norm_step(i, total):
         for r in range(teams):
@@ -526,7 +909,7 @@
             total = total + jnp.sum(part * part, axis=0, keepdims=True)
         return total
 
-    total = lax.fori_loop(0, blocks, norm_step, jnp.zeros((1, width), f32))
+    total = lax.fori_loop(0, size // bits, norm_step, jnp.zeros((1, width), f32))
     scale = lax.rsqrt(jnp.sum(total, axis=1, keepdims=True) + 1e-07)
 
     def scale_step(i, carry):
@@ -534,161 +917,185 @@
             x_ref[0, rows(i), r * width : (r + 1) * width] = short(wide(m_ref[r, rows(i), :]) * scale)
         return carry
 
-    lax.fori_loop(0, blocks, scale_step, 0)
-
-    def sweep(now, last):
+    lax.fori_loop(0, size // bits, scale_step, 0)
+
+    def sweep(k, carry):
+        now = k % 2
         x = x_ref.at[now]
 
-        def gram_step(i, carry):
-            gram = dot_nt(x[rows(i), :], x[...])
-            gram_ref[rows(i), :] = gram
-            low_ref[rows(i), :] = short(gram)
+        def gram_step(j, carry):
+            gram = dot_nt(x[...], x[columns(j), :])
+            gram_ref[:, columns(j)] = gram
+            low_ref[:, columns(j)] = short(gram)
             return carry
 
-        lax.fori_loop(0, blocks, gram_step, 0)
-
-        def mix_step(i, carry):
-            mixing = coef_two * gram_ref[rows(i), :] + coef_three * dot(low_ref[rows(i), :], low_ref[...])
-            if last:
-                o_ref[rows(i), :] = short(coef_one * wide(x[rows(i), :keep]) + dot(short(mixing), x[:, :keep]))
-            else:
-                x_ref[1 - now, rows(i), :] = short(coef_one * wide(x[rows(i), :]) + dot(short(mixing), x[...]))
+        def mix_step(j, carry):
+            power = dot(low_ref[...], low_ref[:, columns(j)])
+            mix_ref[:, columns(j)] = short(coef_two * gram_ref[:, columns(j)] + coef_three * power)
             return carry
 
-        lax.fori_loop(0, blocks, mix_step, 0)
-
-    def two(k, carry):
-        sweep(0, False)
-        sweep(1, False)
+        def next_step(j, carry):
+            mixed = dot(mix_ref[...], x[:, columns(j)])
+            x_ref[1 - now, :, columns(j)] = short(coef_one * wide(x[:, columns(j)]) + mixed)
+            return carry
+
+        lax.fori_loop(0, size // block, gram_step, 0)
+        lax.fori_loop(0, size // block, mix_step, 0)
+        lax.fori_loop(0, jnp.where(k < 4, size // block, -(-keep // block)), next_step, 0)
         return carry
 
-    lax.fori_loop(0, 2, two, 0)
-    sweep(0, True)
-
-def polar_columns(matrix):
-    teams, size, width = matrix.shape
+    lax.fori_loop(0, 5, sweep, 0)
+    o_ref[...] = x_ref[1, :, :keep]
+
+
+def factor_kernel(block, g_ref, o_ref, current_ref, poly_ref, half_ref, factor_ref):
+    size = poly_ref.shape[0]
+    tile = g_ref.shape[1]
+    tiles = size // tile
+    keep = o_ref.shape[1]
+    first = lax.axis_index("tensor") * keep
+    eye = lax.broadcasted_iota(jnp.int32, (tile, tile), 0) == lax.broadcasted_iota(
+        jnp.int32, (tile, tile), 1
+    )
+    trace = jnp.zeros((1, 1), f32)
+    for k, (i, j) in enumerate(tile_pairs(tiles)):
+        if i == j:
+            diagonal = jnp.where(eye, g_ref[k], 0.0)
+            trace = trace + jnp.sum(jnp.sum(diagonal, axis=0, keepdims=True), axis=1, keepdims=True)
+    scale = lax.rsqrt(trace + 1e-07)
+    scale_two = scale * scale
+
+    def store(slot, rows, columns, value):
+        high = short(value)
+        current_ref[slot, 0, rows, columns] = high
+        current_ref[slot, 1, rows, columns] = short(value - wide(high))
+
+    def span(i):
+        return slice(i * tile, (i + 1) * tile)
+
+    for k, (i, j) in enumerate(tile_pairs(tiles)):
+        part = g_ref[k] * scale_two
+        store(0, span(i), span(j), part)
+        if i != j:
+            store(0, span(j), span(i), part.T)
+
+    def cols(j):
+        return pl.ds(pl.multiple_of(j * block, block), block)
+
+    def sweep(k, exact, last):
+        now = k % 2
+        high_ref, low_ref = current_ref.at[now, 0], current_ref.at[now, 1]
+
+        def poly_step(j, carry):
+            power = dot(high_ref[...], high_ref[:, cols(j)])
+            if not exact:
+                power = power + dot(high_ref[...], low_ref[:, cols(j)])
+            r = lax.broadcasted_iota(jnp.int32, (size, block), 0)
+            c = lax.broadcasted_iota(jnp.int32, (size, block), 1) + j * block
+            present = wide(high_ref[:, cols(j)]) + wide(low_ref[:, cols(j)])
+            poly = coef_two * present + coef_three * power
+            poly_ref[:, cols(j)] = short(poly + jnp.where(r == c, coef_one, 0.0))
+            return carry
+
+        def half_step(j, carry):
+            half = dot(poly_ref[...], high_ref[:, cols(j)])
+            if exact:
+                half = half + dot(poly_ref[...], low_ref[:, cols(j)])
+            high = short(half)
+            half_ref[0, :, cols(j)] = high
+            if exact:
+                half_ref[1, :, cols(j)] = short(half - wide(high))
+            return carry
+
+        def next_step(j, carry):
+            new = dot(half_ref[0], poly_ref[:, cols(j)])
+            if exact:
+                new = new + dot(half_ref[1], poly_ref[:, cols(j)])
+            store(1 - now, slice(None), cols(j), new)
+            return carry
+
+        lax.fori_loop(0, size // block, poly_step, 0)
+        if not last:
+            lax.fori_loop(0, size // block, half_step, 0)
+            lax.fori_loop(0, size // block, next_step, 0)
+
+    def exact_sweep(k, carry):
+        sweep(k, True, False)
+
+        @pl.when(k == 0)
+        def _():
+            factor_ref[...] = poly_ref[:, pl.ds(pl.multiple_of(first, 128), keep)]
+
+        @pl.when(k > 0)
+        def _():
+            factor_ref[...] = short(dot(poly_ref[...], factor_ref[...]))
+
+        return carry
+
+    def plain_sweep(k, carry):
+        sweep(k, False, False)
+        factor_ref[...] = short(dot(poly_ref[...], factor_ref[...]))
+        return carry
+
+    lax.fori_loop(0, 2, exact_sweep, 0)
+    lax.fori_loop(2, 4, plain_sweep, 0)
+    sweep(4, False, True)
+    o_ref[...] = short(dot(poly_ref[...], factor_ref[...]) * scale)
+
+
+def step_kernel(
+    block,
+    square_ref,
+    tiles_ref,
+    o_ref,
+    x_ref,
+    gram_ref,
+    low_ref,
+    mix_ref,
+    current_ref,
+    poly_ref,
+    half_ref,
+    factor_ref,
+):
+    index = lax.axis_index("dp")
+
+    @pl.when(index < 4)
+    def _():
+        polar_kernel(block, square_ref, o_ref, x_ref, gram_ref, low_ref, mix_ref)
+
+    @pl.when(jnp.logical_or(index == 4, index == 5))
+    def _():
+        factor_kernel(block, tiles_ref, o_ref, current_ref, poly_ref, half_ref, factor_ref)
+
+    @pl.when(index > 5)
+    def _():
+        o_ref[...] = jnp.zeros_like(o_ref)
+
+
+def orthogonal_columns(square, tiles):
+    teams, size, width = square.shape
+    vmem = pl.BlockSpec(memory_space=pltpu.VMEM)
     return pl.pallas_call(
-        functools.partial(polar_kernel, 512),
-        name="polar",
+        functools.partial(step_kernel, 512),
+        name="orthogonal_columns",
         out_shape=jax.ShapeDtypeStruct((size, width), bf16),
-        in_specs=[pl.BlockSpec(memory_space=pltpu.VMEM)],
-        out_specs=pl.BlockSpec(memory_space=pltpu.VMEM),
+        in_specs=[vmem] * 2,
+        out_specs=vmem,
         scratch_shapes=[
             pltpu.VMEM((2, size, teams * width), bf16),
             pltpu.VMEM((size, size), f32),
             pltpu.VMEM((size, size), bf16),
+            pltpu.VMEM((size, size), bf16),
+            pltpu.VMEM((2, 2, size, size), bf16),
+            pltpu.VMEM((size, size), bf16),
+            pltpu.VMEM((2, size, size), bf16),
+            pltpu.VMEM((size, width), bf16),
         ],
-        compiler_params=pltpu.CompilerParams(vmem_limit_bytes=32 * 2**20),
-    )(matrix)
-
-
-def factor_kernel(block, g_ref, o_ref, cur_ref, high_ref, low_ref, poly_ref, factor_ref):
-    tile = g_ref.shape[1]
-    tiles = cur_ref.shape[1] // tile
-    size = cur_ref.shape[1]
-    blocks = size // block
-    keep = o_ref.shape[1]
-    first = lax.axis_index("tensor") * keep
-    k = 0
-    trace = jnp.zeros((1, 1), f32)
-    eye = (lax.broadcasted_iota(jnp.int32, (tile, tile), 0) == lax.broadcasted_iota(jnp.int32, (tile, tile), 1))
-    for i in range(tiles):
-        for j in range(i, tiles):
-            part = g_ref[k]
-            cur_ref[0, i*tile:(i+1)*tile, j*tile:(j+1)*tile] = part
-            if i != j:
-                cur_ref[0, j*tile:(j+1)*tile, i*tile:(i+1)*tile] = part.T
-            else:
-                diag = jnp.where(eye, part, 0.0)
-                trace = trace + jnp.sum(jnp.sum(diag, axis=0, keepdims=True), axis=1, keepdims=True)
-            k += 1
-    scale = lax.rsqrt(trace + 1e-07)
-    scale_two = scale * scale
-
-    def rows(i):
-        return pl.ds(pl.multiple_of(i * block, block), block)
-
-    def scale_step(i, carry):
-        cur_ref[0, rows(i), :] = cur_ref[0, rows(i), :] * scale_two
-        return carry
-
-    lax.fori_loop(0, blocks, scale_step, 0)
-
-    def sweep(k, exact, finer):
-        now = k % 2
-        cur = cur_ref.at[now]
-
-        def split_step(i, carry):
-            value = cur[rows(i), :]
-            high = short(value)
-            high_ref[rows(i), :] = high
-            if exact or finer:
-                low_ref[rows(i), :] = short(value - wide(high))
-            return carry
-
-        lax.fori_loop(0, blocks, split_step, 0)
-
-        def poly_step(i, carry):
-            r = lax.broadcasted_iota(jnp.int32, (block, size), 0) + i * block
-            c = lax.broadcasted_iota(jnp.int32, (block, size), 1)
-            power = dot(high_ref[rows(i), :], high_ref[...])
-            if finer:
-                power = power + dot(high_ref[rows(i), :], low_ref[...])
-            poly = coef_two * cur[rows(i), :] + coef_three * power
-            poly = poly + jnp.where(r == c, coef_one, 0.0)
-            poly_ref[rows(i), :] = short(poly)
-            return carry
-
-        lax.fori_loop(0, blocks, poly_step, 0)
-
-        def next_step(i, carry):
-            half = dot(poly_ref[rows(i), :], high_ref[...])
-            if exact:
-                half = half + dot(poly_ref[rows(i), :], low_ref[...])
-            half_high = short(half)
-            new = dot(half_high, poly_ref[...])
-            if exact:
-                new = new + dot(short(half - wide(half_high)), poly_ref[...])
-            cur_ref[1 - now, rows(i), :] = new
-            return carry
-
-        if k < 4:
-            lax.fori_loop(0, blocks, next_step, 0)
-
-        def factor_step(i, carry):
-            if k == 0:
-                columns = pl.ds(pl.multiple_of(first, 128), keep)
-                factor_ref[0, rows(i), :] = poly_ref[rows(i), columns]
-            else:
-                before = factor_ref[1 - now]
-                new = dot(poly_ref[rows(i), :], before)
-                if k < 4:
-                    factor_ref[now, rows(i), :] = short(new)
-                else:
-                    o_ref[rows(i), :] = short(new * scale)
-            return carry
-
-        lax.fori_loop(0, blocks, factor_step, 0)
-
-    for k in range(5):
-        sweep(k, k < 2, k > 2)
-
-def factor_columns(tiles, size, keep):
-    return pl.pallas_call(
-        functools.partial(factor_kernel, 512),
-        name="factor",
-        out_shape=jax.ShapeDtypeStruct((size, keep), bf16),
-        in_specs=[pl.BlockSpec(memory_space=pltpu.VMEM)],
-        out_specs=pl.BlockSpec(memory_space=pltpu.VMEM),
-        scratch_shapes=[
-            pltpu.VMEM((2, size, size), f32),
-            pltpu.VMEM((size, size), bf16),
-            pltpu.VMEM((size, size), bf16),
-            pltpu.VMEM((size, size), bf16),
-            pltpu.VMEM((2, size, keep), bf16),
-        ],
-        compiler_params=pltpu.CompilerParams(vmem_limit_bytes=40 * 2**20),
-    )(tiles)
+        compiler_params=pltpu.CompilerParams(vmem_limit_bytes=48 * 2**20),
+        cost_estimate=pl.CostEstimate(
+            flops=40 * size**3, bytes_accessed=8 * size * size, transcendentals=0
+        ),
+    )(square, tiles)
 
 
 def body(
@@ -753,21 +1160,8 @@
             pieces += [ring_core.send(p, -hop) for p in line]
         return pieces
 
-    def spread_rows(piece):
-        return jnp.concatenate(spread_list(piece), 0)
-
     def spread_columns(piece):
         return to_given(jnp.concatenate(spread_list(piece), 1), piece.shape[1], 1)
-
-    def reduce_rows(partial):
-        block = wides * share
-        held = partial[:block]
-        for hop in range(1, cores):
-            held = held + wide(core_ring.send(short(partial[hop * block : (hop + 1) * block]), hop))
-        total = held[(wides - 1) * share :]
-        for i in range(wides - 2, -1, -1):
-            total = held[i * share : (i + 1) * share] + wide(x_ring.send(short(total), 1))
-        return total
 
     def own_rows(value):
         return cut(value, team, share, 0)
@@ -805,29 +1199,21 @@
     valid_own = own_rows((slots < end_all).astype(f32))
     segments = to_relative(segments, share)
 
-    def fetch(rows):
-        sent = short(mm(choose, cut(rows, team, width, 1))).reshape(groups, per_peer, width)
-        got = lax.all_to_all(sent, "dp", split_axis=0, concat_axis=0, tiled=True)
-        return got.reshape(count, width)
-
-    def give_back(rows):
-        parts = len(rows)
-        both = jnp.concatenate([r.reshape(share, teams, width) for r in rows], 2)
-        columns = lax.all_to_all(
-            both.reshape(share, teams * parts * width), "tensor", split_axis=1, concat_axis=0, tiled=True
-        )
-        got = lax.all_to_all(
-            columns.reshape(groups, per_peer, parts * width), "dp", split_axis=0, concat_axis=0, tiled=True
-        )
-        pieces = spread_list(short(mm_tn(choose, got.reshape(count, parts * width))))
-        return [
-            to_given(jnp.concatenate([p[:, k * width : (k + 1) * width] for p in pieces], 1), width, 1)
-            for k in range(parts)
-        ]
-
-    packed_x = to_relative(spread_columns(fetch(tokens)), share)
-    grad_rows = lax.all_to_all(
-        fetch(cotangent), "tensor", split_axis=0, concat_axis=1, tiled=True
+    own_columns = jnp.concatenate([cut(tokens, team, width, 1), cut(cotangent, team, width, 1)], 1)
+    sent = short(mm(choose, own_columns)).reshape(groups, per_peer, 2 * width)
+    got = lax.all_to_all(sent, "dp", split_axis=0, concat_axis=0, tiled=True)
+    got = got.reshape(count, 2 * width)
+
+    packed_x = to_relative(spread_columns(got[:, :width]), share)
+    turns = []
+    for hop in range(teams):
+        block = cut(got[:, width:], (team + hop) % teams, share, 0)
+        if hop > 0:
+            block = lax.ppermute(block, "tensor", [(i, (i + hop) % teams) for i in range(teams)])
+        turns.append(block)
+    turns = jnp.concatenate(turns, 1)
+    grad_rows = jnp.concatenate(
+        [cut(turns, (team - other) % teams, width, 1) for other in range(teams)], 1
     )
 
     wqkv_low = short(w_qkv)
@@ -848,43 +1234,31 @@
     context = short(
         jnp.einsum("hqk,khd->qhd", probs_low, values, preferred_element_type=f32)
     ).reshape(count, width)
-    mid = wide(packed_x[:share]) + reduce_rows(mm(context, wout_low)) + vectors[0]
-    normed_one, inverse_one, hidden = norm_forward(mid, vectors[1], vectors[2])
-    hidden_low = spread_rows(short(hidden))
-    pre_act = mm(hidden_low, wup_low) + bias_up
-    phi = 0.5 * lax.erfc(-pre_act * math.sqrt(0.5))
-    act_low = short(pre_act * phi)
-    slope = phi + pre_act * jnp.exp(-0.5 * pre_act * pre_act) * (1.0 / math.sqrt(2.0 * math.pi))
-    normed_two, inverse_two, result = norm_forward(
-        hidden + reduce_rows(mm(act_low, wdown_low)) + vectors[3], vectors[4], vectors[5]
-    )
-
-    grad_result = wide(grad_rows) * valid_own[:, None]
-    grad_z = norm_backward(grad_result, normed_two, inverse_two, vectors[4])
-    grad_z_low = spread_rows(short(grad_z))
-    grad_pre = short(mm_nt(grad_z_low, wdown_low) * slope)
-    grad_hidden = grad_z + reduce_rows(mm_nt(grad_pre, wup_low))
-    grad_down = short(mm_tn(act_low, grad_z_low))
-    grad_up = short(mm_tn(hidden_low, grad_pre))
-    grad_bias_up = jnp.sum(grad_pre, axis=0, dtype=f32)
-    grad_mid = norm_backward(grad_hidden, normed_one, inverse_one, vectors[1])
-    vector_part = jnp.stack(
-        [
-            jnp.sum(grad_mid, axis=0),
-            jnp.sum(grad_hidden * normed_one, axis=0),
-            jnp.sum(grad_hidden, axis=0),
-            jnp.sum(grad_z, axis=0),
-            jnp.sum(grad_result * normed_two, axis=0),
-            jnp.sum(grad_result, axis=0),
-        ]
-    )
-    extra = 16
-    joined = jnp.concatenate(
-        [short(grad_mid), short(vector_part), jnp.zeros((extra - 6, D), bf16)], 0
-    )
-    pieces = spread_list(joined)
-    grad_mid_low = jnp.concatenate([p[:share] for p in pieces], 0)
-    vector_part = sum(wide(p[share : share + 6]) for p in pieces)
+    (
+        hidden_low,
+        act_low,
+        grad_z_low,
+        grad_pre,
+        grad_mid_low,
+        grad_mid,
+        result,
+        vector_part,
+        grad_down,
+        grad_up,
+    ) = middle(
+        context.reshape(teams, share, width),
+        packed_x[:share],
+        wout_low,
+        wup_low,
+        wdown_low,
+        bias_up,
+        vectors,
+        grad_rows,
+        valid_own[:, None],
+    )
+    grad_bias_up = jnp.sum(grad_pre, axis=(0, 1), dtype=f32)
+    grad_mid_low = grad_mid_low.reshape(count, D)
+    vector_part = vector_part[:6]
     grad_out_t = short(mm_tn(grad_mid_low, context))
     grad_context = short(mm_nt(grad_mid_low, wout_low)).reshape(count, heads, HEAD)
     grad_probs = jnp.einsum("qhd,khd->hqk", grad_context, values, preferred_element_type=f32)
@@ -920,9 +1294,21 @@
     )
     rows_small = -(-small.size // (16 * columns)) * 16
     small = jnp.pad(short(small), (0, rows_small * columns - small.size)).reshape(rows_small, columns)
-    down_sum, up_sum, qkvo_sum, small_sum, square, gram_tiles = sums_over_dp(
-        inner, grad_down, grad_up, grad_qkvo, small, (mom_qkv, mom_out, mom_up, mom_down)
-    )
+    down_sum, up_sum, qkvo_sum, small_sum, square, gram_tiles, given = sums_over_dp(
+        inner,
+        grad_down,
+        grad_up,
+        grad_qkvo,
+        small,
+        short(input_part).reshape(teams, groups // teams, per_peer, D),
+        grad_mid.reshape(groups // teams, per_peer, D),
+        result.reshape(groups // teams, per_peer, D),
+        (mom_qkv, mom_out, mom_up, mom_down),
+    )
+    pieces = spread_list(short(mm_tn(choose, given.reshape(count, 2 * width))))
+    output = to_given(jnp.concatenate([p[:, :width] for p in pieces], 1), width, 1)
+    grad_tokens = wide(to_given(jnp.concatenate([p[:, width:] for p in pieces], 1), width, 1))
+
     qkvo_sum = wide(qkvo_sum)
     small_sum = small_sum.reshape(-1)
     gradients = (
@@ -941,21 +1327,7 @@
 
     up_low, down_low = short(moments[2]), short(moments[3])
 
-    def no_work(square, blocks):
-        return jnp.zeros((D, width), bf16)
-
-    def square_work(square, blocks):
-        return polar_columns(square)
-
-    def gram_work(square, blocks):
-        return factor_columns(blocks, D, width)
-
-    stepped = lax.switch(
-        (group >= 4).astype(jnp.int32) + (group >= 6).astype(jnp.int32),
-        [square_work, gram_work, no_work],
-        square,
-        gram_tiles,
-    )
+    stepped = orthogonal_columns(square, gram_tiles)
     dp_rows = D // groups
     steps = lax.all_to_all(
         stepped.reshape(groups, dp_rows, width), "dp", split_axis=0, concat_axis=0, tiled=True
@@ -977,10 +1349,6 @@
     for param, moment in zip((bias_qv, bias_up, vectors), moments[4:]):
         masters.append(param - rate_vector * moment)
 
-    output, grad_tokens = give_back(
-        [short(result), short(grad_mid + reduce_rows(input_part))]
-    )
-    grad_tokens = wide(grad_tokens)
     return (output, grad_tokens, *gradients, *moments, *masters)
 
 

time: 499 us -> 430 us (0.86)
  Pallas kernels: 196 us -> 262 us
  waiting for transfers between devices: 64.4 us -> 17.9 us
  starting transfers between devices: 84.7 us -> 38.7 us
  matrix products: 63.4 us -> 38.8 us
  loops' own time: 6.31 us -> 0 us
  other arithmetic: 44 us -> 38.4 us
    pallas_call x1 -> x2, Pallas kernels: 36.4 us -> 103 us  [the longest x1 64.8 us: middle(): pl.pallas_call(middle_kernel, name='middle', out_shape=(rows, inner, rows...]
    ppermute x26 -> x9, waiting for transfers between devices: 46.1 us -> 4.49 us  [send(): return lax.ppermute(value, self.axes, pairs)]
    ppermute x26 -> x9, starting transfers between devices: 35.4 us -> 5.19 us  [send(): return lax.ppermute(value, self.axes, pairs)]
    all_to_all x5 -> x1, starting transfers between devices: 25.9 us -> 6.38 us  [body(): got = lax.all_to_all(sent, 'dp', split_axis=0, concat_axis=0, tiled=True)]
    dot_general x10 -> x6, matrix products: 21.7 us -> 6.66 us  [mm(): return jnp.dot(short(left), short(right), preferred_element_type=f32)]
    another operation x1 -> x0, loops' own time: 6.31 us -> none  [body(): lax.switch((group >= 4).astype(jnp.int32) + (group >= 6).astype(jnp.int32...]
    dot_general x5 -> x3, matrix products: 10.8 us -> 5.84 us  [mm_tn(): lax.dot_general(short(left), short(right), (((0,), (0,)), ((), ())), pref...]
    all_to_all x5 -> x1, waiting for transfers between devices: 18.3 us -> 13.4 us  [body(): got = lax.all_to_all(sent, 'dp', split_axis=0, concat_axis=0, tiled=True)]
  transfers between devices with their start and end apart: 32 -> 14, of which waited for: 19 -> 4; matrix products, arithmetic and copies ran while one was open for 15% -> 9% of each run, Pallas kernels for 40% -> 9%
where the time goes in v3:
time: 430 us; the launch traced here: 426 us
  Pallas kernels  262 us (61%)
  matrix products  38.8 us (9%)
  starting transfers between devices  38.7 us (9%)
  other arithmetic  38.4 us (9%)
  local copies, waits for them, and re-layouts  27 us (6%)
  waiting for transfers between devices  17.9 us (4%)
    pallas_call x1, Pallas kernels, sums_over_dp(): pl.pallas_call(functools.partial(sum_kernel, inner, tile), name='sums_ove...  158 us
    pallas_call x1, Pallas kernels, middle(): pl.pallas_call(middle_kernel, name='middle', out_shape=(rows, inner, rows...  64.8 us
    pallas_call x1, Pallas kernels, orthogonal_columns(): pl.pallas_call(functools.partial(step_kernel, 512), name='orthogonal_colu...  38.6 us
    all_to_all x1, starting transfers between devices, body(): lax.all_to_all(stepped.reshape(groups, dp_rows, width), 'dp', split_axis=...  22.9 us
    unnamed x81, local copies, waits for them, and re-layouts  16.9 us
    all_to_all x1, waiting for transfers between devices, body(): got = lax.all_to_all(sent, 'dp', split_axis=0, concat_axis=0, tiled=True)  13.4 us
    add x4, other arithmetic, body(): momentum_decay * old + grad  13.3 us
  transfers between devices with their start and end apart: 14, of which 4 were waited for; matrix products, arithmetic and copies ran while one was open for 9% of the time, Pallas kernels for 9%

profile of v3, /device:TPU:1, one launch (start us, length us, event | category | flops | bytes accessed | tf_op | source)
XLA Modules:
  0.0 426.2 jit_solution(10408805585583785416)
XLA Ops:
  2.1 1.4 fusion.79
  7.1 1.1 constant_dynamic-slice_fusion.29
  8.3 1.5 fusion.16
  9.8 6.4 %all-to-all-start = ((bf16[8,72,512]{2,1,0:T(8,128)(2,1)}), bf16[8,72,512]{2,1,0:T(8,128)(2,1)S(1)}, u32[]{:S(2)}, u32[]{:S(2)}) async-start(bf16[8,72,512]{2,1,0:T(8,128)(2,1)} %bitcast), calls=%async_computation | async-start | bytes 1179648 | tf_op jit(solution)/shard_map/all_to_all | solution.py:1204
  17.4 13.4 %all-to-all-done = bf16[8,72,512]{2,1,0:T(8,128)(2,1)S(1)} async-done(((bf16[8,72,512]{2,1,0:T(8,128)(2,1)}), bf16[8,72,512]{2,1,0:T(8,128)(2,1)S(1)}, u32[]{:S(2)}, u32[]{:S(2)}) %all-to-all-start) | async-done | bytes 589856 | tf_op jit(solution)/shard_map/all_to_all | solution.py:1204
  30.9 1.3 collective-permute-start
  33.2 2.4 collective-permute-start.5
  35.9 1.5 collective-permute-start.3
  38.2 1.3 copy.91
  39.5 3.3 convert_element_type.134
  42.9 1.6 convert_element_type.145.up_ref
  44.5 1.3 copy-done.12
  45.8 1.6 convert_element_type.146.down_ref
  49.7 1.1 pad_maximum_fusion.2
  51.3 1.4 copy-done.9
  53.9 1.6 fusion.38
  55.9 4.8 %fusion.80 = (f32[4,576]{1,0:T(4,128)S(1)}, f32[4,576,576]{1,2,0:T(8,128)}) fusion(pred[576,576]{0,1:T(8,128)(4,1)S(1)} %copy-done.21, bf16[576,4,64]{0,2,1:T(8,128)(2,1)S(1)} %bitcast.98, bf16[576,4,64]{0,2,1:T(8,128)(2,1)S(1)} %bitcast.102), kind=kOutput, calls=%fused_computation.167 | convolution fusion | flops 175178304 | bytes 6239232 | tf_op jit(solution)/shard_map/sub | solution.py:1231
  60.7 3.4 fusion.32
  64.8 64.8 %middle.1 = (bf16[4,144,1024]{2,1,0:T(8,128)(2,1)}, bf16[4,144,1024]{2,1,0:T(8,128)(2,1)}, bf16[4,144,1024]{2,1,0:T(8,128)(2,1)}, bf16[4,144,1024]{2,1,0:T(8,128...) custom-call(bf16[4,144,256]{2,1,0:T(8,128)(2,1)S(1)} %copy.83.contex, ...), custom_call_target="tpu_custom_call" | custom-call | flops 7247757312 | bytes 8388608 | tf_op jit(solution)/shard_map/middle/pallas_call | solution.py:848
  129.6 1.8 convolution_convert_fusion.2
  131.6 4.5 %bitcast_reduce_fusion = (bf16[4,64]{1,0:T(4,128)(2,1)S(1)}, bf16[4,64,576]{2,1,0:T(8,128)(2,1)}) fusion(bf16[576,4,64]{0,2,1:T(8,128)(2,1)S(1)} %bitcast.113, f32[4,576,576]{1,2,0:T(8,128)} %get-tuple-element.193, f32[4,576]{1,0:T(4,128)S(1)} %get-tuple-element.192), kind=kOutput, calls=%fused_computation.85 | convolution fusion | flops 172818176 | bytes 5907968 | tf_op jit(solution)/shard_map/hqk,qhd->khd/dot_general | solution.py:1268
  136.1 3.8 multiply_reduce_fusion
  142.7 2.7 convolution_convert_fusion.1
  145.6 1.6 reduce.4
  147.3 1.6 fusion.54
  150.1 1.5 convolution_convert_fusion
  151.6 1.6 pad_maximum_fusion.1.qkvo_ref
  153.2 1.6 add_convert_fusion
  154.8 158.4 %sums_over_dp.1 = (bf16[1024,1024]{1,0:T(8,128)(2,1)}, bf16[1024,1024]{1,0:T(8,128)(2,1)}, bf16[1024,1024]{1,0:T(8,128)(2,1)}, f32[16,1024]{1,0:T(8,128)S(1)}, b...) custom-call(bf16[1024,1024]{1,0:T(8,128)(2,1)} %get-tuple-element.37.down_ref, ...), custom_call_target="tpu_custom_call" | custom-call | flops 3145728 | bytes 12582912 | tf_op jit(solution)/shard_map/sums_over_dp/pallas_call | solution.py:553
  313.2 1.7 fusion.17
  316.8 1.7 copy-done.2
  318.5 1.6 copy-done.3
  320.1 38.6 %orthogonal_columns.1 = bf16[1024,256]{1,0:T(8,128)(2,1)} custom-call(bf16[4,1024,256]{2,1,0:T(8,128)(2,1)S(1)} %copy-done.3, f32[10,256,256]{2,1,0:T(8,128)S(1)} %copy-done.2), custom_call_target="tpu_custom_call" | custom-call | flops 42949672960 | bytes 8388608 | tf_op jit(solution)/shard_map/orthogonal_columns/pallas_call | solution.py:1078
  358.7 22.9 %all-to-all-start.1 = ((bf16[8,128,256]{2,1,0:T(8,128)(2,1)}), bf16[8,128,256]{2,1,0:T(8,128)(2,1)S(1)}, u32[]{:S(2)}, u32[]{:S(2)}) async-start(bf16[8,128,256]{2,1,0:T(8,128)(2,1)} %bitcast.36), calls=%async_computation.1 | async-start | bytes 1048576 | tf_op jit(solution)/shard_map/all_to_all | solution.py:1332
  385.5 4.9 %multiply_add_fusion.1 = (f32[1024,1024]{1,0:T(8,128)}, f32[1024,1024]{1,0:T(8,128)}) fusion(f32[1024,1024]{1,0:T(8,128)S(1)} %copy-done.4, bf16[1024,1024]{1,0:T(8,128)(2,1)S(1)} %copy-done.16), kind=kLoop, calls=%fused_computation.7 | loop fusion | flops 3145728 | bytes 14680064 | tf_op jit(solution)/shard_map/add | solution.py:1325
  390.4 4.9 %multiply_add_fusion = (f32[1024,1024]{1,0:T(8,128)}, f32[1024,1024]{1,0:T(8,128)}) fusion(f32[1024,1024]{1,0:T(8,128)S(1)} %copy-done.5, bf16[1024,1024]{1,0:T(8,128)(2,1)S(1)} %copy-done.15), kind=kLoop, calls=%fused_computation.6 | loop fusion | flops 3145728 | bytes 14680064 | tf_op jit(solution)/shard_map/add | solution.py:1325
  395.2 3.4 multiply_add_fusion.2
  399.8 1.3 copy.94
  401.1 1.3 copy.93
  402.4 1.1 fusion.72
  406.5 3.8 collective-permute-done.9
  410.3 1.3 collective-permute-start.11
  411.5 1.8 multiply_subtract_fusion
  416.2 1.8 copy-done.6
  418.0 2.5 fusion.21
  420.5 2.6 fusion.27
  423.0 1.2 pad_maximum_fusion.6
  424.2 1.7 maximum_convert_fusion
  (166 shorter events, 28.3 us)
Async XLA Ops:
  8.2 23.9 %copy-start.32 = (f32[2,256]{1,0:T(2,128)S(1)}, f32[2,256]{1,0:T(2,128)}, u32[]{:S(2)}) copy-start(f32[2,256]{1,0:T(2,128)} %param.26) | copy-start | bytes 6148
  8.3 24.2 %copy-start.18 = (f32[256,1024]{1,0:T(8,128)S(1)}, f32[256,1024]{1,0:T(8,128)}, u32[]{:S(2)}) copy-start(f32[256,1024]{1,0:T(8,128)} %param.23) | copy-start | bytes 3145732
  9.8 21.1 %all-to-all-start = ((bf16[8,72,512]{2,1,0:T(8,128)(2,1)}), bf16[8,72,512]{2,1,0:T(8,128)(2,1)S(1)}, u32[]{:S(2)}, u32[]{:S(2)}) async-start(bf16[8,72,512]{2,1,0:T(8,128)(2,1)} %bitcast), calls=%async_computation | async-start | bytes 1179648 | tf_op jit(solution)/shard_map/all_to_all | solution.py:1204
  16.4 21.8 %copy-start.13 = (f32[256,1024]{1,0:T(8,128)S(1)}, f32[256,1024]{1,0:T(8,128)}, u32[]{:S(2)}) copy-start(f32[256,1024]{1,0:T(8,128)} %mom_out_ref.1) | copy-start | bytes 3145732
  30.9 16.6 %collective-permute-start = (bf16[576,256]{1,0:T(8,128)(2,1)S(1)}, bf16[576,256]{1,0:T(8,128)(2,1)}, u32[]{:S(2)}, u32[]{:S(2)}) collective-permute-start(bf16[576,256]{1,0:T(8,128)(2,1)S(1)} %get-tuple-element.166), channel_id=1, source_target_pairs={{0,2},{1,3},{2,0},{3,1},{4,6},{5,7},{6,4},{7,5},{8,10},{9,11},{10,... | collective-permute-start | bytes 884744 | tf_op jit(solution)/shard_map/ppermute | solution.py:81
  33.2 14.8 %collective-permute-start.5 = (bf16[144,256]{1,0:T(8,128)(2,1)}, bf16[144,256]{1,0:T(8,128)(2,1)S(1)}, u32[]{:S(2)}, u32[]{:S(2)}) collective-permute-start(bf16[144,256]{1,0:T(8,128)(2,1)} %get-tuple-element.176), channel_id=1, source_target_pairs={{0,3},{1,0},{2,1},{3,2},{4,7},{5,4},{6,5},{7,6},{8,11},{9,8},{10,9... | collective-permute-start | bytes 221192 | tf_op jit(solution)/shard_map/ppermute | solution.py:1212
  35.6 12.3 %collective-permute-start.4 = (bf16[144,256]{1,0:T(8,128)(2,1)S(1)}, bf16[144,256]{1,0:T(8,128)(2,1)S(1)}, u32[]{:S(2)}, u32[]{:S(2)}) collective-permute-start(bf16[144,256]{1,0:T(8,128)(2,1)S(1)} %get-tuple-element.177), channel_id=1, source_target_pairs={{0,2},{1,3},{2,0},{3,1},{4,6},{5,7},{6,4},{7,5},{8,10},{9,11},{10,... | collective-permute-start | bytes 221192 | tf_op jit(solution)/shard_map/ppermute | solution.py:1212
  35.9 12.1 %collective-permute-start.3 = (bf16[144,256]{1,0:T(8,128)(2,1)S(1)}, bf16[144,256]{1,0:T(8,128)(2,1)}, u32[]{:S(2)}, u32[]{:S(2)}) collective-permute-start(bf16[144,256]{1,0:T(8,128)(2,1)S(1)} %get-tuple-element.178), channel_id=1, source_target_pairs={{0,1},{1,2},{2,3},{3,0},{4,5},{5,6},{6,7},{7,4},{8,9},{9,10},{10,1... | collective-permute-start | bytes 221192 | tf_op jit(solution)/shard_map/ppermute | solution.py:1212
  39.5 3.3 copy-start.11
  42.9 2.9 copy-start.12
  47.4 1.9 collective-permute-start.1
  47.5 2.2 collective-permute-start.2
  51.0 1.7 copy-start.9
  51.2 2.6 copy-start.25
  51.2 2.6 copy-start.27
  51.2 2.6 copy-start.29
  53.9 2.0 copy-start.21
  55.7 5.0 %copy-start.23 = (bf16[576,256]{0,1:T(8,128)(2,1)}, bf16[576,256]{0,1:T(8,128)(2,1)S(1)}, u32[]{:S(2)}) copy-start(bf16[576,256]{0,1:T(8,128)(2,1)S(1)} %copy.79) | copy-start | bytes 884740
  60.7 4.1 copy-start
  60.7 4.1 copy-start.1
  131.6 4.6 %copy-start.24 = (bf16[576,256]{0,1:T(8,128)(2,1)S(1)}, bf16[576,256]{0,1:T(8,128)(2,1)}, u32[]{:S(2)}) copy-start(bf16[576,256]{0,1:T(8,128)(2,1)} %copy-done.23) | copy-start | bytes 884740
  131.6 8.4 %slice-start = ((s8[5898240]{0:T(1024)(128)(4,1)}), s8[4194304]{0:T(1024)(128)(4,1)S(1)}, s32[]{:S(2)}) async-start(s8[5898240]{0:T(1024)(128)(4,1)} %bitcast.92), calls=%async_computation.2 | async-start | bytes 8388608
  136.1 3.8 slice-start.1
  145.4 3.5 copy-start.10
  148.9 1.2 copy-start.30
  150.1 1.5 copy-start.20
  313.2 2.9 copy-start.31
  314.9 89.3 %collective-permute-start.7 = (bf16[576,512]{1,0:T(8,128)(2,1)}, bf16[576,512]{1,0:T(8,128)(2,1)}, u32[]{:S(2)}, u32[]{:S(2)}) collective-permute-start(bf16[576,512]{1,0:T(8,128)(2,1)} %fusion.17), channel_id=1, source_target_pairs={{0,1},{1,0},{2,3},{3,2},{4,5},{5,4},{6,7},{7,6},{8,9},{9,8},{10,11... | collective-permute-start | bytes 1769480 | tf_op jit(solution)/shard_map/ppermute | solution.py:81
  315.3 88.3 %collective-permute-start.6 = (bf16[576,512]{1,0:T(8,128)(2,1)}, bf16[576,512]{1,0:T(8,128)(2,1)S(1)}, u32[]{:S(2)}, u32[]{:S(2)}) collective-permute-start(bf16[576,512]{1,0:T(8,128)(2,1)} %fusion.17), channel_id=1, source_target_pairs={{0,2},{1,3},{2,0},{3,1},{4,6},{5,7},{6,4},{7,5},{8,10},{9,11},{10,... | collective-permute-start | bytes 1769480 | tf_op jit(solution)/shard_map/ppermute | solution.py:81
  316.8 1.7 copy-start.2
  318.5 1.6 copy-start.3
  320.1 61.5 %copy-start.17 = (bf16[1024,1024]{1,0:T(8,128)(2,1)S(1)}, bf16[1024,1024]{1,0:T(8,128)(2,1)}, u32[]{:S(2)}) copy-start(bf16[1024,1024]{1,0:T(8,128)(2,1)} %get-tuple-element.45) | copy-start | bytes 6291460
  358.7 46.7 %all-to-all-start.1 = ((bf16[8,128,256]{2,1,0:T(8,128)(2,1)}), bf16[8,128,256]{2,1,0:T(8,128)(2,1)S(1)}, u32[]{:S(2)}, u32[]{:S(2)}) async-start(bf16[8,128,256]{2,1,0:T(8,128)(2,1)} %bitcast.36), calls=%async_computation.1 | async-start | bytes 1048576 | tf_op jit(solution)/shard_map/all_to_all | solution.py:1332
  382.1 1.2 copy-start.14
  382.1 2.5 copy-start.4
  383.3 2.2 copy-start.16
  385.5 4.9 %copy-start.5 = (f32[1024,1024]{1,0:T(8,128)S(1)}, f32[1024,1024]{1,0:T(8,128)}, u32[]{:S(2)}) copy-start(f32[1024,1024]{1,0:T(8,128)} %mom_down_ref.1) | copy-start | bytes 12582916
  385.5 4.9 %copy-start.15 = (bf16[1024,1024]{1,0:T(8,128)(2,1)S(1)}, bf16[1024,1024]{1,0:T(8,128)(2,1)}, u32[]{:S(2)}) copy-start(bf16[1024,1024]{1,0:T(8,128)(2,1)} %get-tuple-element.47) | copy-start | bytes 6291460
  390.4 4.9 %copy-start.8 = (f32[3,1024,256]{2,1,0:T(8,128)S(1)}, f32[3,1024,256]{2,1,0:T(8,128)}, u32[]{:S(2)}) copy-start(f32[3,1024,256]{2,1,0:T(8,128)} %mom_qkv_ref.1) | copy-start | bytes 9437188
  395.2 3.4 copy-start.33
  395.2 4.0 copy-start.34
  402.4 3.3 copy-start.19
  403.6 10.8 %collective-permute-start.8 = (bf16[576,512]{1,0:T(8,128)(2,1)S(1)}, bf16[576,512]{1,0:T(8,128)(2,1)}, u32[]{:S(2)}, u32[]{:S(2)}) collective-permute-start(bf16[576,512]{1,0:T(8,128)(2,1)S(1)} %collective-permute-done.6), channel_id=1, source_target_pairs={{0,1},{1,0},{2,3},{3,2},{4,5},{5,4},{6,7},{7,6},{8,9},{9,8},{10,11... | collective-permute-start | bytes 1769480 | tf_op jit(solution)/shard_map/ppermute | solution.py:81
  405.4 8.0 %collective-permute-start.10 = (bf16[256,256]{1,0:T(8,128)(2,1)S(1)}, bf16[256,256]{1,0:T(8,128)(2,1)S(1)}, u32[]{:S(2)}, u32[]{:S(2)}) collective-permute-start(bf16[256,256]{1,0:T(8,128)(2,1)S(1)} %bitcast.104), channel_id=1, source_target_pairs={{0,1},{1,0},{2,3},{3,2},{4,5},{5,4},{6,7},{7,6},{8,9},{9,8},{10,11... | collective-permute-start | bytes 393224 | tf_op jit(solution)/shard_map/ppermute | solution.py:81
  405.5 4.8 %collective-permute-start.9 = (bf16[256,256]{1,0:T(8,128)(2,1)S(1)}, bf16[256,256]{1,0:T(8,128)(2,1)}, u32[]{:S(2)}, u32[]{:S(2)}) collective-permute-start(bf16[256,256]{1,0:T(8,128)(2,1)S(1)} %bitcast.105), channel_id=1, source_target_pairs={{0,2},{1,3},{2,0},{3,1},{4,6},{5,7},{6,4},{7,5},{8,10},{9,11},{10,... | collective-permute-start | bytes 393224 | tf_op jit(solution)/shard_map/ppermute | solution.py:81
  410.3 3.1 collective-permute-start.11
  415.8 2.2 copy-start.6
  418.0 2.5 copy-start.7
  (3 other events, 3.2 us)

commit v4 on v3

--- a/solution.py
+++ b/solution.py
@@ -982,13 +982,13 @@
     def cols(j):
         return pl.ds(pl.multiple_of(j * block, block), block)
 
-    def sweep(k, exact, last):
+    def sweep(k, exact, exact_next, last):
         now = k % 2
         high_ref, low_ref = current_ref.at[now, 0], current_ref.at[now, 1]
 
         def poly_step(j, carry):
             power = dot(high_ref[...], high_ref[:, cols(j)])
-            if not exact:
+            if last:
                 power = power + dot(high_ref[...], low_ref[:, cols(j)])
             r = lax.broadcasted_iota(jnp.int32, (size, block), 0)
             c = lax.broadcasted_iota(jnp.int32, (size, block), 1) + j * block
@@ -1003,13 +1003,13 @@
                 half = half + dot(poly_ref[...], low_ref[:, cols(j)])
             high = short(half)
             half_ref[0, :, cols(j)] = high
-            if exact:
+            if exact_next:
                 half_ref[1, :, cols(j)] = short(half - wide(high))
             return carry
 
         def next_step(j, carry):
             new = dot(half_ref[0], poly_ref[:, cols(j)])
-            if exact:
+            if exact_next:
                 new = new + dot(half_ref[1], poly_ref[:, cols(j)])
             store(1 - now, slice(None), cols(j), new)
             return carry
@@ -1019,27 +1019,17 @@
             lax.fori_loop(0, size // block, half_step, 0)
             lax.fori_loop(0, size // block, next_step, 0)
 
-    def exact_sweep(k, carry):
-        sweep(k, True, False)
-
-        @pl.when(k == 0)
-        def _():
-            factor_ref[...] = poly_ref[:, pl.ds(pl.multiple_of(first, 128), keep)]
-
-        @pl.when(k > 0)
-        def _():
-            factor_ref[...] = short(dot(poly_ref[...], factor_ref[...]))
-
-        return carry
-
     def plain_sweep(k, carry):
-        sweep(k, False, False)
+        sweep(k, False, False, False)
         factor_ref[...] = short(dot(poly_ref[...], factor_ref[...]))
         return carry
 
-    lax.fori_loop(0, 2, exact_sweep, 0)
+    sweep(0, True, True, False)
+    factor_ref[...] = poly_ref[:, pl.ds(pl.multiple_of(first, 128), keep)]
+    sweep(1, True, False, False)
+    factor_ref[...] = short(dot(poly_ref[...], factor_ref[...]))
     lax.fori_loop(2, 4, plain_sweep, 0)
-    sweep(4, False, True)
+    sweep(4, False, False, True)
     o_ref[...] = short(dot(poly_ref[...], factor_ref[...]) * scale)
 
 

time: 430 us -> 423 us (0.984)
  starting transfers between devices: 38.7 us -> 27.4 us
  Pallas kernels: 262 us -> 267 us
    all_to_all x1, starting transfers between devices: 22.9 us -> 11.6 us  [body(): lax.all_to_all(stepped.reshape(groups, dp_rows, width), 'dp', split_axis=...]
    pallas_call x1, Pallas kernels: 38.6 us -> 43.4 us  [orthogonal_columns(): pl.pallas_call(functools.partial(step_kernel, 512), name='orthogonal_colu...]
  transfers between devices with their start and end apart: 14 -> 14, of which waited for: 4 -> 4; matrix products, arithmetic and copies ran while one was open for 9% -> 9% of each run, Pallas kernels for 9% -> 10%
where the time goes in v4:
time: 423 us; the launch traced here: 420 us
  Pallas kernels  267 us (63%)
  matrix products  38.8 us (9%)
  other arithmetic  38.4 us (9%)
  starting transfers between devices  27.4 us (6%)
  local copies, waits for them, and re-layouts  27 us (6%)
  waiting for transfers between devices  17.9 us (4%)
    pallas_call x1, Pallas kernels, sums_over_dp(): pl.pallas_call(functools.partial(sum_kernel, inner, tile), name='sums_ove...  158 us
    pallas_call x1, Pallas kernels, middle(): pl.pallas_call(middle_kernel, name='middle', out_shape=(rows, inner, rows...  64.8 us
    pallas_call x1, Pallas kernels, orthogonal_columns(): pl.pallas_call(functools.partial(step_kernel, 512), name='orthogonal_colu...  43.4 us
    unnamed x81, local copies, waits for them, and re-layouts  16.9 us
    all_to_all x1, waiting for transfers between devices, body(): got = lax.all_to_all(sent, 'dp', split_axis=0, concat_axis=0, tiled=True)  13.4 us
    add x4, other arithmetic, body(): momentum_decay * old + grad  13.3 us
    all_to_all x1, starting transfers between devices, body(): lax.all_to_all(stepped.reshape(groups, dp_rows, width), 'dp', split_axis=...  11.6 us
  transfers between devices with their start and end apart: 14, of which 4 were waited for; matrix products, arithmetic and copies ran while one was open for 9% of the time, Pallas kernels for 10%

profile of v4, /device:TPU:1, one launch (start us, length us, event | category | flops | bytes accessed | tf_op | source)
XLA Modules:
  0.0 419.7 jit_solution(14636687411117371762)
XLA Ops:
  2.1 1.4 fusion.79
  7.1 1.1 constant_dynamic-slice_fusion.29
  8.3 1.5 fusion.16
  9.8 6.4 %all-to-all-start = ((bf16[8,72,512]{2,1,0:T(8,128)(2,1)}), bf16[8,72,512]{2,1,0:T(8,128)(2,1)S(1)}, u32[]{:S(2)}, u32[]{:S(2)}) async-start(bf16[8,72,512]{2,1,0:T(8,128)(2,1)} %bitcast), calls=%async_computation | async-start | bytes 1179648 | tf_op jit(solution)/shard_map/all_to_all | solution.py:1194
  17.4 13.4 %all-to-all-done = bf16[8,72,512]{2,1,0:T(8,128)(2,1)S(1)} async-done(((bf16[8,72,512]{2,1,0:T(8,128)(2,1)}), bf16[8,72,512]{2,1,0:T(8,128)(2,1)S(1)}, u32[]{:S(2)}, u32[]{:S(2)}) %all-to-all-start) | async-done | bytes 589856 | tf_op jit(solution)/shard_map/all_to_all | solution.py:1194
  30.9 1.3 collective-permute-start
  33.2 2.4 collective-permute-start.5
  35.9 1.5 collective-permute-start.3
  38.2 1.3 copy.91
  39.5 3.3 convert_element_type.134
  42.9 1.6 convert_element_type.145.up_ref
  44.5 1.3 copy-done.12
  45.8 1.6 convert_element_type.146.down_ref
  49.7 1.1 pad_maximum_fusion.2
  51.3 1.4 copy-done.9
  53.9 1.6 fusion.38
  55.9 4.8 %fusion.80 = (f32[4,576]{1,0:T(4,128)S(1)}, f32[4,576,576]{1,2,0:T(8,128)}) fusion(pred[576,576]{0,1:T(8,128)(4,1)S(1)} %copy-done.21, bf16[576,4,64]{0,2,1:T(8,128)(2,1)S(1)} %bitcast.98, bf16[576,4,64]{0,2,1:T(8,128)(2,1)S(1)} %bitcast.102), kind=kOutput, calls=%fused_computation.167 | convolution fusion | flops 175178304 | bytes 6239232 | tf_op jit(solution)/shard_map/sub | solution.py:1221
  60.7 3.4 fusion.32
  64.8 64.8 %middle.1 = (bf16[4,144,1024]{2,1,0:T(8,128)(2,1)}, bf16[4,144,1024]{2,1,0:T(8,128)(2,1)}, bf16[4,144,1024]{2,1,0:T(8,128)(2,1)}, bf16[4,144,1024]{2,1,0:T(8,128...) custom-call(bf16[4,144,256]{2,1,0:T(8,128)(2,1)S(1)} %copy.83.contex, ...), custom_call_target="tpu_custom_call" | custom-call | flops 7247757312 | bytes 8388608 | tf_op jit(solution)/shard_map/middle/pallas_call | solution.py:848
  129.6 1.8 convolution_convert_fusion.2
  131.6 4.5 %bitcast_reduce_fusion = (bf16[4,64]{1,0:T(4,128)(2,1)S(1)}, bf16[4,64,576]{2,1,0:T(8,128)(2,1)}) fusion(bf16[576,4,64]{0,2,1:T(8,128)(2,1)S(1)} %bitcast.113, f32[4,576,576]{1,2,0:T(8,128)} %get-tuple-element.193, f32[4,576]{1,0:T(4,128)S(1)} %get-tuple-element.192), kind=kOutput, calls=%fused_computation.85 | convolution fusion | flops 172818176 | bytes 5907968 | tf_op jit(solution)/shard_map/hqk,qhd->khd/dot_general | solution.py:1258
  136.1 3.8 multiply_reduce_fusion
  142.7 2.7 convolution_convert_fusion.1
  145.6 1.6 reduce.4
  147.3 1.6 fusion.54
  150.1 1.5 convolution_convert_fusion
  151.6 1.6 pad_maximum_fusion.1.qkvo_ref
  153.2 1.6 add_convert_fusion
  154.8 158.4 %sums_over_dp.1 = (bf16[1024,1024]{1,0:T(8,128)(2,1)}, bf16[1024,1024]{1,0:T(8,128)(2,1)}, bf16[1024,1024]{1,0:T(8,128)(2,1)}, f32[16,1024]{1,0:T(8,128)S(1)}, b...) custom-call(bf16[1024,1024]{1,0:T(8,128)(2,1)} %get-tuple-element.37.down_ref, ...), custom_call_target="tpu_custom_call" | custom-call | flops 3145728 | bytes 12582912 | tf_op jit(solution)/shard_map/sums_over_dp/pallas_call | solution.py:553
  313.2 1.7 fusion.17
  316.8 1.7 copy-done.2
  318.5 1.6 copy-done.3
  320.1 43.4 %orthogonal_columns.1 = bf16[1024,256]{1,0:T(8,128)(2,1)} custom-call(bf16[4,1024,256]{2,1,0:T(8,128)(2,1)S(1)} %copy-done.3, f32[10,256,256]{2,1,0:T(8,128)S(1)} %copy-done.2), custom_call_target="tpu_custom_call" | custom-call | flops 42949672960 | bytes 8388608 | tf_op jit(solution)/shard_map/orthogonal_columns/pallas_call | solution.py:1068
  363.6 11.6 %all-to-all-start.1 = ((bf16[8,128,256]{2,1,0:T(8,128)(2,1)}), bf16[8,128,256]{2,1,0:T(8,128)(2,1)S(1)}, u32[]{:S(2)}, u32[]{:S(2)}) async-start(bf16[8,128,256]{2,1,0:T(8,128)(2,1)} %bitcast.36), calls=%async_computation.1 | async-start | bytes 1048576 | tf_op jit(solution)/shard_map/all_to_all | solution.py:1322
  379.0 4.9 %multiply_add_fusion.1 = (f32[1024,1024]{1,0:T(8,128)}, f32[1024,1024]{1,0:T(8,128)}) fusion(f32[1024,1024]{1,0:T(8,128)S(1)} %copy-done.4, bf16[1024,1024]{1,0:T(8,128)(2,1)S(1)} %copy-done.16), kind=kLoop, calls=%fused_computation.7 | loop fusion | flops 3145728 | bytes 14680064 | tf_op jit(solution)/shard_map/add | solution.py:1315
  383.9 4.9 %multiply_add_fusion = (f32[1024,1024]{1,0:T(8,128)}, f32[1024,1024]{1,0:T(8,128)}) fusion(f32[1024,1024]{1,0:T(8,128)S(1)} %copy-done.5, bf16[1024,1024]{1,0:T(8,128)(2,1)S(1)} %copy-done.15), kind=kLoop, calls=%fused_computation.6 | loop fusion | flops 3145728 | bytes 14680064 | tf_op jit(solution)/shard_map/add | solution.py:1315
  388.8 3.4 multiply_add_fusion.2
  393.4 1.3 copy.94
  394.7 1.3 copy.93
  396.0 1.1 fusion.72
  400.0 3.8 collective-permute-done.9
  403.8 1.3 collective-permute-start.11
  405.1 1.8 multiply_subtract_fusion
  409.8 1.8 copy-done.6
  411.6 2.5 fusion.21
  414.0 2.6 fusion.27
  416.6 1.2 pad_maximum_fusion.6
  417.8 1.7 maximum_convert_fusion
  (166 shorter events, 28.3 us)
Async XLA Ops:
  8.2 23.9 %copy-start.32 = (f32[2,256]{1,0:T(2,128)S(1)}, f32[2,256]{1,0:T(2,128)}, u32[]{:S(2)}) copy-start(f32[2,256]{1,0:T(2,128)} %param.26) | copy-start | bytes 6148
  8.3 24.2 %copy-start.18 = (f32[256,1024]{1,0:T(8,128)S(1)}, f32[256,1024]{1,0:T(8,128)}, u32[]{:S(2)}) copy-start(f32[256,1024]{1,0:T(8,128)} %param.23) | copy-start | bytes 3145732
  9.8 21.1 %all-to-all-start = ((bf16[8,72,512]{2,1,0:T(8,128)(2,1)}), bf16[8,72,512]{2,1,0:T(8,128)(2,1)S(1)}, u32[]{:S(2)}, u32[]{:S(2)}) async-start(bf16[8,72,512]{2,1,0:T(8,128)(2,1)} %bitcast), calls=%async_computation | async-start | bytes 1179648 | tf_op jit(solution)/shard_map/all_to_all | solution.py:1194
  16.4 21.8 %copy-start.13 = (f32[256,1024]{1,0:T(8,128)S(1)}, f32[256,1024]{1,0:T(8,128)}, u32[]{:S(2)}) copy-start(f32[256,1024]{1,0:T(8,128)} %mom_out_ref.1) | copy-start | bytes 3145732
  30.9 16.6 %collective-permute-start = (bf16[576,256]{1,0:T(8,128)(2,1)S(1)}, bf16[576,256]{1,0:T(8,128)(2,1)}, u32[]{:S(2)}, u32[]{:S(2)}) collective-permute-start(bf16[576,256]{1,0:T(8,128)(2,1)S(1)} %get-tuple-element.166), channel_id=1, source_target_pairs={{0,2},{1,3},{2,0},{3,1},{4,6},{5,7},{6,4},{7,5},{8,10},{9,11},{10,... | collective-permute-start | bytes 884744 | tf_op jit(solution)/shard_map/ppermute | solution.py:81
  33.2 14.8 %collective-permute-start.5 = (bf16[144,256]{1,0:T(8,128)(2,1)}, bf16[144,256]{1,0:T(8,128)(2,1)S(1)}, u32[]{:S(2)}, u32[]{:S(2)}) collective-permute-start(bf16[144,256]{1,0:T(8,128)(2,1)} %get-tuple-element.176), channel_id=1, source_target_pairs={{0,3},{1,0},{2,1},{3,2},{4,7},{5,4},{6,5},{7,6},{8,11},{9,8},{10,9... | collective-permute-start | bytes 221192 | tf_op jit(solution)/shard_map/ppermute | solution.py:1202
  35.6 12.3 %collective-permute-start.4 = (bf16[144,256]{1,0:T(8,128)(2,1)S(1)}, bf16[144,256]{1,0:T(8,128)(2,1)S(1)}, u32[]{:S(2)}, u32[]{:S(2)}) collective-permute-start(bf16[144,256]{1,0:T(8,128)(2,1)S(1)} %get-tuple-element.177), channel_id=1, source_target_pairs={{0,2},{1,3},{2,0},{3,1},{4,6},{5,7},{6,4},{7,5},{8,10},{9,11},{10,... | collective-permute-start | bytes 221192 | tf_op jit(solution)/shard_map/ppermute | solution.py:1202
  35.9 12.1 %collective-permute-start.3 = (bf16[144,256]{1,0:T(8,128)(2,1)S(1)}, bf16[144,256]{1,0:T(8,128)(2,1)}, u32[]{:S(2)}, u32[]{:S(2)}) collective-permute-start(bf16[144,256]{1,0:T(8,128)(2,1)S(1)} %get-tuple-element.178), channel_id=1, source_target_pairs={{0,1},{1,2},{2,3},{3,0},{4,5},{5,6},{6,7},{7,4},{8,9},{9,10},{10,1... | collective-permute-start | bytes 221192 | tf_op jit(solution)/shard_map/ppermute | solution.py:1202
  39.5 3.3 copy-start.11
  42.9 2.9 copy-start.12
  47.4 1.9 collective-permute-start.1
  47.5 2.2 collective-permute-start.2
  51.0 1.7 copy-start.9
  51.2 2.6 copy-start.25
  51.2 2.6 copy-start.27
  51.2 2.6 copy-start.29
  53.9 2.0 copy-start.21
  55.7 5.0 %copy-start.23 = (bf16[576,256]{0,1:T(8,128)(2,1)}, bf16[576,256]{0,1:T(8,128)(2,1)S(1)}, u32[]{:S(2)}) copy-start(bf16[576,256]{0,1:T(8,128)(2,1)S(1)} %copy.79) | copy-start | bytes 884740
  60.7 4.1 copy-start
  60.7 4.1 copy-start.1
  131.6 4.6 %copy-start.24 = (bf16[576,256]{0,1:T(8,128)(2,1)S(1)}, bf16[576,256]{0,1:T(8,128)(2,1)}, u32[]{:S(2)}) copy-start(bf16[576,256]{0,1:T(8,128)(2,1)} %copy-done.23) | copy-start | bytes 884740
  131.6 8.4 %slice-start = ((s8[5898240]{0:T(1024)(128)(4,1)}), s8[4194304]{0:T(1024)(128)(4,1)S(1)}, s32[]{:S(2)}) async-start(s8[5898240]{0:T(1024)(128)(4,1)} %bitcast.92), calls=%async_computation.2 | async-start | bytes 8388608
  136.1 3.8 slice-start.1
  145.4 3.5 copy-start.10
  148.9 1.2 copy-start.30
  150.1 1.5 copy-start.20
  313.2 2.9 copy-start.31
  314.9 82.9 %collective-permute-start.7 = (bf16[576,512]{1,0:T(8,128)(2,1)}, bf16[576,512]{1,0:T(8,128)(2,1)}, u32[]{:S(2)}, u32[]{:S(2)}) collective-permute-start(bf16[576,512]{1,0:T(8,128)(2,1)} %fusion.17), channel_id=1, source_target_pairs={{0,1},{1,0},{2,3},{3,2},{4,5},{5,4},{6,7},{7,6},{8,9},{9,8},{10,11... | collective-permute-start | bytes 1769480 | tf_op jit(solution)/shard_map/ppermute | solution.py:81
  315.3 81.8 %collective-permute-start.6 = (bf16[576,512]{1,0:T(8,128)(2,1)}, bf16[576,512]{1,0:T(8,128)(2,1)S(1)}, u32[]{:S(2)}, u32[]{:S(2)}) collective-permute-start(bf16[576,512]{1,0:T(8,128)(2,1)} %fusion.17), channel_id=1, source_target_pairs={{0,2},{1,3},{2,0},{3,1},{4,6},{5,7},{6,4},{7,5},{8,10},{9,11},{10,... | collective-permute-start | bytes 1769480 | tf_op jit(solution)/shard_map/ppermute | solution.py:81
  316.8 1.7 copy-start.2
  318.5 1.6 copy-start.3
  320.1 55.0 %copy-start.17 = (bf16[1024,1024]{1,0:T(8,128)(2,1)S(1)}, bf16[1024,1024]{1,0:T(8,128)(2,1)}, u32[]{:S(2)}) copy-start(bf16[1024,1024]{1,0:T(8,128)(2,1)} %get-tuple-element.45) | copy-start | bytes 6291460
  363.6 35.3 %all-to-all-start.1 = ((bf16[8,128,256]{2,1,0:T(8,128)(2,1)}), bf16[8,128,256]{2,1,0:T(8,128)(2,1)S(1)}, u32[]{:S(2)}, u32[]{:S(2)}) async-start(bf16[8,128,256]{2,1,0:T(8,128)(2,1)} %bitcast.36), calls=%async_computation.1 | async-start | bytes 1048576 | tf_op jit(solution)/shard_map/all_to_all | solution.py:1322
  375.6 1.2 copy-start.14
  375.6 2.5 copy-start.4
  376.9 2.2 copy-start.16
  379.0 4.9 %copy-start.5 = (f32[1024,1024]{1,0:T(8,128)S(1)}, f32[1024,1024]{1,0:T(8,128)}, u32[]{:S(2)}) copy-start(f32[1024,1024]{1,0:T(8,128)} %mom_down_ref.1) | copy-start | bytes 12582916
  379.0 4.9 %copy-start.15 = (bf16[1024,1024]{1,0:T(8,128)(2,1)S(1)}, bf16[1024,1024]{1,0:T(8,128)(2,1)}, u32[]{:S(2)}) copy-start(bf16[1024,1024]{1,0:T(8,128)(2,1)} %get-tuple-element.47) | copy-start | bytes 6291460
  383.9 4.9 %copy-start.8 = (f32[3,1024,256]{2,1,0:T(8,128)S(1)}, f32[3,1024,256]{2,1,0:T(8,128)}, u32[]{:S(2)}) copy-start(f32[3,1024,256]{2,1,0:T(8,128)} %mom_qkv_ref.1) | copy-start | bytes 9437188
  388.8 3.4 copy-start.33
  388.8 4.0 copy-start.34
  396.0 3.3 copy-start.19
  397.1 10.8 %collective-permute-start.8 = (bf16[576,512]{1,0:T(8,128)(2,1)S(1)}, bf16[576,512]{1,0:T(8,128)(2,1)}, u32[]{:S(2)}, u32[]{:S(2)}) collective-permute-start(bf16[576,512]{1,0:T(8,128)(2,1)S(1)} %collective-permute-done.6), channel_id=1, source_target_pairs={{0,1},{1,0},{2,3},{3,2},{4,5},{5,4},{6,7},{7,6},{8,9},{9,8},{10,11... | collective-permute-start | bytes 1769480 | tf_op jit(solution)/shard_map/ppermute | solution.py:81
  398.9 8.0 %collective-permute-start.10 = (bf16[256,256]{1,0:T(8,128)(2,1)S(1)}, bf16[256,256]{1,0:T(8,128)(2,1)S(1)}, u32[]{:S(2)}, u32[]{:S(2)}) collective-permute-start(bf16[256,256]{1,0:T(8,128)(2,1)S(1)} %bitcast.104), channel_id=1, source_target_pairs={{0,1},{1,0},{2,3},{3,2},{4,5},{5,4},{6,7},{7,6},{8,9},{9,8},{10,11... | collective-permute-start | bytes 393224 | tf_op jit(solution)/shard_map/ppermute | solution.py:81
  399.0 4.8 %collective-permute-start.9 = (bf16[256,256]{1,0:T(8,128)(2,1)S(1)}, bf16[256,256]{1,0:T(8,128)(2,1)}, u32[]{:S(2)}, u32[]{:S(2)}) collective-permute-start(bf16[256,256]{1,0:T(8,128)(2,1)S(1)} %bitcast.105), channel_id=1, source_target_pairs={{0,2},{1,3},{2,0},{3,1},{4,6},{5,7},{6,4},{7,5},{8,10},{9,11},{10,... | collective-permute-start | bytes 393224 | tf_op jit(solution)/shard_map/ppermute | solution.py:81
  403.8 3.1 collective-permute-start.11
  409.4 2.2 copy-start.6
  411.6 2.5 copy-start.7
  (3 other events, 3.2 us)

commit v5 on v4

--- a/solution.py
+++ b/solution.py
@@ -601,7 +601,7 @@
             dma((2, groups)),
         ],
         compiler_params=pltpu.CompilerParams(
-            collective_id=0, has_side_effects=True, vmem_limit_bytes=52 * 2**20
+            collective_id=0, has_side_effects=True, vmem_limit_bytes=31 * 2**20
         ),
         cost_estimate=pl.CostEstimate(
             flops=length, bytes_accessed=4 * length, transcendentals=0

time: 423 us -> 427 us (level)
  Pallas kernels: 267 us -> 254 us
  local copies, waits for them, and re-layouts: 27 us -> 36.8 us
  starting transfers between devices: 27.4 us -> 32.2 us
    pallas_call x1, Pallas kernels: 158 us -> 151 us  [sums_over_dp(): pl.pallas_call(functools.partial(sum_kernel, inner, tile), name='sums_ove...]
    unnamed x81 -> x115, local copies, waits for them, and re-layouts: 16.9 us -> 23.2 us
    pallas_call x1, Pallas kernels: 43.4 us -> 38.8 us  [orthogonal_columns(): pl.pallas_call(functools.partial(step_kernel, 512), name='orthogonal_colu...]
    all_to_all x1, starting transfers between devices: 11.6 us -> 16.2 us  [body(): lax.all_to_all(stepped.reshape(groups, dp_rows, width), 'dp', split_axis=...]
  transfers between devices with their start and end apart: 14 -> 14, of which waited for: 4 -> 2; matrix products, arithmetic and copies ran while one was open for 9% -> 10% of each run, Pallas kernels for 10% -> 9%
where the time goes in v5:
time: 427 us; the launch traced here: 423 us
  Pallas kernels  254 us (59%)
  matrix products  39.8 us (9%)
  other arithmetic  39.1 us (9%)
  local copies, waits for them, and re-layouts  36.8 us (9%)
  starting transfers between devices  32.2 us (8%)
  waiting for transfers between devices  17.1 us (4%)
    pallas_call x1, Pallas kernels, sums_over_dp(): pl.pallas_call(functools.partial(sum_kernel, inner, tile), name='sums_ove...  151 us
    pallas_call x1, Pallas kernels, middle(): pl.pallas_call(middle_kernel, name='middle', out_shape=(rows, inner, rows...  64.7 us
    pallas_call x1, Pallas kernels, orthogonal_columns(): pl.pallas_call(functools.partial(step_kernel, 512), name='orthogonal_colu...  38.8 us
    unnamed x115, local copies, waits for them, and re-layouts  23.2 us
    all_to_all x1, starting transfers between devices, body(): lax.all_to_all(stepped.reshape(groups, dp_rows, width), 'dp', split_axis=...  16.2 us
    add x4, other arithmetic, body(): momentum_decay * old + grad  14.3 us
    all_to_all x1, waiting for transfers between devices, body(): got = lax.all_to_all(sent, 'dp', split_axis=0, concat_axis=0, tiled=True)  14.2 us
    dot_general x5, matrix products, mm_nt(): lax.dot_general(short(left), short(right), (((1,), (1,)), ((), ())), pref...  9.43 us
  transfers between devices with their start and end apart: 14, of which 2 were waited for; matrix products, arithmetic and copies ran while one was open for 10% of the time, Pallas kernels for 9%

profile of v5, /device:TPU:1, one launch (start us, length us, event | category | flops | bytes accessed | tf_op | source)
XLA Modules:
  0.0 423.4 jit_solution(3951923906695152646)
XLA Ops:
  2.1 1.4 fusion.79
  8.3 1.5 fusion.16
  9.8 6.4 %all-to-all-start = ((bf16[8,72,512]{2,1,0:T(8,128)(2,1)}), bf16[8,72,512]{2,1,0:T(8,128)(2,1)S(1)}, u32[]{:S(2)}, u32[]{:S(2)}) async-start(bf16[8,72,512]{2,1,0:T(8,128)(2,1)} %bitcast), calls=%async_computation | async-start | bytes 1179648 | tf_op jit(solution)/shard_map/all_to_all | solution.py:1194
  16.7 14.2 %all-to-all-done = bf16[8,72,512]{2,1,0:T(8,128)(2,1)S(1)} async-done(((bf16[8,72,512]{2,1,0:T(8,128)(2,1)}), bf16[8,72,512]{2,1,0:T(8,128)(2,1)S(1)}, u32[]{:S(2)}, u32[]{:S(2)}) %all-to-all-start) | async-done | bytes 589856 | tf_op jit(solution)/shard_map/all_to_all | solution.py:1194
  32.4 1.3 convert_element_type.144.out_ref
  34.4 2.4 collective-permute-start.5
  37.1 1.6 collective-permute-start.3
  40.4 1.3 copy.91
  41.7 3.3 convert_element_type.134
  45.0 1.6 convert_element_type.145.up_ref
  47.9 1.6 convert_element_type.146.down_ref
  53.1 1.4 copy-done.20
  55.8 1.9 fusion.38
  58.8 4.8 %fusion.80 = (f32[4,576]{1,0:T(4,128)S(1)}, f32[4,576,576]{1,2,0:T(8,128)}) fusion(pred[576,576]{0,1:T(8,128)(4,1)S(1)} %broadcast_compare_fusion, bf16[576,4,64]{0,2,1:T(8,128)(2,1)S(1)} %bitcast.98, bf16[576,4,64]{0,2,1:T(8,128)(2,1)S(1)} %bitcast.102), kind=kOutput, calls=%fused_computation.167 | convolution fusion | flops 175178304 | bytes 6239232 | tf_op jit(solution)/shard_map/sub | solution.py:1221
  63.6 3.5 fusion.32
  67.8 64.7 %middle.1 = (bf16[4,144,1024]{2,1,0:T(8,128)(2,1)}, bf16[4,144,1024]{2,1,0:T(8,128)(2,1)}, bf16[4,144,1024]{2,1,0:T(8,128)(2,1)}, bf16[4,144,1024]{2,1,0:T(8,128...) custom-call(bf16[4,144,256]{2,1,0:T(8,128)(2,1)S(1)} %copy.83.contex, ...), custom_call_target="tpu_custom_call" | custom-call | flops 7247757312 | bytes 8388608 | tf_op jit(solution)/shard_map/middle/pallas_call | solution.py:848
  133.3 1.8 convolution_convert_fusion.2
  135.4 4.5 %bitcast_reduce_fusion = (bf16[4,64]{1,0:T(4,128)(2,1)S(1)}, bf16[4,64,576]{2,1,0:T(8,128)(2,1)}) fusion(bf16[576,4,64]{0,2,1:T(8,128)(2,1)S(1)} %bitcast.113, f32[4,576,576]{1,2,0:T(8,128)} %get-tuple-element.193, f32[4,576]{1,0:T(4,128)S(1)} %copy-done.45), kind=kOutput, calls=%fused_computation.85 | convolution fusion | flops 172818176 | bytes 5907968 | tf_op jit(solution)/shard_map/hqk,qhd->khd/dot_general | solution.py:1258
  139.9 3.8 multiply_reduce_fusion
  146.5 2.0 convolution_convert_fusion.1
  148.7 1.5 reduce.4
  150.2 1.6 fusion.54
  151.9 1.7 fusion.55
  153.6 1.5 convolution_convert_fusion
  155.4 1.8 add_convert_fusion
  157.9 150.9 %sums_over_dp.1 = (bf16[1024,1024]{1,0:T(8,128)(2,1)S(1)}, bf16[1024,1024]{1,0:T(8,128)(2,1)S(1)}, bf16[1024,1024]{1,0:T(8,128)(2,1)S(1)}, f32[16,1024]{1,0:T(8,...) custom-call(bf16[1024,1024]{1,0:T(8,128)(2,1)S(1)} %copy-done.1, ...), custom_call_target="tpu_custom_call" | custom-call | flops 3145728 | bytes 12582912 | tf_op jit(solution)/shard_map/sums_over_dp/pallas_call | solution.py:553
  308.8 1.3 copy-done.3
  310.1 1.3 copy-done.5
  311.5 1.5 copy-done.11
  313.0 1.3 copy-done.13
  314.3 1.7 fusion.17
  318.0 1.7 copy-done.12
  319.8 1.6 copy-done.14
  321.4 38.8 %orthogonal_columns.1 = bf16[1024,256]{1,0:T(8,128)(2,1)} custom-call(bf16[4,1024,256]{2,1,0:T(8,128)(2,1)S(1)} %copy-done.14, f32[10,256,256]{2,1,0:T(8,128)S(1)} %copy-done.12), custom_call_target="tpu_custom_call" | custom-call | flops 42949672960 | bytes 8388608 | tf_op jit(solution)/shard_map/orthogonal_columns/pallas_call | solution.py:1068
  360.2 16.2 %all-to-all-start.1 = ((bf16[8,128,256]{2,1,0:T(8,128)(2,1)}), bf16[8,128,256]{2,1,0:T(8,128)(2,1)}, u32[]{:S(2)}, u32[]{:S(2)}) async-start(bf16[8,128,256]{2,1,0:T(8,128)(2,1)} %bitcast.36), calls=%async_computation.1 | async-start | bytes 1048576 | tf_op jit(solution)/shard_map/all_to_all | solution.py:1322
  376.4 2.0 convert_element_type.165
  378.5 1.4 slice_bitcast_fusion
  382.5 4.9 %multiply_add_fusion.1 = (f32[1024,1024]{1,0:T(8,128)}, f32[1024,1024]{1,0:T(8,128)}) fusion(f32[1024,1024]{1,0:T(8,128)S(1)} %copy-done.15, bf16[1024,1024]{1,0:T(8,128)(2,1)S(1)} %copy-done.4), kind=kLoop, calls=%fused_computation.7 | loop fusion | flops 3145728 | bytes 14680064 | tf_op jit(solution)/shard_map/add | solution.py:1315
  387.4 4.9 %multiply_add_fusion = (f32[1024,1024]{1,0:T(8,128)}, f32[1024,1024]{1,0:T(8,128)}) fusion(f32[1024,1024]{1,0:T(8,128)S(1)} %copy-done.16, bf16[1024,1024]{1,0:T(8,128)(2,1)S(1)} %get-tuple-element.47), kind=kLoop, calls=%fused_computation.6 | loop fusion | flops 3145728 | bytes 14680064 | tf_op jit(solution)/shard_map/add | solution.py:1315
  392.3 3.4 multiply_add_fusion.2
  396.9 1.3 copy.94
  398.2 1.3 copy.93
  406.3 2.9 collective-permute-done.9
  410.5 1.8 multiply_subtract_fusion
  413.3 1.8 copy-done.17
  415.1 2.5 fusion.21
  417.5 2.6 fusion.27
  421.3 1.7 maximum_convert_fusion
  (200 shorter events, 37.6 us)
Async XLA Ops:
  7.1 2.6 copy-start.48
  8.3 23.9 %copy-start.46 = (f32[2,256]{1,0:T(2,128)S(1)}, f32[2,256]{1,0:T(2,128)}, u32[]{:S(2)}) copy-start(f32[2,256]{1,0:T(2,128)} %param.26) | copy-start | bytes 6148
  9.8 21.1 %all-to-all-start = ((bf16[8,72,512]{2,1,0:T(8,128)(2,1)}), bf16[8,72,512]{2,1,0:T(8,128)(2,1)S(1)}, u32[]{:S(2)}, u32[]{:S(2)}) async-start(bf16[8,72,512]{2,1,0:T(8,128)(2,1)} %bitcast), calls=%async_computation | async-start | bytes 1179648 | tf_op jit(solution)/shard_map/all_to_all | solution.py:1194
  16.4 24.0 %copy-start = (f32[256,1024]{1,0:T(8,128)S(1)}, f32[256,1024]{1,0:T(8,128)}, u32[]{:S(2)}) copy-start(f32[256,1024]{1,0:T(8,128)} %mom_out_ref.1) | copy-start | bytes 3145732
  30.9 18.7 %collective-permute-start = (bf16[576,256]{1,0:T(8,128)(2,1)S(1)}, bf16[576,256]{1,0:T(8,128)(2,1)S(1)}, u32[]{:S(2)}, u32[]{:S(2)}) collective-permute-start(bf16[576,256]{1,0:T(8,128)(2,1)S(1)} %get-tuple-element.166), channel_id=1, source_target_pairs={{0,2},{1,3},{2,0},{3,1},{4,6},{5,7},{6,4},{7,5},{8,10},{9,11},{10,... | collective-permute-start | bytes 884744 | tf_op jit(solution)/shard_map/ppermute | solution.py:81
  34.4 15.7 %collective-permute-start.5 = (bf16[144,256]{1,0:T(8,128)(2,1)}, bf16[144,256]{1,0:T(8,128)(2,1)S(1)}, u32[]{:S(2)}, u32[]{:S(2)}) collective-permute-start(bf16[144,256]{1,0:T(8,128)(2,1)} %get-tuple-element.176), channel_id=1, source_target_pairs={{0,3},{1,0},{2,1},{3,2},{4,7},{5,4},{6,5},{7,6},{8,11},{9,8},{10,9... | collective-permute-start | bytes 221192 | tf_op jit(solution)/shard_map/ppermute | solution.py:1202
  36.9 13.3 %collective-permute-start.4 = (bf16[144,256]{1,0:T(8,128)(2,1)S(1)}, bf16[144,256]{1,0:T(8,128)(2,1)S(1)}, u32[]{:S(2)}, u32[]{:S(2)}) collective-permute-start(bf16[144,256]{1,0:T(8,128)(2,1)S(1)} %get-tuple-element.177), channel_id=1, source_target_pairs={{0,2},{1,3},{2,0},{3,1},{4,6},{5,7},{6,4},{7,5},{8,10},{9,11},{10,... | collective-permute-start | bytes 221192 | tf_op jit(solution)/shard_map/ppermute | solution.py:1202
  37.1 13.0 %collective-permute-start.3 = (bf16[144,256]{1,0:T(8,128)(2,1)S(1)}, bf16[144,256]{1,0:T(8,128)(2,1)S(1)}, u32[]{:S(2)}, u32[]{:S(2)}) collective-permute-start(bf16[144,256]{1,0:T(8,128)(2,1)S(1)} %get-tuple-element.178), channel_id=1, source_target_pairs={{0,1},{1,2},{2,3},{3,0},{4,5},{5,6},{6,7},{7,4},{8,9},{9,10},{10,1... | collective-permute-start | bytes 221192 | tf_op jit(solution)/shard_map/ppermute | solution.py:1202
  41.7 3.3 copy-start.21
  45.0 2.9 copy-start.22
  49.6 2.9 collective-permute-start.1
  49.6 2.9 collective-permute-start.2
  53.1 1.9 copy-start.34
  53.1 1.9 copy-start.36
  53.1 1.9 copy-start.38
  55.8 3.0 copy-start.26
  58.8 4.8 %copy-start.28 = (bf16[576,256]{0,1:T(8,128)(2,1)}, bf16[576,256]{0,1:T(8,128)(2,1)S(1)}, u32[]{:S(2)}) copy-start(bf16[576,256]{0,1:T(8,128)(2,1)S(1)} %copy.81) | copy-start | bytes 884740
  63.6 3.5 copy-start.44
  63.6 4.2 copy-start.8
  63.6 4.2 copy-start.10
  133.3 2.0 copy-start.45
  135.3 4.6 %copy-start.33 = (bf16[576,256]{0,1:T(8,128)(2,1)S(1)}, bf16[576,256]{0,1:T(8,128)(2,1)}, u32[]{:S(2)}) copy-start(bf16[576,256]{0,1:T(8,128)(2,1)} %copy.79) | copy-start | bytes 884740
  135.4 8.4 %slice-start = ((s8[5898240]{0:T(1024)(128)(4,1)}), s8[4194304]{0:T(1024)(128)(4,1)S(1)}, s32[]{:S(2)}) async-start(s8[5898240]{0:T(1024)(128)(4,1)} %bitcast.93), calls=%async_computation.2 | async-start | bytes 8388608
  139.9 3.8 slice-start.1
  155.4 2.4 copy-start.2
  155.4 2.5 copy-start.7
  157.9 156.4 %copy-start.49 = (s32[576]{0:T(1024)S(1)}, s32[576]{0:T(1024)}, u32[]{:S(2)}) copy-start(s32[576]{0:T(1024)} %copy-done.48) | copy-start | bytes 6916
  314.3 3.1 copy-start.9
  314.3 3.1 copy-start.43
  316.0 86.4 %collective-permute-start.7 = (bf16[576,512]{1,0:T(8,128)(2,1)}, bf16[576,512]{1,0:T(8,128)(2,1)}, u32[]{:S(2)}, u32[]{:S(2)}) collective-permute-start(bf16[576,512]{1,0:T(8,128)(2,1)} %fusion.17), channel_id=1, source_target_pairs={{0,1},{1,0},{2,3},{3,2},{4,5},{5,4},{6,7},{7,6},{8,9},{9,8},{10,11... | collective-permute-start | bytes 1769480 | tf_op jit(solution)/shard_map/ppermute | solution.py:81
  316.4 84.3 %collective-permute-start.6 = (bf16[576,512]{1,0:T(8,128)(2,1)}, bf16[576,512]{1,0:T(8,128)(2,1)}, u32[]{:S(2)}, u32[]{:S(2)}) collective-permute-start(bf16[576,512]{1,0:T(8,128)(2,1)} %fusion.17), channel_id=1, source_target_pairs={{0,2},{1,3},{2,0},{3,1},{4,6},{5,7},{6,4},{7,5},{8,10},{9,11},{10,... | collective-permute-start | bytes 1769480 | tf_op jit(solution)/shard_map/ppermute | solution.py:81
  360.2 43.3 %all-to-all-start.1 = ((bf16[8,128,256]{2,1,0:T(8,128)(2,1)}), bf16[8,128,256]{2,1,0:T(8,128)(2,1)}, u32[]{:S(2)}, u32[]{:S(2)}) async-start(bf16[8,128,256]{2,1,0:T(8,128)(2,1)} %bitcast.36), calls=%async_computation.1 | async-start | bytes 1048576 | tf_op jit(solution)/shard_map/all_to_all | solution.py:1322
  378.4 3.3 copy-start.15
  379.8 2.7 copy-start.4
  382.5 4.9 %copy-start.16 = (f32[1024,1024]{1,0:T(8,128)S(1)}, f32[1024,1024]{1,0:T(8,128)}, u32[]{:S(2)}) copy-start(f32[1024,1024]{1,0:T(8,128)} %mom_down_ref.1) | copy-start | bytes 12582916
  387.4 4.9 %copy-start.19 = (f32[3,1024,256]{2,1,0:T(8,128)S(1)}, f32[3,1024,256]{2,1,0:T(8,128)}, u32[]{:S(2)}) copy-start(f32[3,1024,256]{2,1,0:T(8,128)} %mom_qkv_ref.1) | copy-start | bytes 9437188
  392.3 3.4 copy-start.50
  392.3 4.0 copy-start.47
  392.3 4.0 copy-start.51
  392.3 4.6 %copy-start.24 = (f32[256,1024]{0,1:T(8,128)S(1)}, f32[256,1024]{0,1:T(8,128)}, u32[]{:S(2)}) copy-start(f32[256,1024]{0,1:T(8,128)} %multiply_add_fusion.3) | copy-start | bytes 3145732
  395.7 2.5 copy-start.25
  399.5 5.1 %copy-start.30 = (f32[256,128]{0,1:T(8,128)S(1)}, f32[256,128]{0,1:T(8,128)}, u32[]{:S(2)}) copy-start(f32[256,128]{0,1:T(8,128)} %copy.102) | copy-start | bytes 393220
  400.7 11.8 %collective-permute-start.8 = (bf16[576,512]{1,0:T(8,128)(2,1)}, bf16[576,512]{1,0:T(8,128)(2,1)S(1)}, u32[]{:S(2)}, u32[]{:S(2)}) collective-permute-start(bf16[576,512]{1,0:T(8,128)(2,1)} %collective-permute-done.6), channel_id=1, source_target_pairs={{0,1},{1,0},{2,3},{3,2},{4,5},{5,4},{6,7},{7,6},{8,9},{9,8},{10,11... | collective-permute-start | bytes 1769480 | tf_op jit(solution)/shard_map/ppermute | solution.py:81
  404.4 7.9 %collective-permute-start.10 = (bf16[256,256]{1,0:T(8,128)(2,1)S(1)}, bf16[256,256]{1,0:T(8,128)(2,1)S(1)}, u32[]{:S(2)}, u32[]{:S(2)}) collective-permute-start(bf16[256,256]{1,0:T(8,128)(2,1)S(1)} %bitcast.104), channel_id=1, source_target_pairs={{0,1},{1,0},{2,3},{3,2},{4,5},{5,4},{6,7},{7,6},{8,9},{9,8},{10,11... | collective-permute-start | bytes 393224 | tf_op jit(solution)/shard_map/ppermute | solution.py:81
  404.5 4.7 %collective-permute-start.9 = (bf16[256,256]{1,0:T(8,128)(2,1)S(1)}, bf16[256,256]{1,0:T(8,128)(2,1)S(1)}, u32[]{:S(2)}, u32[]{:S(2)}) collective-permute-start(bf16[256,256]{1,0:T(8,128)(2,1)S(1)} %bitcast.105), channel_id=1, source_target_pairs={{0,2},{1,3},{2,0},{3,1},{4,6},{5,7},{6,4},{7,5},{8,10},{9,11},{10,... | collective-permute-start | bytes 393224 | tf_op jit(solution)/shard_map/ppermute | solution.py:81
  409.2 3.1 collective-permute-start.11
  412.9 2.2 copy-start.17
  415.1 2.5 copy-start.18
  (20 other events, 26.2 us)

commit v6 on v4

--- a/solution.py
+++ b/solution.py
@@ -637,6 +637,7 @@
     vector_sum_ref,
     grad_down_ref,
     grad_up_ref,
+    bias_sum_ref,
     slope,
     held,
     core_out,
@@ -787,8 +788,12 @@
         for c in range(0, units, step):
             at = slice(c, c + step)
             grad = dot_nt(rows, down_ref[at, :])
+            total = jnp.zeros((1, at.stop - at.start), f32)
             for r, part in ((i, slice(0, share)), (wides + i, slice(share, 2 * share))):
-                grad_pre_ref[r, :, at] = short(grad[part] * slope[r, :, at])
+                low = short(grad[part] * slope[r, :, at])
+                grad_pre_ref[r, :, at] = low
+                total = total + sums(wide(low))
+            bias_sum_ref[:, at] = total if i == 0 else bias_sum_ref[:, at] + total
         keep(2, i, dot_nt(pair(grad_pre_ref, i), up_ref[...]))
 
     def every(ref, at):
@@ -859,9 +864,10 @@
             jax.ShapeDtypeStruct((8, model), f32),
             jax.ShapeDtypeStruct((units, model), bf16),
             jax.ShapeDtypeStruct((model, units), bf16),
+            jax.ShapeDtypeStruct((1, units), f32),
         ),
         in_specs=[vmem] * 9,
-        out_specs=[vmem] * 10,
+        out_specs=[vmem] * 11,
         scratch_shapes=[
             pltpu.VMEM((teams, share, units), f32),
             pltpu.VMEM((wides, share, model), f32),
@@ -1159,14 +1165,21 @@
     position = jnp.arange(count, dtype=jnp.int32)
     peer = jnp.arange(groups, dtype=jnp.int32)
     packed = packing.reshape(groups, count)
-    source = packed // count
-    source_mine = lax.dynamic_index_in_dim(source, group, 0, keepdims=False)
-    masks = jnp.concatenate([source == group, source_mine[None, :] == peer[:, None]], 0)
+    mine_packed = lax.dynamic_index_in_dim(packed, group, 0, keepdims=False)
+    offset = packed - group * count
+    offset_mine = mine_packed[None, :] - peer[:, None] * count
+    masks = jnp.concatenate(
+        [
+            jnp.logical_and(offset >= 0, offset < count),
+            jnp.logical_and(offset_mine >= 0, offset_mine < count),
+        ],
+        0,
+    )
     before = (position[:, None] < position[None, :]).astype(bf16)
     rank = mm(masks.astype(bf16), before).astype(jnp.int32)
     key = jnp.where(masks, rank, -1)
     value = jnp.concatenate(
-        [packed % count, jnp.broadcast_to(position[None, :], (groups, count))], 0
+        [offset, jnp.broadcast_to(position[None, :], (groups, count))], 0
     )
     slot_in_message = jnp.arange(per_peer, dtype=jnp.int32)
     picked = jnp.sum(
@@ -1235,6 +1248,7 @@
         vector_part,
         grad_down,
         grad_up,
+        grad_bias_up,
     ) = middle(
         context.reshape(teams, share, width),
         packed_x[:share],
@@ -1246,7 +1260,7 @@
         grad_rows,
         valid_own[:, None],
     )
-    grad_bias_up = jnp.sum(grad_pre, axis=(0, 1), dtype=f32)
+    grad_bias_up = grad_bias_up[0]
     grad_mid_low = grad_mid_low.reshape(count, D)
     vector_part = vector_part[:6]
     grad_out_t = short(mm_tn(grad_mid_low, context))
@@ -1266,18 +1280,15 @@
     grad_bias_pair = jnp.stack(
         [jnp.sum(grad_queries, axis=0, dtype=f32), jnp.sum(grad_values, axis=0, dtype=f32)]
     )
+    grad_projected = jnp.concatenate([grad_queries, grad_keys, grad_values], 1)
     grad_qkvo = jnp.concatenate(
         [
-            short(mm_tn(packed_x, jnp.concatenate([grad_queries, grad_keys, grad_values], 1))),
+            short(mm_tn(packed_x, grad_projected)),
             grad_out_t,
         ],
         1,
     )
-    input_part = (
-        mm_nt(grad_queries, wqkv_low[0])
-        + mm_nt(grad_keys, wqkv_low[1])
-        + mm_nt(grad_values, wqkv_low[2])
-    )
+    input_part = mm_nt(grad_projected, jnp.concatenate([wqkv_low[k] for k in range(3)], 1))
     columns = D
     small = jnp.concatenate(
         [vector_part.reshape(-1), grad_bias_pair.reshape(-1), grad_bias_up.reshape(-1)]

time: 423 us -> 420 us (level)
    unnamed x81 -> x85, local copies, waits for them, and re-layouts: 16.9 us -> 15.8 us
  transfers between devices with their start and end apart: 14 -> 14, of which waited for: 4 -> 4; matrix products, arithmetic and copies ran while one was open for 9% -> 10% of each run, Pallas kernels for 10% -> 10%
where the time goes in v6:
time: 420 us; the launch traced here: 416 us
  Pallas kernels  266 us (63%)
  matrix products  37.9 us (9%)
  other arithmetic  35.9 us (9%)
  local copies, waits for them, and re-layouts  29.5 us (7%)
  starting transfers between devices  28.4 us (7%)
  waiting for transfers between devices  15.3 us (4%)
    pallas_call x1, Pallas kernels, sums_over_dp(): pl.pallas_call(functools.partial(sum_kernel, inner, tile), name='sums_ove...  157 us
    pallas_call x1, Pallas kernels, middle(): pl.pallas_call(middle_kernel, name='middle', out_shape=(rows, inner, rows...  64.7 us
    pallas_call x1, Pallas kernels, orthogonal_columns(): pl.pallas_call(functools.partial(step_kernel, 512), name='orthogonal_colu...  43.4 us
    unnamed x85, local copies, waits for them, and re-layouts  15.8 us
    add x4, other arithmetic, body(): momentum_decay * old + grad  13.3 us
    all_to_all x1, starting transfers between devices, body(): lax.all_to_all(stepped.reshape(groups, dp_rows, width), 'dp', split_axis=...  11.6 us
    all_to_all x1, waiting for transfers between devices, body(): got = lax.all_to_all(sent, 'dp', split_axis=0, concat_axis=0, tiled=True)  10.1 us
    convert_element_type x5, other arithmetic, short(): return value.astype(bf16)  9.94 us
  transfers between devices with their start and end apart: 14, of which 4 were waited for; matrix products, arithmetic and copies ran while one was open for 10% of the time, Pallas kernels for 10%

profile of v6, /device:TPU:1, one launch (start us, length us, event | category | flops | bytes accessed | tf_op | source)
XLA Modules:
  0.0 416.2 jit_solution(12430174171825782048)
XLA Ops:
  0.7 1.4 fusion.83
  6.3 1.1 constant_dynamic-slice_fusion.29
  7.4 1.5 fusion.25
  8.9 6.4 %all-to-all-start = ((bf16[8,72,512]{2,1,0:T(8,128)(2,1)}), bf16[8,72,512]{2,1,0:T(8,128)(2,1)S(1)}, u32[]{:S(2)}, u32[]{:S(2)}) async-start(bf16[8,72,512]{2,1,0:T(8,128)(2,1)} %bitcast), calls=%async_computation | async-start | bytes 1179648 | tf_op jit(solution)/shard_map/all_to_all | solution.py:1207
  15.3 2.0 convert_element_type.131
  18.6 1.2 slice_bitcast_fusion.5
  19.8 10.1 %all-to-all-done = bf16[8,72,512]{2,1,0:T(8,128)(2,1)S(1)} async-done(((bf16[8,72,512]{2,1,0:T(8,128)(2,1)}), bf16[8,72,512]{2,1,0:T(8,128)(2,1)S(1)}, u32[]{:S(2)}, u32[]{:S(2)}) %all-to-all-start) | async-done | bytes 589856 | tf_op jit(solution)/shard_map/all_to_all | solution.py:1207
  30.7 1.2 collective-permute-start
  32.2 1.3 convert_element_type.141.out_ref
  34.5 2.5 collective-permute-start.5
  37.3 1.6 collective-permute-start.3
  40.6 1.3 copy.91
  41.9 4.0 convert_element_type.142.up_ref
  45.9 1.6 convert_element_type.143.down_ref
  50.2 1.4 copy-done.10
  52.8 1.6 fusion.48
  54.9 4.8 %fusion.84 = (f32[4,576]{1,0:T(4,128)S(1)}, f32[4,576,576]{1,2,0:T(8,128)}) fusion(pred[576,576]{0,1:T(8,128)(4,1)S(1)} %copy-done.21, bf16[576,4,64]{0,2,1:T(8,128)(2,1)S(1)} %bitcast.89, bf16[576,4,64]{0,2,1:T(8,128)(2,1)S(1)} %bitcast.91), kind=kOutput, calls=%fused_computation.167 | convolution fusion | flops 175178304 | bytes 6239232 | tf_op jit(solution)/shard_map/sub | solution.py:1234
  59.7 3.4 fusion.41
  63.8 64.7 %middle.1 = (bf16[4,144,1024]{2,1,0:T(8,128)(2,1)}, bf16[4,144,1024]{2,1,0:T(8,128)(2,1)}, bf16[4,144,1024]{2,1,0:T(8,128)(2,1)}, bf16[4,144,1024]{2,1,0:T(8,128...) custom-call(bf16[4,144,256]{2,1,0:T(8,128)(2,1)S(1)} %copy.83.contex, ...), custom_call_target="tpu_custom_call" | custom-call | flops 7247757312 | bytes 8388608 | tf_op jit(solution)/shard_map/middle/pallas_call | solution.py:853
  128.5 1.8 convolution_convert_fusion.2
  130.6 4.5 %bitcast_reduce_fusion = (bf16[4,64]{1,0:T(4,128)(2,1)S(1)}, bf16[4,64,576]{2,1,0:T(8,128)(2,1)}) fusion(bf16[576,4,64]{0,2,1:T(8,128)(2,1)S(1)} %bitcast.103, f32[4,576,576]{1,2,0:T(8,128)} %get-tuple-element.194, f32[4,576]{1,0:T(4,128)S(1)} %get-tuple-element.193), kind=kOutput, calls=%fused_computation.85 | convolution fusion | flops 172818176 | bytes 5907968 | tf_op jit(solution)/shard_map/hqk,qhd->khd/dot_general | solution.py:1272
  135.1 3.8 multiply_reduce_fusion
  141.9 1.9 convolution_convert_fusion.1
  144.0 2.6 convolution_convert_fusion
  146.7 1.6 pad_maximum_fusion.1.qkvo_ref
  149.0 2.4 fusion.15
  151.4 157.5 %sums_over_dp.1 = (bf16[1024,1024]{1,0:T(8,128)(2,1)}, bf16[1024,1024]{1,0:T(8,128)(2,1)}, bf16[1024,1024]{1,0:T(8,128)(2,1)}, f32[16,1024]{1,0:T(8,128)S(1)}, b...) custom-call(bf16[1024,1024]{1,0:T(8,128)(2,1)} %get-tuple-element.37.down_ref, ...), custom_call_target="tpu_custom_call" | custom-call | flops 3145728 | bytes 12582912 | tf_op jit(solution)/shard_map/sums_over_dp/pallas_call | solution.py:553
  308.8 1.7 fusion.26
  310.5 1.3 collective-permute-start.7
  313.3 1.7 copy-done.2
  315.0 1.6 copy-done.3
  316.6 43.4 %orthogonal_columns.1 = bf16[1024,256]{1,0:T(8,128)(2,1)} custom-call(bf16[4,1024,256]{2,1,0:T(8,128)(2,1)S(1)} %copy-done.3, f32[10,256,256]{2,1,0:T(8,128)S(1)} %copy-done.2), custom_call_target="tpu_custom_call" | custom-call | flops 42949672960 | bytes 8388608 | tf_op jit(solution)/shard_map/orthogonal_columns/pallas_call | solution.py:1074
  360.1 11.6 %all-to-all-start.1 = ((bf16[8,128,256]{2,1,0:T(8,128)(2,1)}), bf16[8,128,256]{2,1,0:T(8,128)(2,1)S(1)}, u32[]{:S(2)}, u32[]{:S(2)}) async-start(bf16[8,128,256]{2,1,0:T(8,128)(2,1)} %bitcast.33), calls=%async_computation.1 | async-start | bytes 1048576 | tf_op jit(solution)/shard_map/all_to_all | solution.py:1333
  375.5 4.9 %multiply_add_fusion.1 = (f32[1024,1024]{1,0:T(8,128)}, f32[1024,1024]{1,0:T(8,128)}) fusion(f32[1024,1024]{1,0:T(8,128)S(1)} %copy-done.4, bf16[1024,1024]{1,0:T(8,128)(2,1)S(1)} %copy-done.15), kind=kLoop, calls=%fused_computation.7 | loop fusion | flops 3145728 | bytes 14680064 | tf_op jit(solution)/shard_map/add | solution.py:1326
  380.4 4.9 %multiply_add_fusion = (f32[1024,1024]{1,0:T(8,128)}, f32[1024,1024]{1,0:T(8,128)}) fusion(f32[1024,1024]{1,0:T(8,128)S(1)} %copy-done.5, bf16[1024,1024]{1,0:T(8,128)(2,1)S(1)} %copy-done.14), kind=kLoop, calls=%fused_computation.6 | loop fusion | flops 3145728 | bytes 14680064 | tf_op jit(solution)/shard_map/add | solution.py:1326
  385.3 3.4 multiply_add_fusion.2
  389.9 1.3 copy.94
  391.2 1.3 copy.93
  392.5 1.1 fusion.76
  394.3 1.1 fusion.78
  396.5 3.8 collective-permute-done.9
  400.3 1.3 collective-permute-start.11
  401.6 1.8 multiply_subtract_fusion
  406.3 1.8 copy-done.6
  408.1 2.5 fusion.30
  410.5 2.6 fusion.36
  413.1 1.2 pad_maximum_fusion.6
  414.3 1.7 maximum_convert_fusion
  (164 shorter events, 27.5 us)
Async XLA Ops:
  8.9 21.1 %all-to-all-start = ((bf16[8,72,512]{2,1,0:T(8,128)(2,1)}), bf16[8,72,512]{2,1,0:T(8,128)(2,1)S(1)}, u32[]{:S(2)}, u32[]{:S(2)}) async-start(bf16[8,72,512]{2,1,0:T(8,128)(2,1)} %bitcast), calls=%async_computation | async-start | bytes 1179648 | tf_op jit(solution)/shard_map/all_to_all | solution.py:1207
  17.4 13.3 %copy-start.9 = (bf16[3,1024,256]{2,1,0:T(8,128)(2,1)}, bf16[3,1024,256]{2,1,0:T(8,128)(2,1)S(1)}, u32[]{:S(2)}) copy-start(bf16[3,1024,256]{2,1,0:T(8,128)(2,1)S(1)} %convert_element_type.131) | copy-start | bytes 4718596
  17.6 14.3 %copy-start.33 = (f32[2,256]{1,0:T(2,128)S(1)}, f32[2,256]{1,0:T(2,128)}, u32[]{:S(2)}) copy-start(f32[2,256]{1,0:T(2,128)} %param.26) | copy-start | bytes 6148
  19.8 20.8 %copy-start.12 = (f32[256,1024]{1,0:T(8,128)S(1)}, f32[256,1024]{1,0:T(8,128)}, u32[]{:S(2)}) copy-start(f32[256,1024]{1,0:T(8,128)} %mom_out_ref.1) | copy-start | bytes 3145732
  30.7 16.8 %collective-permute-start = (bf16[576,256]{1,0:T(8,128)(2,1)S(1)}, bf16[576,256]{1,0:T(8,128)(2,1)S(1)}, u32[]{:S(2)}, u32[]{:S(2)}) collective-permute-start(bf16[576,256]{1,0:T(8,128)(2,1)S(1)} %get-tuple-element.169), channel_id=1, source_target_pairs={{0,2},{1,3},{2,0},{3,1},{4,6},{5,7},{6,4},{7,5},{8,10},{9,11},{10,... | collective-permute-start | bytes 884744 | tf_op jit(solution)/shard_map/ppermute | solution.py:81
  34.5 13.5 %collective-permute-start.5 = (bf16[144,256]{1,0:T(8,128)(2,1)S(1)}, bf16[144,256]{1,0:T(8,128)(2,1)S(1)}, u32[]{:S(2)}, u32[]{:S(2)}) collective-permute-start(bf16[144,256]{1,0:T(8,128)(2,1)S(1)} %get-tuple-element.179), channel_id=1, source_target_pairs={{0,3},{1,0},{2,1},{3,2},{4,7},{5,4},{6,5},{7,6},{8,11},{9,8},{10,9... | collective-permute-start | bytes 221192 | tf_op jit(solution)/shard_map/ppermute | solution.py:1215
  37.0 11.0 %collective-permute-start.4 = (bf16[144,256]{1,0:T(8,128)(2,1)S(1)}, bf16[144,256]{1,0:T(8,128)(2,1)S(1)}, u32[]{:S(2)}, u32[]{:S(2)}) collective-permute-start(bf16[144,256]{1,0:T(8,128)(2,1)S(1)} %get-tuple-element.180), channel_id=1, source_target_pairs={{0,2},{1,3},{2,0},{3,1},{4,6},{5,7},{6,4},{7,5},{8,10},{9,11},{10,... | collective-permute-start | bytes 221192 | tf_op jit(solution)/shard_map/ppermute | solution.py:1215
  37.3 10.7 %collective-permute-start.3 = (bf16[144,256]{1,0:T(8,128)(2,1)S(1)}, bf16[144,256]{1,0:T(8,128)(2,1)S(1)}, u32[]{:S(2)}, u32[]{:S(2)}) collective-permute-start(bf16[144,256]{1,0:T(8,128)(2,1)S(1)} %get-tuple-element.181), channel_id=1, source_target_pairs={{0,1},{1,2},{2,3},{3,0},{4,5},{5,6},{6,7},{7,4},{8,9},{9,10},{10,1... | collective-permute-start | bytes 221192 | tf_op jit(solution)/shard_map/ppermute | solution.py:1215
  41.9 4.0 copy-start.11
  47.5 1.6 collective-permute-start.1
  47.5 2.0 collective-permute-start.2
  49.8 1.7 copy-start.10
  50.1 2.6 copy-start.28
  50.1 2.6 copy-start.30
  50.2 2.6 copy-start.31
  52.7 6.9 %copy-start.24 = (bf16[576,256]{0,1:T(8,128)(2,1)}, bf16[576,256]{0,1:T(8,128)(2,1)S(1)}, u32[]{:S(2)}) copy-start(bf16[576,256]{0,1:T(8,128)(2,1)S(1)} %copy.79) | copy-start | bytes 884740
  52.8 2.1 copy-start.21
  59.6 4.1 copy-start
  59.6 4.1 copy-start.1
  63.0 65.5 %copy-start.22 = (bf16[4,64,576]{2,1,0:T(8,128)(2,1)}, bf16[4,64,576]{2,1,0:T(8,128)(2,1)S(1)}, u32[]{:S(2)}) copy-start(bf16[4,64,576]{2,1,0:T(8,128)(2,1)S(1)} %fusion.41) | copy-start | bytes 884740
  130.5 4.6 %copy-start.25 = (bf16[576,256]{0,1:T(8,128)(2,1)S(1)}, bf16[576,256]{0,1:T(8,128)(2,1)}, u32[]{:S(2)}) copy-start(bf16[576,256]{0,1:T(8,128)(2,1)} %copy-done.24) | copy-start | bytes 884740
  130.5 8.4 %slice-start = ((s8[5898240]{0:T(1024)(128)(4,1)}), s8[4194304]{0:T(1024)(128)(4,1)S(1)}, s32[]{:S(2)}) async-start(s8[5898240]{0:T(1024)(128)(4,1)} %bitcast.86), calls=%async_computation.2 | async-start | bytes 8388608
  135.1 3.8 slice-start.1
  140.9 3.1 copy-start.29
  141.6 2.4 copy-start.26
  146.7 1.7 copy-start.18
  146.7 1.9 copy-start.27
  146.7 2.3 copy-start.36
  308.8 3.8 copy-start.32
  310.5 83.8 %collective-permute-start.7 = (bf16[576,512]{1,0:T(8,128)(2,1)}, bf16[576,512]{1,0:T(8,128)(2,1)}, u32[]{:S(2)}, u32[]{:S(2)}) collective-permute-start(bf16[576,512]{1,0:T(8,128)(2,1)} %fusion.26), channel_id=1, source_target_pairs={{0,1},{1,0},{2,3},{3,2},{4,5},{5,4},{6,7},{7,6},{8,9},{9,8},{10,11... | collective-permute-start | bytes 1769480 | tf_op jit(solution)/shard_map/ppermute | solution.py:81
  311.8 81.8 %collective-permute-start.6 = (bf16[576,512]{1,0:T(8,128)(2,1)}, bf16[576,512]{1,0:T(8,128)(2,1)S(1)}, u32[]{:S(2)}, u32[]{:S(2)}) collective-permute-start(bf16[576,512]{1,0:T(8,128)(2,1)} %fusion.26), channel_id=1, source_target_pairs={{0,2},{1,3},{2,0},{3,1},{4,6},{5,7},{6,4},{7,5},{8,10},{9,11},{10,... | collective-permute-start | bytes 1769480 | tf_op jit(solution)/shard_map/ppermute | solution.py:81
  313.3 1.7 copy-start.2
  316.6 55.0 %copy-start.16 = (bf16[1024,1024]{1,0:T(8,128)(2,1)S(1)}, bf16[1024,1024]{1,0:T(8,128)(2,1)}, u32[]{:S(2)}) copy-start(bf16[1024,1024]{1,0:T(8,128)(2,1)} %get-tuple-element.45) | copy-start | bytes 6291460
  360.1 35.3 %all-to-all-start.1 = ((bf16[8,128,256]{2,1,0:T(8,128)(2,1)}), bf16[8,128,256]{2,1,0:T(8,128)(2,1)S(1)}, u32[]{:S(2)}, u32[]{:S(2)}) async-start(bf16[8,128,256]{2,1,0:T(8,128)(2,1)} %bitcast.33), calls=%async_computation.1 | async-start | bytes 1048576 | tf_op jit(solution)/shard_map/all_to_all | solution.py:1333
  372.1 2.5 copy-start.4
  373.4 2.2 copy-start.15
  375.5 4.9 %copy-start.5 = (f32[1024,1024]{1,0:T(8,128)S(1)}, f32[1024,1024]{1,0:T(8,128)}, u32[]{:S(2)}) copy-start(f32[1024,1024]{1,0:T(8,128)} %mom_down_ref.1) | copy-start | bytes 12582916
  375.5 4.9 %copy-start.14 = (bf16[1024,1024]{1,0:T(8,128)(2,1)S(1)}, bf16[1024,1024]{1,0:T(8,128)(2,1)}, u32[]{:S(2)}) copy-start(bf16[1024,1024]{1,0:T(8,128)(2,1)} %get-tuple-element.47) | copy-start | bytes 6291460
  380.4 4.9 %copy-start.8 = (f32[3,1024,256]{2,1,0:T(8,128)S(1)}, f32[3,1024,256]{2,1,0:T(8,128)}, u32[]{:S(2)}) copy-start(f32[3,1024,256]{2,1,0:T(8,128)} %mom_qkv_ref.1) | copy-start | bytes 9437188
  385.3 3.4 copy-start.34
  385.3 4.0 copy-start.35
  392.5 3.3 copy-start.17
  393.6 10.8 %collective-permute-start.8 = (bf16[576,512]{1,0:T(8,128)(2,1)S(1)}, bf16[576,512]{1,0:T(8,128)(2,1)}, u32[]{:S(2)}, u32[]{:S(2)}) collective-permute-start(bf16[576,512]{1,0:T(8,128)(2,1)S(1)} %collective-permute-done.6), channel_id=1, source_target_pairs={{0,1},{1,0},{2,3},{3,2},{4,5},{5,4},{6,7},{7,6},{8,9},{9,8},{10,11... | collective-permute-start | bytes 1769480 | tf_op jit(solution)/shard_map/ppermute | solution.py:81
  395.4 8.0 %collective-permute-start.10 = (bf16[256,256]{1,0:T(8,128)(2,1)S(1)}, bf16[256,256]{1,0:T(8,128)(2,1)S(1)}, u32[]{:S(2)}, u32[]{:S(2)}) collective-permute-start(bf16[256,256]{1,0:T(8,128)(2,1)S(1)} %bitcast.94), channel_id=1, source_target_pairs={{0,1},{1,0},{2,3},{3,2},{4,5},{5,4},{6,7},{7,6},{8,9},{9,8},{10,11... | collective-permute-start | bytes 393224 | tf_op jit(solution)/shard_map/ppermute | solution.py:81
  395.5 4.8 %collective-permute-start.9 = (bf16[256,256]{1,0:T(8,128)(2,1)S(1)}, bf16[256,256]{1,0:T(8,128)(2,1)}, u32[]{:S(2)}, u32[]{:S(2)}) collective-permute-start(bf16[256,256]{1,0:T(8,128)(2,1)S(1)} %bitcast.95), channel_id=1, source_target_pairs={{0,2},{1,3},{2,0},{3,1},{4,6},{5,7},{6,4},{7,5},{8,10},{9,11},{10,... | collective-permute-start | bytes 393224 | tf_op jit(solution)/shard_map/ppermute | solution.py:81
  400.3 3.1 collective-permute-start.11
  405.9 2.2 copy-start.6
  408.1 2.5 copy-start.7
  (5 other events, 7.1 us)

commit v7 on v6

--- a/solution.py
+++ b/solution.py
@@ -1225,9 +1225,12 @@
     wdown_low = short(w_down)
     heads = width // HEAD
     score_scale = HEAD ** (-0.5)
-    queries = short(mm(packed_x, wqkv_low[0]) + bias_qv[0]).reshape(count, heads, HEAD)
-    keys = short(mm(packed_x, wqkv_low[1])).reshape(count, heads, HEAD)
-    values = short(mm(packed_x, wqkv_low[2]) + bias_qv[1]).reshape(count, heads, HEAD)
+    wqkv_wide = jnp.concatenate([wqkv_low[k] for k in range(3)], 1)
+    bias_wide = jnp.concatenate([bias_qv[0], jnp.zeros((width,), f32), bias_qv[1]])
+    projected = short(mm(packed_x, wqkv_wide) + bias_wide)
+    queries, keys, values = (
+        projected[:, k * width : (k + 1) * width].reshape(count, heads, HEAD) for k in range(3)
+    )
     raw = jnp.einsum("qhd,khd->hqk", queries, keys, preferred_element_type=f32)
     same = segments[:, None] == segments[None, :]
     masked = jnp.where(same[None], raw * score_scale, masked_score)
@@ -1288,7 +1291,7 @@
         ],
         1,
     )
-    input_part = mm_nt(grad_projected, jnp.concatenate([wqkv_low[k] for k in range(3)], 1))
+    input_part = mm_nt(grad_projected, wqkv_wide)
     columns = D
     small = jnp.concatenate(
         [vector_part.reshape(-1), grad_bias_pair.reshape(-1), grad_bias_up.reshape(-1)]

time: 420 us -> 419 us (level)
  transfers between devices with their start and end apart: 14 -> 14, of which waited for: 4 -> 3; matrix products, arithmetic and copies ran while one was open for 10% -> 9% of each run, Pallas kernels for 10% -> 10%
where the time goes in v7:
time: 419 us; the launch traced here: 415 us
  Pallas kernels  268 us (64%)
  matrix products  35.8 us (9%)
  other arithmetic  34.7 us (8%)
  local copies, waits for them, and re-layouts  29.7 us (7%)
  starting transfers between devices  28.1 us (7%)
  waiting for transfers between devices  14.3 us (3%)
    pallas_call x1, Pallas kernels, sums_over_dp(): pl.pallas_call(functools.partial(sum_kernel, inner, tile), name='sums_ove...  158 us
    pallas_call x1, Pallas kernels, middle(): pl.pallas_call(middle_kernel, name='middle', out_shape=(rows, inner, rows...  67.1 us
    pallas_call x1, Pallas kernels, orthogonal_columns(): pl.pallas_call(functools.partial(step_kernel, 512), name='orthogonal_colu...  43.4 us
    unnamed x85, local copies, waits for them, and re-layouts  16.5 us
    add x4, other arithmetic, body(): momentum_decay * old + grad  13.3 us
    all_to_all x1, starting transfers between devices, body(): lax.all_to_all(stepped.reshape(groups, dp_rows, width), 'dp', split_axis=...  11.6 us
    all_to_all x1, waiting for transfers between devices, body(): got = lax.all_to_all(sent, 'dp', split_axis=0, concat_axis=0, tiled=True)  9.59 us
    convert_element_type x5, other arithmetic, short(): return value.astype(bf16)  8.73 us
  transfers between devices with their start and end apart: 14, of which 3 were waited for; matrix products, arithmetic and copies ran while one was open for 9% of the time, Pallas kernels for 10%

profile of v7, /device:TPU:1, one launch (start us, length us, event | category | flops | bytes accessed | tf_op | source)
XLA Modules:
  0.0 414.7 jit_solution(8117347591363575499)
XLA Ops:
  0.7 1.4 fusion.74
  6.3 1.1 constant_dynamic-slice_fusion.29
  7.4 1.5 fusion.16
  8.9 6.4 %all-to-all-start = ((bf16[8,72,512]{2,1,0:T(8,128)(2,1)}), bf16[8,72,512]{2,1,0:T(8,128)(2,1)}, u32[]{:S(2)}, u32[]{:S(2)}) async-start(bf16[8,72,512]{2,1,0:T(8,128)(2,1)} %bitcast), calls=%async_computation | async-start | bytes 1179648 | tf_op jit(solution)/shard_map/all_to_all | solution.py:1207
  16.0 2.0 convert_element_type.125
  19.3 1.2 slice_bitcast_fusion.6
  20.5 9.6 %all-to-all-done = bf16[8,72,512]{2,1,0:T(8,128)(2,1)} async-done(((bf16[8,72,512]{2,1,0:T(8,128)(2,1)}), bf16[8,72,512]{2,1,0:T(8,128)(2,1)}, u32[]{:S(2)}, u32[]{:S(2)}) %all-to-all-start) | async-done | bytes 589856 | tf_op jit(solution)/shard_map/all_to_all | solution.py:1207
  31.1 1.3 collective-permute-start
  34.1 1.3 copy.91
  35.4 4.0 convert_element_type.134.up_ref
  39.4 1.6 convert_element_type.135.down_ref
  41.1 2.5 collective-permute-start.5
  43.8 1.6 collective-permute-start.3
  46.0 1.4 collective-permute-done.4
  47.6 1.1 pad_maximum_fusion.3
  50.6 1.1 add_convert_fusion
  52.7 4.8 %fusion.75 = (f32[4,576]{1,0:T(4,128)S(1)}, f32[4,576,576]{1,2,0:T(8,128)}) fusion(pred[576,576]{0,1:T(8,128)(4,1)S(1)} %copy-done.24, bf16[576,4,64]{0,2,1:T(8,128)(2,1)S(1)} %bitcast.85, bf16[576,4,64]{0,2,1:T(8,128)(2,1)S(1)} %bitcast.87), kind=kOutput, calls=%fused_computation.161 | convolution fusion | flops 175178304 | bytes 6239232 | tf_op jit(solution)/shard_map/sub | solution.py:1237
  57.5 3.3 fusion.32
  62.2 67.1 %middle.1 = (bf16[4,144,1024]{2,1,0:T(8,128)(2,1)}, bf16[4,144,1024]{2,1,0:T(8,128)(2,1)}, bf16[4,144,1024]{2,1,0:T(8,128)(2,1)}, bf16[4,144,1024]{2,1,0:T(8,128...) custom-call(bf16[4,144,256]{2,1,0:T(8,128)(2,1)S(1)} %copy.83.contex, ...), custom_call_target="tpu_custom_call" | custom-call | flops 7247757312 | bytes 8388608 | tf_op jit(solution)/shard_map/middle/pallas_call | solution.py:853
  129.3 1.8 convolution_convert_fusion.3
  131.3 3.9 bitcast_reduce_fusion
  135.2 3.8 multiply_reduce_fusion
  142.4 2.4 convolution_convert_fusion.1
  144.8 2.6 convolution_convert_fusion
  147.5 2.1 convolution_convert_fusion.2
  149.8 1.6 pad_maximum_fusion.1.qkvo_ref
  151.4 157.8 %sums_over_dp.1 = (bf16[1024,1024]{1,0:T(8,128)(2,1)}, bf16[1024,1024]{1,0:T(8,128)(2,1)}, bf16[1024,1024]{1,0:T(8,128)(2,1)}, f32[16,1024]{1,0:T(8,128)S(1)}, b...) custom-call(bf16[1024,1024]{1,0:T(8,128)(2,1)} %get-tuple-element.37.down_ref, ...), custom_call_target="tpu_custom_call" | custom-call | flops 3145728 | bytes 12582912 | tf_op jit(solution)/shard_map/sums_over_dp/pallas_call | solution.py:553
  309.2 1.7 fusion.17
  312.9 1.7 copy-done.2
  314.7 1.6 copy-done.3
  316.2 43.4 %orthogonal_columns.1 = bf16[1024,256]{1,0:T(8,128)(2,1)} custom-call(bf16[4,1024,256]{2,1,0:T(8,128)(2,1)S(1)} %copy-done.3, f32[10,256,256]{2,1,0:T(8,128)S(1)} %copy-done.2), custom_call_target="tpu_custom_call" | custom-call | flops 42949672960 | bytes 8388608 | tf_op jit(solution)/shard_map/orthogonal_columns/pallas_call | solution.py:1074
  359.6 11.6 %all-to-all-start.1 = ((bf16[8,128,256]{2,1,0:T(8,128)(2,1)}), bf16[8,128,256]{2,1,0:T(8,128)(2,1)S(1)}, u32[]{:S(2)}, u32[]{:S(2)}) async-start(bf16[8,128,256]{2,1,0:T(8,128)(2,1)} %bitcast.33), calls=%async_computation.1 | async-start | bytes 1048576 | tf_op jit(solution)/shard_map/all_to_all | solution.py:1336
  375.0 4.9 %multiply_add_fusion.1 = (f32[1024,1024]{1,0:T(8,128)}, f32[1024,1024]{1,0:T(8,128)}) fusion(f32[1024,1024]{1,0:T(8,128)S(1)} %copy-done.4, bf16[1024,1024]{1,0:T(8,128)(2,1)S(1)} %copy-done.13), kind=kLoop, calls=%fused_computation.7 | loop fusion | flops 3145728 | bytes 14680064 | tf_op jit(solution)/shard_map/add | solution.py:1329
  379.9 4.9 %multiply_add_fusion = (f32[1024,1024]{1,0:T(8,128)}, f32[1024,1024]{1,0:T(8,128)}) fusion(f32[1024,1024]{1,0:T(8,128)S(1)} %copy-done.5, bf16[1024,1024]{1,0:T(8,128)(2,1)S(1)} %copy-done.12), kind=kLoop, calls=%fused_computation.6 | loop fusion | flops 3145728 | bytes 14680064 | tf_op jit(solution)/shard_map/add | solution.py:1329
  384.8 3.4 multiply_add_fusion.2
  389.4 1.3 copy.94
  390.7 1.3 copy.93
  392.0 1.1 fusion.67
  393.8 1.1 fusion.69
  396.5 3.2 collective-permute-done.9
  399.7 1.3 collective-permute-start.11
  401.0 1.8 multiply_subtract_fusion
  403.0 1.1 fusion.70
  404.8 1.8 copy-done.6
  406.6 2.5 fusion.21
  409.0 2.6 fusion.27
  411.6 1.2 pad_maximum_fusion.7
  412.8 1.7 maximum_convert_fusion
  (165 shorter events, 25.8 us)
Async XLA Ops:
  7.4 8.6 %copy-start.16 = (f32[256,1024]{1,0:T(8,128)S(1)}, f32[256,1024]{1,0:T(8,128)}, u32[]{:S(2)}) copy-start(f32[256,1024]{1,0:T(8,128)} %param.23) | copy-start | bytes 3145732
  8.9 21.2 %all-to-all-start = ((bf16[8,72,512]{2,1,0:T(8,128)(2,1)}), bf16[8,72,512]{2,1,0:T(8,128)(2,1)}, u32[]{:S(2)}, u32[]{:S(2)}) async-start(bf16[8,72,512]{2,1,0:T(8,128)(2,1)} %bitcast), calls=%async_computation | async-start | bytes 1179648 | tf_op jit(solution)/shard_map/all_to_all | solution.py:1207
  16.0 2.3 copy-start.34
  19.3 14.8 %copy-start.10 = (f32[256,1024]{1,0:T(8,128)S(1)}, f32[256,1024]{1,0:T(8,128)}, u32[]{:S(2)}) copy-start(f32[256,1024]{1,0:T(8,128)} %mom_out_ref.1) | copy-start | bytes 3145732
  31.1 14.4 %collective-permute-start = (bf16[576,256]{1,0:T(8,128)(2,1)S(1)}, bf16[576,256]{1,0:T(8,128)(2,1)S(1)}, u32[]{:S(2)}, u32[]{:S(2)}) collective-permute-start(bf16[576,256]{1,0:T(8,128)(2,1)S(1)} %get-tuple-element.172), channel_id=1, source_target_pairs={{0,2},{1,3},{2,0},{3,1},{4,6},{5,7},{6,4},{7,5},{8,10},{9,11},{10,... | collective-permute-start | bytes 884744 | tf_op jit(solution)/shard_map/ppermute | solution.py:81
  35.4 4.0 copy-start.9
  41.1 4.9 %collective-permute-start.5 = (bf16[144,256]{1,0:T(8,128)(2,1)S(1)}, bf16[144,256]{1,0:T(8,128)(2,1)S(1)}, u32[]{:S(2)}, u32[]{:S(2)}) collective-permute-start(bf16[144,256]{1,0:T(8,128)(2,1)S(1)} %get-tuple-element.182), channel_id=1, source_target_pairs={{0,3},{1,0},{2,1},{3,2},{4,7},{5,4},{6,5},{7,6},{8,11},{9,8},{10,9... | collective-permute-start | bytes 221192 | tf_op jit(solution)/shard_map/ppermute | solution.py:1215
  43.6 3.8 collective-permute-start.4
  43.8 3.6 collective-permute-start.3
  45.4 2.1 collective-permute-start.1
  45.5 2.1 copy-start.26
  45.5 2.1 collective-permute-start.2
  48.9 1.2 copy-start.20
  48.9 1.7 copy-start.22
  49.2 2.5 copy-start.29
  49.2 2.4 copy-start.31
  57.5 4.8 %copy-start = (f32[6,1024]{1,0:T(8,128)S(1)}, f32[6,1024]{1,0:T(8,128)}, u32[]{:S(2)}) copy-start(f32[6,1024]{1,0:T(8,128)} %vectors_ref.1) | copy-start | bytes 73732
  57.5 4.8 %copy-start.1 = (f32[1024]{0:T(1024)S(1)}, f32[1024]{0:T(1024)}, u32[]{:S(2)}) copy-start(f32[1024]{0:T(1024)} %param.27) | copy-start | bytes 12292
  131.3 7.7 %slice-start = ((s8[5898240]{0:T(1024)(128)(4,1)}), s8[4194304]{0:T(1024)(128)(4,1)S(1)}, s32[]{:S(2)}) async-start(s8[5898240]{0:T(1024)(128)(4,1)} %bitcast.83), calls=%async_computation.2 | async-start | bytes 8388608
  135.2 3.8 slice-start.1
  141.0 1.2 copy-start.21
  141.0 1.3 copy-start.23
  142.4 2.4 copy-start.28
  142.4 2.4 copy-start.30
  142.4 2.4 copy-start.32
  147.4 2.4 copy-start.15
  309.2 3.1 copy-start.33
  310.9 82.9 %collective-permute-start.7 = (bf16[576,512]{1,0:T(8,128)(2,1)}, bf16[576,512]{1,0:T(8,128)(2,1)}, u32[]{:S(2)}, u32[]{:S(2)}) collective-permute-start(bf16[576,512]{1,0:T(8,128)(2,1)} %fusion.17), channel_id=1, source_target_pairs={{0,1},{1,0},{2,3},{3,2},{4,5},{5,4},{6,7},{7,6},{8,9},{9,8},{10,11... | collective-permute-start | bytes 1769480 | tf_op jit(solution)/shard_map/ppermute | solution.py:81
  311.4 81.7 %collective-permute-start.6 = (bf16[576,512]{1,0:T(8,128)(2,1)}, bf16[576,512]{1,0:T(8,128)(2,1)S(1)}, u32[]{:S(2)}, u32[]{:S(2)}) collective-permute-start(bf16[576,512]{1,0:T(8,128)(2,1)} %fusion.17), channel_id=1, source_target_pairs={{0,2},{1,3},{2,0},{3,1},{4,6},{5,7},{6,4},{7,5},{8,10},{9,11},{10,... | collective-permute-start | bytes 1769480 | tf_op jit(solution)/shard_map/ppermute | solution.py:81
  312.9 1.7 copy-start.2
  314.7 1.6 copy-start.3
  316.2 54.9 %copy-start.14 = (bf16[1024,1024]{1,0:T(8,128)(2,1)S(1)}, bf16[1024,1024]{1,0:T(8,128)(2,1)}, u32[]{:S(2)}) copy-start(bf16[1024,1024]{1,0:T(8,128)(2,1)} %get-tuple-element.45) | copy-start | bytes 6291460
  359.6 35.3 %all-to-all-start.1 = ((bf16[8,128,256]{2,1,0:T(8,128)(2,1)}), bf16[8,128,256]{2,1,0:T(8,128)(2,1)S(1)}, u32[]{:S(2)}, u32[]{:S(2)}) async-start(bf16[8,128,256]{2,1,0:T(8,128)(2,1)} %bitcast.33), calls=%async_computation.1 | async-start | bytes 1048576 | tf_op jit(solution)/shard_map/all_to_all | solution.py:1336
  371.6 1.2 copy-start.11
  371.7 2.5 copy-start.4
  372.9 2.2 copy-start.13
  375.0 4.9 %copy-start.5 = (f32[1024,1024]{1,0:T(8,128)S(1)}, f32[1024,1024]{1,0:T(8,128)}, u32[]{:S(2)}) copy-start(f32[1024,1024]{1,0:T(8,128)} %mom_down_ref.1) | copy-start | bytes 12582916
  375.0 4.9 %copy-start.12 = (bf16[1024,1024]{1,0:T(8,128)(2,1)S(1)}, bf16[1024,1024]{1,0:T(8,128)(2,1)}, u32[]{:S(2)}) copy-start(bf16[1024,1024]{1,0:T(8,128)(2,1)} %get-tuple-element.47) | copy-start | bytes 6291460
  379.9 4.9 %copy-start.8 = (f32[3,1024,256]{2,1,0:T(8,128)S(1)}, f32[3,1024,256]{2,1,0:T(8,128)}, u32[]{:S(2)}) copy-start(f32[3,1024,256]{2,1,0:T(8,128)} %mom_qkv_ref.1) | copy-start | bytes 9437188
  384.8 3.4 copy-start.35
  384.8 4.0 copy-start.36
  392.0 3.8 copy-start.17
  393.1 9.8 %collective-permute-start.8 = (bf16[576,512]{1,0:T(8,128)(2,1)S(1)}, bf16[576,512]{1,0:T(8,128)(2,1)}, u32[]{:S(2)}, u32[]{:S(2)}) collective-permute-start(bf16[576,512]{1,0:T(8,128)(2,1)S(1)} %collective-permute-done.6), channel_id=1, source_target_pairs={{0,1},{1,0},{2,3},{3,2},{4,5},{5,4},{6,7},{7,6},{8,9},{9,8},{10,11... | collective-permute-start | bytes 1769480 | tf_op jit(solution)/shard_map/ppermute | solution.py:81
  394.9 7.8 %collective-permute-start.10 = (bf16[256,256]{1,0:T(8,128)(2,1)S(1)}, bf16[256,256]{1,0:T(8,128)(2,1)S(1)}, u32[]{:S(2)}, u32[]{:S(2)}) collective-permute-start(bf16[256,256]{1,0:T(8,128)(2,1)S(1)} %bitcast.90), channel_id=1, source_target_pairs={{0,1},{1,0},{2,3},{3,2},{4,5},{5,4},{6,7},{7,6},{8,9},{9,8},{10,11... | collective-permute-start | bytes 393224 | tf_op jit(solution)/shard_map/ppermute | solution.py:81
  395.0 4.7 %collective-permute-start.9 = (bf16[256,256]{1,0:T(8,128)(2,1)S(1)}, bf16[256,256]{1,0:T(8,128)(2,1)S(1)}, u32[]{:S(2)}, u32[]{:S(2)}) collective-permute-start(bf16[256,256]{1,0:T(8,128)(2,1)S(1)} %bitcast.91), channel_id=1, source_target_pairs={{0,2},{1,3},{2,0},{3,1},{4,6},{5,7},{6,4},{7,5},{8,10},{9,11},{10,... | collective-permute-start | bytes 393224 | tf_op jit(solution)/shard_map/ppermute | solution.py:81
  399.7 3.1 collective-permute-start.11
  404.4 2.2 copy-start.6
  406.6 2.5 copy-start.7
  (5 other events, 4.5 us)
